TPU v7x, 32 devices: a whole 2x2x4 slice. The times are simulated.
32 devices in a mesh: dx: 4 (over x, core), dy: 8 (over z, y).
Axes of the slice: x: 2, y: 2, z: 4, core: 2. Of those that a mesh axis runs over, the one named last changes fastest.
Arguments:
- features: bfloat16 [4, 8, 384, 128], P('dx', 'dy'), may hold values from -6 to 6
- positions: bfloat16 [4, 8, 3, 384], P('dx', 'dy'), may hold values from 0 to 1
- atom_count: int32 [4, 8], P('dx', 'dy'), may hold values from 192 to 384, as said below
- ghost_index: int32 [4, 8, 256], P('dx', 'dy'), may hold values from 0 to 383, as said below
- neighbour_list: int32 [4, 8, 384, 32], P('dx', 'dy'), may hold values from 0 to 2687, as said below
- cell_index: int32 [4, 8, 384], P('dx', 'dy'), may hold values from 0 to 65535
- w_self: bfloat16 [128, 128], replicated, may hold values from -0.5 to 0.5
- w_pair: bfloat16 [128, 256], replicated, may hold values from -0.5 to 0.5
- w_radial: float32 [8, 128], replicated, may hold values from -2 to 2
- w_expand: bfloat16 [128, 1024], replicated, may hold values from -0.5 to 0.5
- w_contract: bfloat16 [1024, 128], replicated, may hold values from -0.1875 to 0.1875
- w_final: bfloat16 [128, 128], replicated, may hold values from -0.5 to 0.5
- w_charge: bfloat16 [128], replicated, may hold values from -0.5 to 0.5
Outputs:
- forces: float32 [4, 8, 3, 384], P('dx', 'dy')
Inputs may be any that keep to these rules, and one draw needn't show every extreme that they name: `atom_count`: each domain holds at least half of 384 live atoms in its first slots, and some domain is full. `ghost_index`: each entry is a live slot of the same domain. `neighbour_list`: each entry is a live slot of the domain itself or a slot of a ghost block other than block 4 (the domain's own exports).
All inputs are finite; a program needn't handle non-finite values.
Results may differ from a plain program's by a relative error of at most 0.0049.
Values may be sent and summed in bfloat16 or wider, within the bound.
No kernel may reach another device: no remote copies, remote signals or barrier semaphores. Data moves between devices by JAX's collectives and lax.ppermute only.
A program may use at most 128 MiB of HBM per device.

v0:
```python
import math

import jax
import jax.numpy as jnp
from jax import lax
from jax.sharding import PartitionSpec as P

ATOM_BLOCK = 64
GRID_X = 8
GRID_Y = 8
GRID_Z = 1024


box_side = 1.0
cutoff_sq = 6.25
smearing = 1.0


def extended(array, sides, width):
    for axis, dim in sides:
        devices, length = (lax.axis_size(axis), array.shape[dim])
        up = [(i, (i + 1) % devices) for i in range(devices)]
        down = [(j, i) for i, j in up]
        last = lax.slice_in_dim(array, length - width, length, axis=dim)
        leading = lax.slice_in_dim(array, 0, width, axis=dim)
        before = lax.ppermute(last, axis, up)
        after = lax.ppermute(leading, axis, down)
        array = jnp.concatenate([before, array, after], axis=dim)
    return array


def short_range(
    features,
    projected,
    own_coords,
    ext_coords,
    block_lists_all,
    w_self,
    w_radial,
    w_expand,
    w_contract,
    w_final,
):
    channels = features.shape[1]
    atom_rows = features.shape[0]
    per_atom = block_lists_all.shape[1]
    basis_count = w_radial.shape[0]
    block_count = atom_rows // ATOM_BLOCK
    own_term = jnp.dot(features, w_self, preferred_element_type=jnp.float32)
    spacing = cutoff_sq / (basis_count - 1)
    centers = jnp.arange(basis_count, dtype=jnp.float32) * spacing
    edge_scale = 1.0 / math.sqrt(per_atom)

    def one_block(inputs):
        own_rows, near_coords, block_lists = inputs
        flat_list = block_lists.reshape(-1)
        gathered = jnp.take(projected, flat_list, axis=0)
        bias_rows = gathered[:, :channels].astype(jnp.float32)
        value_rows = gathered[:, channels:].astype(jnp.float32)
        far_coords = jnp.take(ext_coords, flat_list, axis=1)
        start_coords = jnp.broadcast_to(
            near_coords[:, :, None], (3, near_coords.shape[1], per_atom)
        ).reshape(3, -1)
        displace = far_coords - start_coords
        dist_sq = jnp.sum(displace * displace, axis=0)
        basis_rows = jnp.exp(-jnp.square((dist_sq[None, :] - centers[:, None]) / spacing))
        envelope = jnp.square(jnp.maximum(0.0, 1.0 - dist_sq / cutoff_sq))
        radial = lax.dot_general(
            basis_rows,
            w_radial,
            (((0,), (0,)), ((), ())),
            precision=lax.Precision.HIGHEST,
            preferred_element_type=jnp.float32,
        )
        own_edges = jnp.broadcast_to(
            own_rows[:, None, :], (own_rows.shape[0], per_atom, channels)
        ).reshape(-1, channels)
        edge_in = jax.nn.silu(radial + own_edges + bias_rows).astype(jnp.bfloat16)
        latent = jax.nn.silu(jnp.dot(edge_in, w_expand, preferred_element_type=jnp.float32)).astype(
            jnp.bfloat16
        )
        mixed_out = jnp.dot(latent, w_contract, preferred_element_type=jnp.float32)
        weight = mixed_out * envelope[:, None] * value_rows
        scalar = weight.reshape(-1, per_atom, channels).sum(axis=1) * edge_scale
        vector = (displace[:, :, None] * weight[None]).reshape(3, -1, per_atom, channels).sum(
            axis=2
        ) * edge_scale
        invariant = (scalar + jnp.sum(vector * vector, axis=0) / 3.0).astype(jnp.bfloat16)
        gating = jax.nn.silu(jnp.dot(invariant, w_final, preferred_element_type=jnp.float32))
        return jnp.sum(vector * gating[None], axis=2) / math.sqrt(channels)

    own_blocks = own_term.reshape(block_count, ATOM_BLOCK, channels)
    coord_blocks = own_coords.reshape(3, block_count, ATOM_BLOCK).transpose(1, 0, 2)
    list_blocks = block_lists_all.reshape(block_count, ATOM_BLOCK, per_atom)
    result = lax.map(one_block, (own_blocks, coord_blocks, list_blocks))
    return result.transpose(1, 0, 2).reshape(3, atom_rows)


def dft_tables(count):
    modes = jnp.arange(count, dtype=jnp.int32)
    product = modes[:, None] * modes[None, :] % count
    angle = product.astype(jnp.float32) * (2.0 * math.pi / count)
    return (jnp.cos(angle), jnp.sin(angle))


def transform_axis(real_part, imag_part, axis, inverse):
    count = real_part.shape[axis]
    cosine, sine = dft_tables(count)
    letters = "abcdef"[: real_part.ndim]
    source = letters[:axis] + "z" + letters[axis + 1 :]
    target = letters[:axis] + "w" + letters[axis + 1 :]
    formula = source + ",zw->" + target

    def apply_table(values, table):
        return jnp.einsum(formula, values, table, precision=lax.Precision.HIGHEST)

    real_cos = apply_table(real_part, cosine)
    real_sin = apply_table(real_part, sine)
    imag_cos = apply_table(imag_part, cosine)
    imag_sin = apply_table(imag_part, sine)
    if inverse:
        return (real_cos - imag_sin, imag_cos + real_sin)
    return (real_cos + imag_sin, imag_cos - real_sin)


def rotate(real_part, imag_part, cosine, sine, formula, inverse):

    def apply_table(values, table):
        return jnp.einsum(formula, values, table, precision=lax.Precision.HIGHEST)

    real_cos = apply_table(real_part, cosine)
    real_sin = apply_table(real_part, sine)
    if imag_part is None:
        return (real_cos, -real_sin)
    imag_cos = apply_table(imag_part, cosine)
    imag_sin = apply_table(imag_part, sine)
    if inverse:
        return (real_cos - imag_sin, imag_cos + real_sin)
    return (real_cos + imag_sin, imag_cos - real_sin)


def factored_transform(real_part, imag_part, inverse):
    count = real_part.shape[-1]
    factor = 1
    for trial in range(1, math.isqrt(count) + 1):
        if count % trial == 0:
            factor = trial
    second = count // factor
    leading = real_part.shape[:-1]
    split_shape = leading + (factor, second)
    real_split = real_part.reshape(split_shape)
    imag_split = None if imag_part is None else imag_part.reshape(split_shape)
    cos_first, sin_first = dft_tables(factor)
    section_real, section_imag = rotate(
        real_split, imag_split, cos_first, sin_first, "...ts,tk->...ks", inverse
    )
    rows_iota = lax.broadcasted_iota(jnp.int32, (factor, second), 0)
    cols_iota = lax.broadcasted_iota(jnp.int32, (factor, second), 1)
    twist_angle = (rows_iota * cols_iota % count).astype(jnp.float32) * (2.0 * math.pi / count)
    twist_cos = jnp.cos(twist_angle)
    twist_sin = jnp.sin(twist_angle)
    if inverse:
        turned_real = section_real * twist_cos - section_imag * twist_sin
        turned_imag = section_imag * twist_cos + section_real * twist_sin
    else:
        turned_real = section_real * twist_cos + section_imag * twist_sin
        turned_imag = section_imag * twist_cos - section_real * twist_sin
    cos_second, sin_second = dft_tables(second)
    out_real, out_imag = rotate(
        turned_real, turned_imag, cos_second, sin_second, "...ks,sm->...mk", inverse
    )
    return (out_real.reshape(leading + (count,)), out_imag.reshape(leading + (count,)))


def signed_block(start, count, total):
    modes = start + jnp.arange(count, dtype=jnp.int32)
    return jnp.where(modes < total // 2, modes, modes - total)


def green_terms(sig_x, sig_y, sig_z, mesh_x, mesh_y, mesh_z):
    waves = []
    derivatives = []
    for signed, count in ((sig_x, mesh_x), (sig_y, mesh_y), (sig_z, mesh_z)):
        wave = signed.astype(jnp.float32) * (2.0 * math.pi / count)
        waves.append(wave)
        derivatives.append(jnp.where(signed * 2 == -count, jnp.zeros_like(wave), wave))
    wave_sq = waves[0] * waves[0] + waves[1] * waves[1] + waves[2] * waves[2]
    is_zero = (sig_x == 0) & (sig_y == 0) & (sig_z == 0)
    safe_sq = jnp.where(is_zero, jnp.ones_like(wave_sq), wave_sq)
    green = jnp.where(
        is_zero,
        jnp.zeros_like(wave_sq),
        4.0 * math.pi * jnp.exp(-0.5 * smearing * smearing * wave_sq) / safe_sq,
    )
    return (derivatives, green)


def field_spectra(spectrum, sig_x, sig_y, sig_z, mesh_x, mesh_y, mesh_z):
    derivatives, green = green_terms(sig_x, sig_y, sig_z, mesh_x, mesh_y, mesh_z)
    real_part = spectrum[0] * green
    imag_part = spectrum[1] * green
    field_real = jnp.stack([wave * imag_part for wave in derivatives])
    field_imag = jnp.stack([-wave * real_part for wave in derivatives])
    return (field_real, field_imag)


def shards(
    features,
    positions,
    atom_count,
    ghost_index,
    neighbour_list,
    cell_index,
    w_self,
    w_pair,
    w_radial,
    w_expand,
    w_contract,
    w_final,
    w_charge,
):
    feat_local = features[0, 0]
    coords_local = positions[0, 0]
    lists_local = neighbour_list[0, 0]
    exports = ghost_index[0, 0]
    count_local = atom_count[0, 0]
    cells_local = cell_index[0, 0]
    channels = feat_local.shape[1]
    ghost_rows = exports.shape[0]
    exported_coords = jnp.take(coords_local, exports, axis=1)
    exported_feat = jnp.take(feat_local, exports, axis=0)
    halo_feat, halo_coords = (
        extended(exported_feat[None, None], (("dx", 0), ("dy", 1)), 1),
        extended(exported_coords[None, None], (("dx", 0), ("dy", 1)), 1),
    )
    ext_feat = jnp.concatenate([feat_local, halo_feat.reshape(9 * ghost_rows, channels)], axis=0)
    projected = jnp.dot(ext_feat, w_pair, preferred_element_type=jnp.float32).astype(jnp.bfloat16)
    shift_rows = lax.broadcasted_iota(jnp.float32, (3, 3, 3, 1), 0) - 1.0
    shift_cols = lax.broadcasted_iota(jnp.float32, (3, 3, 3, 1), 1) - 1.0
    component = lax.broadcasted_iota(jnp.int32, (3, 3, 3, 1), 2)
    offsets = (
        jnp.where(
            component == 0,
            shift_rows,
            jnp.where(component == 1, shift_cols, jnp.zeros_like(shift_rows)),
        )
        * box_side
    )
    ghost_coords = jnp.moveaxis(halo_coords.astype(jnp.float32) + offsets, 2, 0).reshape(
        3, 9 * ghost_rows
    )
    own_coords = coords_local.astype(jnp.float32)
    ext_coords = jnp.concatenate([own_coords, ghost_coords], axis=1)
    short = short_range(
        feat_local,
        projected,
        own_coords,
        ext_coords,
        lists_local,
        w_self,
        w_radial,
        w_expand,
        w_contract,
        w_final,
    )
    atom_rows = feat_local.shape[0]
    live = jnp.arange(atom_rows, dtype=jnp.int32) < count_local
    charge = jnp.dot(feat_local, w_charge, preferred_element_type=jnp.float32)
    charge = jnp.where(live, charge, jnp.zeros_like(charge))
    cycle_x = lax.axis_size("dx")
    cycle_y = lax.axis_size("dy")
    mesh_x = GRID_X * cycle_x
    mesh_y = GRID_Y * cycle_y
    mesh_z = GRID_Z
    density = jax.ops.segment_sum(
        charge, cells_local, num_segments=GRID_X * GRID_Y * GRID_Z
    ).reshape(GRID_X, GRID_Y, GRID_Z)
    real_z, imag_z = factored_transform(density, None, False)
    stacked = jnp.stack([real_z, imag_z])
    moved = lax.all_to_all(stacked, "dy", split_axis=3, concat_axis=2, tiled=True)
    real_y, imag_y = transform_axis(moved[0], moved[1], 1, False)
    moved = lax.all_to_all(
        jnp.stack([real_y, imag_y]), "dx", split_axis=2, concat_axis=1, tiled=True
    )
    real_x, imag_x = transform_axis(moved[0], moved[1], 0, False)
    cols_here = mesh_y // cycle_x
    depth_here = mesh_z // cycle_y
    sig_x = signed_block(0, mesh_x, mesh_x)[:, None, None]
    sig_y = signed_block(lax.axis_index("dx") * cols_here, cols_here, mesh_y)[None, :, None]
    sig_z = signed_block(lax.axis_index("dy") * depth_here, depth_here, mesh_z)[None, None, :]
    field_real, field_imag = field_spectra(
        jnp.stack([real_x, imag_x]), sig_x, sig_y, sig_z, mesh_x, mesh_y, mesh_z
    )
    back_real, back_imag = transform_axis(field_real, field_imag, 1, True)
    moved = lax.all_to_all(
        jnp.stack([back_real, back_imag], axis=1), "dx", split_axis=2, concat_axis=3, tiled=True
    )
    back_real, back_imag = transform_axis(moved[:, 0], moved[:, 1], 2, True)
    moved = lax.all_to_all(
        jnp.stack([back_real, back_imag], axis=1), "dy", split_axis=3, concat_axis=4, tiled=True
    )
    synth_real, synth_imag = factored_transform(moved[:, 0], moved[:, 1], True)
    scale = 1.0 / float(mesh_x * mesh_y * mesh_z)
    field = synth_real * scale
    sampled = jnp.take(field.reshape(3, -1), cells_local, axis=1)
    total = short + charge[None, :] * sampled
    total = jnp.where(live[None, :], total, jnp.zeros_like(total))
    return total[None, None]


def solution(mesh):
    placed = (
        P("dx", "dy", None, None),
        P("dx", "dy", None, None),
        P("dx", "dy"),
        P("dx", "dy", None),
        P("dx", "dy", None, None),
        P("dx", "dy", None),
        P(),
        P(),
        P(),
        P(),
        P(),
        P(),
        P(),
    )
    return jax.shard_map(
        shards, mesh=mesh, in_specs=placed, out_specs=P("dx", "dy", None, None), check_vma=False
    )
```

profile of v0, /device:TPU:0, one launch (start us, length us, event | category | flops | bytes accessed | tf_op | source)
XLA Modules:
  0.0 431.8 jit_solution(3234372355479331196)
XLA Ops:
  4.2 1.9 collective-permute-start.5
  12.8 3.8 scatter_custom_fusion
  19.4 4.9 %fusion.55 = f32[32,8,8,32]{3,0,2,1:T(8,128)S(1)} fusion(f32[32,8,8,32]{3,0,2,1:T(8,128)S(1)} %convolution_negate_fusion, f32[32,8,8,32]{3,0,2,1:T(8,128)S(1)} %fusion.110, f32[32,32]{1,0:T(8,128)S(1)} %copy.102, f32[32,32]{1,0:T(8,128)S(1)} %copy.101), kind=kOutput, calls=%fused_computation.101 | convolution fusion | flops 25376768 | bytes 794624 | tf_op jit(solution)/shard_map/...ks,sm->...mk/dot_general | solution.py:129
  24.3 4.9 %fusion.51 = f32[32,8,8,32]{3,0,2,1:T(8,128)S(1)} fusion(f32[32,8,8,32]{3,0,2,1:T(8,128)S(1)} %fusion.110, f32[32,8,8,32]{3,0,2,1:T(8,128)S(1)} %convolution_negate_fusion, f32[32,32]{1,0:T(8,128)S(1)} %copy.102, f32[32,32]{1,0:T(8,128)S(1)} %copy.101), kind=kOutput, calls=%fused_computation.97 | convolution fusion | flops 25376768 | bytes 794624 | tf_op jit(solution)/shard_map/...ks,sm->...mk/dot_general | solution.py:129
  29.1 5.9 %fusion.42 = f32[8,8,32,32]{3,2,1,0:T(8,128)} fusion(f32[32,8,8,32]{3,0,2,1:T(8,128)S(1)} %fusion.55, f32[32,8,8,32]{3,0,2,1:T(8,128)S(1)} %fusion.110, f32[32,8,8,32]{3,0,2,1:T(8,128)S(1)} %convolution_negate_fusion, f32[32,32]{1,0:T(8,128)S(1)} %copy.102, f32[32,32]{1,0:T(8,128)S(1)} %copy.101), kind=kOutput, calls=%fused_computation.78 | convolution fusion | flops 25442304 | bytes 1056768 | tf_op jit(solution)/shard_map/...ks,sm->...mk/dot_general | solution.py:129
  36.7 5.9 %fusion.41 = f32[8,8,32,32]{3,2,1,0:T(8,128)} fusion(f32[32,8,8,32]{3,0,2,1:T(8,128)S(1)} %fusion.51, f32[32,8,8,32]{3,0,2,1:T(8,128)S(1)} %convolution_negate_fusion, f32[32,8,8,32]{3,0,2,1:T(8,128)S(1)} %fusion.110, f32[32,32]{1,0:T(8,128)S(1)} %copy.102, f32[32,32]{1,0:T(8,128)S(1)} %copy.101), kind=kOutput, calls=%fused_computation.76 | convolution fusion | flops 25442304 | bytes 1056768 | tf_op jit(solution)/shard_map/...ks,sm->...mk/dot_general | solution.py:129
  44.5 6.0 %copy.103 = f32[2,8,8,1024]{2,1,0,3:T(8,128)} copy(f32[2,8,8,1024]{3,2,1,0:T(8,128)S(1)} %pad_maximum_fusion.9) | data formatting | bytes 1048576 | tf_op jit(solution)/shard_map/stack | solution.py:279
  50.5 7.4 %reshape.646 = f32[8,1,16384]{2,1,0:T(1,128)} reshape(f32[1024,2,8,8]{3,2,1,0:T(8,128)} %bitcast.321) | data formatting | bytes 1048576
  57.9 6.6 %all-to-all-start = ((f32[8,1,16384]{2,1,0:T(1,128)}), f32[8,1,16384]{2,1,0:T(1,128)S(1)}, u32[]{:S(2)}, u32[]{:S(2)}) async-start(f32[8,1,16384]{2,1,0:T(1,128)} %reshape.646), calls=%async_computation | async-start | bytes 1048576 | tf_op jit(solution)/shard_map/all_to_all | solution.py:280
  66.3 12.7 %all-to-all-done = f32[8,1,16384]{2,1,0:T(1,128)S(1)} async-done(((f32[8,1,16384]{2,1,0:T(1,128)}), f32[8,1,16384]{2,1,0:T(1,128)S(1)}, u32[]{:S(2)}, u32[]{:S(2)}) %all-to-all-start) | async-done | bytes 524320 | tf_op jit(solution)/shard_map/all_to_all | solution.py:280
  79.5 1.9 reduce.9
  81.4 7.8 %reshape.647 = f32[1024,2,8,8]{3,2,1,0:T(8,128)} reshape(f32[8,16384]{1,0:T(8,128)S(1)} %reduce.9) | data formatting | bytes 1048576
  89.2 5.1 %copy.104 = f32[2,8,8,8,128]{4,2,3,1,0:T(8,128)S(1)} copy(f32[2,8,8,8,128]{2,1,0,4,3:T(8,128)} %bitcast.322) | data formatting | bytes 1048576 | tf_op jit(solution)/shard_map/all_to_all | solution.py:280
  97.5 3.5 all-to-all-start.1
  105.5 3.4 collective-permute-start.3
  115.6 2.1 copy.107
  117.6 3.6 all-to-all-start.2
  126.2 3.2 collective-permute-start.7
  131.0 4.2 collective-permute-done.6
  135.2 2.2 collective-permute-done.7
  138.8 2.4 all-to-all-done.2
  145.4 2.1 copy.109
  147.5 4.7 %all-to-all-start.3 = ((f32[3,2,8,64,128]{4,2,0,1,3:T(8,128)}), f32[3,2,8,64,128]{4,2,0,1,3:T(8,128)}, u32[]{:S(2)}, u32[]{:S(2)}) async-start(f32[3,2,8,64,128]{4,2,0,1,3:T(8,128)} %copy.109), calls=%async_computation.3 | async-start | bytes 3145728 | tf_op jit(solution)/shard_map/all_to_all | solution.py:299
  152.2 194.2 %while.11 = (s32[]{:T(128)}, f32[6,3,64]{2,1,0:T(4,128)}, s32[6,64,32]{2,1,0:T(8,128)}, f32[3,2688]{0,1:T(8,128)}, f32[6,3,64]{1,2,0:T(8,128)}, /*index=5*/f32[8...) while((s32[]{:T(128)}, f32[6,3,64]{2,1,0:T(4,128)}, ...), condition=%wide.region_6.7_spmd.clone, body=%wide.region_0.6_spmd.clone.sunk | while | flops 1117030400 | bytes 18343244 | solution.py:95
  153.1 6.8 %gather_fusion.1 = f32[2048,3]{1,0:T(8,128)S(1)} fusion(f32[3,2688]{0,1:T(8,128)} %get-tuple-element.269, s32[2048]{0:T(1024)S(1)} %broadcast_clamp_fusion.2), kind=kCustom, calls=%fused_computation.clone.clone.1 | custom fusion | bytes 57344 | tf_op jit(solution)/shard_map/while/body/eval_jaxpr/jit(_take)/gather | solution.py:60
  162.1 7.5 %gather_fusion = bf16[2048,256]{1,0:T(8,128)(2,1)S(1)} fusion(bf16[2688,256]{1,0:T(8,128)(2,1)S(1)} %get-tuple-element.273, s32[2048]{0:T(1024)S(1)} %broadcast_clamp_fusion.2), kind=kCustom, calls=%fused_computation.1.clone.clone.1 | custom fusion | bytes 2105344 | tf_op jit(solution)/shard_map/while/body/eval_jaxpr/jit(_take)/gather | solution.py:57
  172.3 1.9 multiply_convert_fusion.8
  174.3 5.7 %bitcast_reduce_fusion.2 = (f32[64,128]{1,0:T(8,128)}, f32[2048,128]{1,0:T(8,128)}) fusion(bf16[2048,256]{1,0:T(8,128)(2,1)} %copy-done.3, f32[2048]{0:T(1024)S(1)} %maximum_multiply_fusion.2, bf16[1024,128]{1,0:T(8,128)(2,1)S(1)} %copy-done.23, bf16[2048,128]{1,0:T(8,128)(2,1)S(1)} %multiply_convert_fusion.8, bf16[128,1024]{1,0:T(8,128)(2,1)S(1)} %copy-done.22), kind=kOutput, calls=%fused_computation.49.clone.1 | convolution fusion | flops 1085267968 | bytes 2662400 | tf_op jit(solution)/shard_map/while/body/eval_jaxpr/dot_general | solution.py:82
  180.8 2.2 multiply_reduce_fusion.6
  185.5 6.8 %gather_fusion.1 = f32[2048,3]{1,0:T(8,128)S(1)} fusion(f32[3,2688]{0,1:T(8,128)} %get-tuple-element.269, s32[2048]{0:T(1024)S(1)} %broadcast_clamp_fusion.2), kind=kCustom, calls=%fused_computation.clone.clone.1 | custom fusion | bytes 57344 | tf_op jit(solution)/shard_map/while/body/eval_jaxpr/jit(_take)/gather | solution.py:60
  194.4 7.5 %gather_fusion = bf16[2048,256]{1,0:T(8,128)(2,1)S(1)} fusion(bf16[2688,256]{1,0:T(8,128)(2,1)S(1)} %get-tuple-element.273, s32[2048]{0:T(1024)S(1)} %broadcast_clamp_fusion.2), kind=kCustom, calls=%fused_computation.1.clone.clone.1 | custom fusion | bytes 2105344 | tf_op jit(solution)/shard_map/while/body/eval_jaxpr/jit(_take)/gather | solution.py:57
  204.7 1.9 multiply_convert_fusion.8
  206.7 5.7 %bitcast_reduce_fusion.2 = (f32[64,128]{1,0:T(8,128)}, f32[2048,128]{1,0:T(8,128)}) fusion(bf16[2048,256]{1,0:T(8,128)(2,1)} %copy-done.3, f32[2048]{0:T(1024)S(1)} %maximum_multiply_fusion.2, bf16[1024,128]{1,0:T(8,128)(2,1)S(1)} %copy-done.23, bf16[2048,128]{1,0:T(8,128)(2,1)S(1)} %multiply_convert_fusion.8, bf16[128,1024]{1,0:T(8,128)(2,1)S(1)} %copy-done.22), kind=kOutput, calls=%fused_computation.49.clone.1 | convolution fusion | flops 1085267968 | bytes 2662400 | tf_op jit(solution)/shard_map/while/body/eval_jaxpr/dot_general | solution.py:82
  213.1 2.2 multiply_reduce_fusion.6
  217.9 6.8 %gather_fusion.1 = f32[2048,3]{1,0:T(8,128)S(1)} fusion(f32[3,2688]{0,1:T(8,128)} %get-tuple-element.269, s32[2048]{0:T(1024)S(1)} %broadcast_clamp_fusion.2), kind=kCustom, calls=%fused_computation.clone.clone.1 | custom fusion | bytes 57344 | tf_op jit(solution)/shard_map/while/body/eval_jaxpr/jit(_take)/gather | solution.py:60
  226.8 7.5 %gather_fusion = bf16[2048,256]{1,0:T(8,128)(2,1)S(1)} fusion(bf16[2688,256]{1,0:T(8,128)(2,1)S(1)} %get-tuple-element.273, s32[2048]{0:T(1024)S(1)} %broadcast_clamp_fusion.2), kind=kCustom, calls=%fused_computation.1.clone.clone.1 | custom fusion | bytes 2105344 | tf_op jit(solution)/shard_map/while/body/eval_jaxpr/jit(_take)/gather | solution.py:57
  237.1 1.9 multiply_convert_fusion.8
  239.0 5.7 %bitcast_reduce_fusion.2 = (f32[64,128]{1,0:T(8,128)}, f32[2048,128]{1,0:T(8,128)}) fusion(bf16[2048,256]{1,0:T(8,128)(2,1)} %copy-done.3, f32[2048]{0:T(1024)S(1)} %maximum_multiply_fusion.2, bf16[1024,128]{1,0:T(8,128)(2,1)S(1)} %copy-done.23, bf16[2048,128]{1,0:T(8,128)(2,1)S(1)} %multiply_convert_fusion.8, bf16[128,1024]{1,0:T(8,128)(2,1)S(1)} %copy-done.22), kind=kOutput, calls=%fused_computation.49.clone.1 | convolution fusion | flops 1085267968 | bytes 2662400 | tf_op jit(solution)/shard_map/while/body/eval_jaxpr/dot_general | solution.py:82
  245.5 2.2 multiply_reduce_fusion.6
  250.2 6.8 %gather_fusion.1 = f32[2048,3]{1,0:T(8,128)S(1)} fusion(f32[3,2688]{0,1:T(8,128)} %get-tuple-element.269, s32[2048]{0:T(1024)S(1)} %broadcast_clamp_fusion.2), kind=kCustom, calls=%fused_computation.clone.clone.1 | custom fusion | bytes 57344 | tf_op jit(solution)/shard_map/while/body/eval_jaxpr/jit(_take)/gather | solution.py:60
  259.2 7.5 %gather_fusion = bf16[2048,256]{1,0:T(8,128)(2,1)S(1)} fusion(bf16[2688,256]{1,0:T(8,128)(2,1)S(1)} %get-tuple-element.273, s32[2048]{0:T(1024)S(1)} %broadcast_clamp_fusion.2), kind=kCustom, calls=%fused_computation.1.clone.clone.1 | custom fusion | bytes 2105344 | tf_op jit(solution)/shard_map/while/body/eval_jaxpr/jit(_take)/gather | solution.py:57
  269.4 1.9 multiply_convert_fusion.8
  271.4 5.7 %bitcast_reduce_fusion.2 = (f32[64,128]{1,0:T(8,128)}, f32[2048,128]{1,0:T(8,128)}) fusion(bf16[2048,256]{1,0:T(8,128)(2,1)} %copy-done.3, f32[2048]{0:T(1024)S(1)} %maximum_multiply_fusion.2, bf16[1024,128]{1,0:T(8,128)(2,1)S(1)} %copy-done.23, bf16[2048,128]{1,0:T(8,128)(2,1)S(1)} %multiply_convert_fusion.8, bf16[128,1024]{1,0:T(8,128)(2,1)S(1)} %copy-done.22), kind=kOutput, calls=%fused_computation.49.clone.1 | convolution fusion | flops 1085267968 | bytes 2662400 | tf_op jit(solution)/shard_map/while/body/eval_jaxpr/dot_general | solution.py:82
  277.9 2.2 multiply_reduce_fusion.6
  282.6 6.8 %gather_fusion.1 = f32[2048,3]{1,0:T(8,128)S(1)} fusion(f32[3,2688]{0,1:T(8,128)} %get-tuple-element.269, s32[2048]{0:T(1024)S(1)} %broadcast_clamp_fusion.2), kind=kCustom, calls=%fused_computation.clone.clone.1 | custom fusion | bytes 57344 | tf_op jit(solution)/shard_map/while/body/eval_jaxpr/jit(_take)/gather | solution.py:60
  291.5 7.5 %gather_fusion = bf16[2048,256]{1,0:T(8,128)(2,1)S(1)} fusion(bf16[2688,256]{1,0:T(8,128)(2,1)S(1)} %get-tuple-element.273, s32[2048]{0:T(1024)S(1)} %broadcast_clamp_fusion.2), kind=kCustom, calls=%fused_computation.1.clone.clone.1 | custom fusion | bytes 2105344 | tf_op jit(solution)/shard_map/while/body/eval_jaxpr/jit(_take)/gather | solution.py:57
  301.8 1.9 multiply_convert_fusion.8
  303.8 5.7 %bitcast_reduce_fusion.2 = (f32[64,128]{1,0:T(8,128)}, f32[2048,128]{1,0:T(8,128)}) fusion(bf16[2048,256]{1,0:T(8,128)(2,1)} %copy-done.3, f32[2048]{0:T(1024)S(1)} %maximum_multiply_fusion.2, bf16[1024,128]{1,0:T(8,128)(2,1)S(1)} %copy-done.23, bf16[2048,128]{1,0:T(8,128)(2,1)S(1)} %multiply_convert_fusion.8, bf16[128,1024]{1,0:T(8,128)(2,1)S(1)} %copy-done.22), kind=kOutput, calls=%fused_computation.49.clone.1 | convolution fusion | flops 1085267968 | bytes 2662400 | tf_op jit(solution)/shard_map/while/body/eval_jaxpr/dot_general | solution.py:82
  310.3 2.2 multiply_reduce_fusion.6
  315.0 6.8 %gather_fusion.1 = f32[2048,3]{1,0:T(8,128)S(1)} fusion(f32[3,2688]{0,1:T(8,128)} %get-tuple-element.269, s32[2048]{0:T(1024)S(1)} %broadcast_clamp_fusion.2), kind=kCustom, calls=%fused_computation.clone.clone.1 | custom fusion | bytes 57344 | tf_op jit(solution)/shard_map/while/body/eval_jaxpr/jit(_take)/gather | solution.py:60
  323.9 7.5 %gather_fusion = bf16[2048,256]{1,0:T(8,128)(2,1)S(1)} fusion(bf16[2688,256]{1,0:T(8,128)(2,1)S(1)} %get-tuple-element.273, s32[2048]{0:T(1024)S(1)} %broadcast_clamp_fusion.2), kind=kCustom, calls=%fused_computation.1.clone.clone.1 | custom fusion | bytes 2105344 | tf_op jit(solution)/shard_map/while/body/eval_jaxpr/jit(_take)/gather | solution.py:57
  334.2 1.9 multiply_convert_fusion.8
  336.2 5.7 %bitcast_reduce_fusion.2 = (f32[64,128]{1,0:T(8,128)}, f32[2048,128]{1,0:T(8,128)}) fusion(bf16[2048,256]{1,0:T(8,128)(2,1)} %copy-done.3, f32[2048]{0:T(1024)S(1)} %maximum_multiply_fusion.2, bf16[1024,128]{1,0:T(8,128)(2,1)S(1)} %copy-done.23, bf16[2048,128]{1,0:T(8,128)(2,1)S(1)} %multiply_convert_fusion.8, bf16[128,1024]{1,0:T(8,128)(2,1)S(1)} %copy-done.22), kind=kOutput, calls=%fused_computation.49.clone.1 | convolution fusion | flops 1085267968 | bytes 2662400 | tf_op jit(solution)/shard_map/while/body/eval_jaxpr/dot_general | solution.py:82
  342.7 2.2 multiply_reduce_fusion.6
  350.5 2.1 reshape_squeeze.11
  352.6 4.5 %fusion.115 = f32[32,3,8,8,32]{4,0,3,2,1:T(8,128)} fusion(f32[3,8,8,32,32]{4,3,2,1,0:T(8,128)S(1)} %reshape_squeeze.11), kind=kOutput, calls=%fused_computation.198 | convolution fusion | flops 75511808 | bytes 1572864 | tf_op jit(solution)/shard_map/...ts,tk->...ks/dot_general | solution.py:129
  357.1 3.4 reshape_squeeze.10
  360.5 4.9 %fusion.117 = f32[32,3,8,8,32]{4,0,3,2,1:T(8,128)S(1)} fusion(f32[3,8,8,32,32]{4,3,2,1,0:T(8,128)} %reshape_squeeze.10), kind=kOutput, calls=%fused_computation.200 | convolution fusion | flops 75511808 | bytes 1572864 | tf_op jit(solution)/shard_map/...ts,tk->...ks/dot_general | solution.py:129
  365.5 3.0 convolution_add_fusion.1
  368.5 3.0 convolution_subtract_fusion
  371.5 14.6 %fusion.25 = f32[32,3,8,8,32]{4,0,3,2,1:T(8,128)S(1)} fusion(f32[32,3,8,8,32]{4,0,3,2,1:T(8,128)S(1)} %convolution_subtract_fusion, f32[32,3,8,8,32]{4,0,3,2,1:T(8,128)S(1)} %convolution_add_fusion.1, f32[32,32]{1,0:T(8,128)S(1)} %copy-done.10, f32[32,32]{1,0:T(8,128)S(1)} %copy-done.8), kind=kOutput, calls=%fused_computation.55 | convolution fusion | flops 76101632 | bytes 2367488 | tf_op jit(solution)/shard_map/...ks,sm->...mk/dot_general | solution.py:129
  386.1 14.4 %multiply_bitcast_fusion = f32[3,8,8,32,32]{4,3,2,1,0:T(8,128)S(1)} fusion(f32[32,3,8,8,32]{4,0,3,2,1:T(8,128)S(1)} %fusion.25, f32[32,3,8,8,32]{4,0,3,2,1:T(8,128)S(1)} %convolution_add_fusion.1, f32[32,3,8,8,32]{4,0,3,2,1:T(8,128)S(1)} %convolution_subtract_fusion, f32[32,32]{1,0:T(8,128)S(1)} %copy-done.10, f32[32,32]{1,0:T(8,128)S(1)} %copy-done.8), kind=kOutput, calls=%fused_computation.59 | convolution fusion | flops 76494848 | bytes 3153920 | tf_op jit(solution)/shard_map/...ks,sm->...mk/dot_general | solution.py:129
  400.6 18.3 %copy.121 = f32[3,8,8,32,32]{0,4,3,2,1:T(8,128)} copy(f32[3,8,8,32,32]{4,3,2,1,0:T(8,128)S(1)} %multiply_bitcast_fusion) | data formatting | bytes 1572864 | tf_op jit(solution)/shard_map/mul | solution.py:304
  418.9 11.7 %gather_fusion.4 = f32[384,3]{1,0:T(8,128)S(1)} fusion(f32[3,65536]{0,1:T(8,128)} %bitcast.320, s32[1024]{0:T(1024)S(1)} %copy-done.16), kind=kCustom, calls=%fused_computation.4 | custom fusion | bytes 10752 | tf_op jit(solution)/shard_map/jit(_take)/gather | solution.py:305
  (316 shorter events, 98.8 us)
Async XLA Ops:
  0.0 138.3 %copy-start = (bf16[128,256]{1,0:T(8,128)(2,1)S(1)}, bf16[128,256]{1,0:T(8,128)(2,1)}, u32[]{:S(2)}) copy-start(bf16[128,256]{1,0:T(8,128)(2,1)} %param.22) | copy-start | bytes 196612
  3.8 119.9 %collective-permute-start.4 = (bf16[1,1,256,128]{3,2,1,0:T(8,128)(2,1)}, bf16[1,1,256,128]{3,2,1,0:T(8,128)(2,1)}, u32[]{:S(2)}, u32[]{:S(2)}) collective-permute-start(bf16[1,1,256,128]{3,2,1,0:T(8,128)(2,1)} %bitcast_select_fusion.3), channel_id=1, source_target_pairs={{0,8},{8,16},{16,24},{24,0},{1,9},{9,17},{17,25},{25,1},{2,10},{10... | collective-permute-start | bytes 196616 | tf_op jit(solution)/shard_map/ppermute | solution.py:26
  4.2 119.5 %collective-permute-start.5 = (bf16[1,1,256,128]{3,2,1,0:T(8,128)(2,1)}, bf16[1,1,256,128]{3,2,1,0:T(8,128)(2,1)}, u32[]{:S(2)}, u32[]{:S(2)}) collective-permute-start(bf16[1,1,256,128]{3,2,1,0:T(8,128)(2,1)} %bitcast_select_fusion.3), channel_id=1, source_target_pairs={{8,0},{16,8},{24,16},{0,24},{9,1},{17,9},{25,17},{1,25},{10,2},{18... | collective-permute-start | bytes 196616 | tf_op jit(solution)/shard_map/ppermute | solution.py:27
  7.0 5.1 %copy-start.11 = (bf16[1,1,3,384]{2,3,1,0:T(8,128)(2,1)}, bf16[1,1,3,384]{2,3,1,0:T(8,128)(2,1)S(1)}, u32[]{:S(2)}) copy-start(bf16[1,1,3,384]{2,3,1,0:T(8,128)(2,1)S(1)} %copy.93) | copy-start | bytes 6916
  8.6 93.4 %collective-permute-start = (bf16[1,1,3,256]{2,3,1,0:T(8,128)(2,1)}, bf16[1,1,3,256]{2,3,1,0:T(8,128)(2,1)}, u32[]{:S(2)}, u32[]{:S(2)}) collective-permute-start(bf16[1,1,3,256]{2,3,1,0:T(8,128)(2,1)} %bitcast_select_fusion.2), channel_id=1, source_target_pairs={{0,8},{8,16},{16,24},{24,0},{1,9},{9,17},{17,25},{25,1},{2,10},{10... | collective-permute-start | bytes 4616 | tf_op jit(solution)/shard_map/ppermute | solution.py:26
  9.3 93.7 %collective-permute-start.1 = (bf16[1,1,3,256]{2,3,1,0:T(8,128)(2,1)}, bf16[1,1,3,256]{2,3,1,0:T(8,128)(2,1)}, u32[]{:S(2)}, u32[]{:S(2)}) collective-permute-start(bf16[1,1,3,256]{2,3,1,0:T(8,128)(2,1)} %bitcast_select_fusion.2), channel_id=1, source_target_pairs={{8,0},{16,8},{24,16},{0,24},{9,1},{17,9},{25,17},{1,25},{10,2},{18... | collective-permute-start | bytes 4616 | tf_op jit(solution)/shard_map/ppermute | solution.py:27
  12.1 4.5 %copy-start.17 = (f32[384]{0:T(512)}, f32[384]{0:T(512)S(1)}, u32[]{:S(2)}) copy-start(f32[384]{0:T(512)S(1)} %broadcast_select_fusion.1) | copy-start | bytes 4612
  19.3 17.4 %copy-start.7 = (f32[32,32]{1,0:T(8,128)}, f32[32,32]{1,0:T(8,128)S(1)}, u32[]{:S(2)}) copy-start(f32[32,32]{1,0:T(8,128)S(1)} %copy.101) | copy-start | bytes 12292
  19.4 17.4 %copy-start.9 = (f32[32,32]{1,0:T(8,128)}, f32[32,32]{1,0:T(8,128)S(1)}, u32[]{:S(2)}) copy-start(f32[32,32]{1,0:T(8,128)S(1)} %copy.102) | copy-start | bytes 12292
  50.5 14.1 %copy-start.19 = (s32[1,1,384]{2,1,0:T(1,128)S(1)}, s32[1,1,384]{2,1,0:T(1,128)}, u32[]{:S(2)}) copy-start(s32[1,1,384]{2,1,0:T(1,128)} %param.20) | copy-start | bytes 4612
  50.5 14.9 %copy-start.12 = (bf16[1,1,3,384]{2,3,1,0:T(8,128)(2,1)S(1)}, bf16[1,1,3,384]{2,3,1,0:T(8,128)(2,1)}, u32[]{:S(2)}) copy-start(bf16[1,1,3,384]{2,3,1,0:T(8,128)(2,1)} %copy-done.11) | copy-start | bytes 6916
  50.5 14.9 %copy-start.5 = (bf16[1,1,384,128]{3,2,1,0:T(8,128)(2,1)S(1)}, bf16[1,1,384,128]{3,2,1,0:T(8,128)(2,1)}, u32[]{:S(2)}) copy-start(bf16[1,1,384,128]{3,2,1,0:T(8,128)(2,1)} %param.15) | copy-start | bytes 294916
  50.5 14.9 %copy-start.14 = (bf16[128,128]{1,0:T(8,128)(2,1)S(1)}, bf16[128,128]{1,0:T(8,128)(2,1)}, u32[]{:S(2)}) copy-start(bf16[128,128]{1,0:T(8,128)(2,1)} %param.21) | copy-start | bytes 98308
  57.9 21.2 %all-to-all-start = ((f32[8,1,16384]{2,1,0:T(1,128)}), f32[8,1,16384]{2,1,0:T(1,128)S(1)}, u32[]{:S(2)}, u32[]{:S(2)}) async-start(f32[8,1,16384]{2,1,0:T(1,128)} %reshape.646), calls=%async_computation | async-start | bytes 1048576 | tf_op jit(solution)/shard_map/all_to_all | solution.py:280
  97.5 12.3 %all-to-all-start.1 = ((f32[2,8,64,128]{3,1,0,2:T(8,128)}), f32[2,8,64,128]{3,1,0,2:T(8,128)S(1)}, u32[]{:S(2)}, u32[]{:S(2)}) async-start(f32[2,8,64,128]{3,1,0,2:T(8,128)} %copy.105), calls=%async_computation.1 | async-start | bytes 1048576 | tf_op jit(solution)/shard_map/all_to_all | solution.py:282
  103.9 19.6 %collective-permute-start.2 = (bf16[3,1,3,256]{3,2,1,0:T(4,128)(2,1)S(1)}, bf16[3,1,3,256]{3,2,1,0:T(4,128)(2,1)S(1)}, u32[]{:S(2)}, u32[]{:S(2)}) collective-permute-start(bf16[3,1,3,256]{3,2,1,0:T(4,128)(2,1)S(1)} %pad_maximum_fusion.13), channel_id=1, source_target_pairs={{0,1},{1,2},{2,3},{3,4},{4,5},{5,6},{6,7},{7,0},{8,9},{9,10},{10,1... | collective-permute-start | bytes 13832 | tf_op jit(solution)/shard_map/ppermute | solution.py:26
  105.5 18.1 %collective-permute-start.3 = (bf16[3,1,3,256]{3,2,1,0:T(4,128)(2,1)S(1)}, bf16[3,1,3,256]{3,2,1,0:T(4,128)(2,1)S(1)}, u32[]{:S(2)}, u32[]{:S(2)}) collective-permute-start(bf16[3,1,3,256]{3,2,1,0:T(4,128)(2,1)S(1)} %pad_maximum_fusion.13), channel_id=1, source_target_pairs={{1,0},{2,1},{3,2},{4,3},{5,4},{6,5},{7,6},{0,7},{9,8},{10,9},{11,1... | collective-permute-start | bytes 13832 | tf_op jit(solution)/shard_map/ppermute | solution.py:27
  115.5 6.3 %copy-start.15 = (bf16[1,1,3,384]{3,2,1,0:T(4,128)(2,1)S(1)}, bf16[1,1,3,384]{3,2,1,0:T(4,128)(2,1)}, u32[]{:S(2)}) copy-start(bf16[1,1,3,384]{3,2,1,0:T(4,128)(2,1)} %param.16) | copy-start | bytes 6916
  115.6 7.2 %copy-start.13 = (s32[1,1,384,32]{2,3,1,0:T(8,128)S(1)}, s32[1,1,384,32]{2,3,1,0:T(8,128)}, u32[]{:S(2)}) copy-start(s32[1,1,384,32]{2,3,1,0:T(8,128)} %param.19) | copy-start | bytes 147460
  117.6 23.6 %all-to-all-start.2 = ((f32[3,2,32,16,128]{4,3,0,1,2:T(8,128)}), f32[3,2,32,16,128]{4,3,0,1,2:T(8,128)S(1)}, u32[]{:S(2)}, u32[]{:S(2)}) async-start(f32[3,2,32,16,128]{4,3,0,1,2:T(8,128)} %copy.107), calls=%async_computation.2 | async-start | bytes 3145728 | tf_op jit(solution)/shard_map/all_to_all | solution.py:295
  124.6 10.5 %collective-permute-start.6 = (bf16[3,1,256,128]{3,2,1,0:T(8,128)(2,1)S(1)}, bf16[3,1,256,128]{3,2,1,0:T(8,128)(2,1)S(1)}, u32[]{:S(2)}, u32[]{:S(2)}) collective-permute-start(bf16[3,1,256,128]{3,2,1,0:T(8,128)(2,1)S(1)} %pad_maximum_fusion.11), channel_id=1, source_target_pairs={{0,1},{1,2},{2,3},{3,4},{4,5},{5,6},{6,7},{7,0},{8,9},{9,10},{10,1... | collective-permute-start | bytes 589832 | tf_op jit(solution)/shard_map/ppermute | solution.py:26
  126.2 11.2 %collective-permute-start.7 = (bf16[3,1,256,128]{3,2,1,0:T(8,128)(2,1)S(1)}, bf16[3,1,256,128]{3,2,1,0:T(8,128)(2,1)S(1)}, u32[]{:S(2)}, u32[]{:S(2)}) collective-permute-start(bf16[3,1,256,128]{3,2,1,0:T(8,128)(2,1)S(1)} %pad_maximum_fusion.11), channel_id=1, source_target_pairs={{1,0},{2,1},{3,2},{4,3},{5,4},{6,5},{7,6},{0,7},{9,8},{10,9},{11,1... | collective-permute-start | bytes 589832 | tf_op jit(solution)/shard_map/ppermute | solution.py:27
  147.5 199.8 %all-to-all-start.3 = ((f32[3,2,8,64,128]{4,2,0,1,3:T(8,128)}), f32[3,2,8,64,128]{4,2,0,1,3:T(8,128)}, u32[]{:S(2)}, u32[]{:S(2)}) async-start(f32[3,2,8,64,128]{4,2,0,1,3:T(8,128)} %copy.109), calls=%async_computation.3 | async-start | bytes 3145728 | tf_op jit(solution)/shard_map/all_to_all | solution.py:299
  169.6 2.7 copy-start.6
  170.2 2.1 copy-start.24
  171.4 2.9 copy-start.3
  172.2 2.1 copy-start.22
  172.2 2.1 copy-start.23
  201.9 2.7 copy-start.6
  202.6 2.1 copy-start.24
  203.7 2.9 copy-start.3
  204.6 2.1 copy-start.22
  204.6 2.1 copy-start.23
  234.3 2.7 copy-start.6
  235.0 2.1 copy-start.24
  236.1 2.9 copy-start.3
  236.9 2.1 copy-start.22
  236.9 2.1 copy-start.23
  266.7 2.7 copy-start.6
  267.3 2.1 copy-start.24
  268.5 2.9 copy-start.3
  269.3 2.1 copy-start.22
  269.3 2.1 copy-start.23
  299.0 2.7 copy-start.6
  299.7 2.1 copy-start.24
  300.9 2.9 copy-start.3
  301.7 2.1 copy-start.22
  301.7 2.1 copy-start.23
  331.4 2.7 copy-start.6
  332.1 2.1 copy-start.24
  333.2 2.9 copy-start.3
  334.1 2.1 copy-start.22
  334.1 2.1 copy-start.23
  360.5 5.0 %copy-start.2 = (f32[3,8,8,32,32]{4,3,2,1,0:T(8,128)S(1)}, f32[3,8,8,32,32]{4,3,2,1,0:T(8,128)}, u32[]{:S(2)}) copy-start(f32[3,8,8,32,32]{4,3,2,1,0:T(8,128)} %reshape_squeeze.10) | copy-start | bytes 2359300
  360.5 5.0 %copy-start.4 = (f32[32,3,8,8,32]{4,0,3,2,1:T(8,128)S(1)}, f32[32,3,8,8,32]{4,0,3,2,1:T(8,128)}, u32[]{:S(2)}) copy-start(f32[32,3,8,8,32]{4,0,3,2,1:T(8,128)} %fusion.115) | copy-start | bytes 2359300
  368.5 3.0 copy-start.8
  368.5 3.0 copy-start.10
  400.5 18.4 %copy-start.16 = (s32[1024]{0:T(1024)S(1)}, s32[1024]{0:T(1024)}, u32[]{:S(2)}) copy-start(s32[1024]{0:T(1024)} %pad_clamp_fusion) | copy-start | bytes 12292
  400.6 30.1 %copy-start.18 = (f32[384]{0:T(512)S(1)}, f32[384]{0:T(512)}, u32[]{:S(2)}) copy-start(f32[384]{0:T(512)} %copy-done.17) | copy-start | bytes 4612
  400.6 30.1 %copy-start.20 = (pred[384]{0:T(512)(128)(4,1)S(1)}, pred[384]{0:T(512)(128)(4,1)}, u32[]{:S(2)}) copy-start(pred[384]{0:T(512)(128)(4,1)} %get-tuple-element.165) | copy-start | bytes 1156
  400.6 30.1 %copy-start.21 = (pred[384]{0:T(512)(128)(4,1)S(1)}, pred[384]{0:T(512)(128)(4,1)}, u32[]{:S(2)}) copy-start(pred[384]{0:T(512)(128)(4,1)} %get-tuple-element.166) | copy-start | bytes 1156
  400.6 31.0 %copy-start.1 = (bf16[128,256]{1,0:T(8,128)(2,1)S(1)}, bf16[128,256]{1,0:T(8,128)(2,1)}, u32[]{:S(2)}) copy-start(bf16[128,256]{1,0:T(8,128)(2,1)} %param.22) | copy-start | bytes 196612
where the time goes:
time: 438 us; the launch traced here: 432 us
  local copies, waits for them, and re-layouts  190 us (43%)
  matrix products  133 us (30%)
  other arithmetic  52.1 us (12%)
  starting transfers between devices  32.3 us (7%)
  waiting for transfers between devices  22.5 us (5%)
    dot_general x28, matrix products, apply_table(): return jnp.einsum(formula, values, table, precision=lax.Precision.HIGHEST)  79.2 us
    gather x6, local copies, waits for them, and re-layouts, one_block(): gathered = jnp.take(projected, flat_list, axis=0)  44.9 us
    gather x6, local copies, waits for them, and re-layouts, one_block(): far_coords = jnp.take(ext_coords, flat_list, axis=1)  40.8 us
    dot_general x6, matrix products, one_block(): mixed_out = jnp.dot(latent, w_contract, preferred_element_type=jnp.float32)  34 us
    unnamed x45, local copies, waits for them, and re-layouts  18.5 us
    mul x1, local copies, waits for them, and re-layouts, shards(): field = synth_real * scale  18.3 us
    reduce_sum x6, other arithmetic, one_block(): (displace[:, :, None] * weight[None]).reshape(3, -1, per_atom, channels)  13.1 us
    all_to_all x1, waiting for transfers between devices, shards(): lax.all_to_all(stacked, 'dy', split_axis=3, concat_axis=2, tiled=True)  12.7 us
  transfers between devices with their start and end apart: 12, of which 5 were waited for; matrix products, arithmetic and copies ran while one was open for 65% of the time, Pallas kernels for 0%

commit v1 on v0

v1 whole, which is shorter than its diff:
```python
import functools
import math

import jax
import jax.numpy as jnp
import numpy as np
from jax import lax
from jax.experimental import pallas as pl
from jax.experimental.pallas import tpu as pltpu
from jax.sharding import PartitionSpec as P

GRID_X = 8
GRID_Y = 8
GRID_Z = 1024
BOX = 1.0
CUTOFF_SQ = 6.25
SMEARING = 1.0

LANES = 128
EXTRA = 16
ROWS = 32
CHUNK_ATOMS = 16
HIGHEST = lax.Precision.HIGHEST
F32 = jnp.float32
BF16 = jnp.bfloat16


def contract_first(a, b, precision=None):
    return lax.dot_general(
        a, b, (((0,), (0,)), ((), ())), precision=precision, preferred_element_type=F32
    )


def contract_last(a, b, precision=None):
    return lax.dot_general(
        a, b, (((1,), (1,)), ((), ())), precision=precision, preferred_element_type=F32
    )


def prepare_kernel(count_ref, feat_ref, pos_ref, export_ref, cell_ref, wq_ref, out_ref, qc_ref):
    atoms = feat_ref.shape[0]
    ghosts = export_ref.shape[1]
    pick = lax.broadcasted_iota(jnp.int32, (atoms, ghosts), 0) == export_ref[...]
    pick = jnp.where(pick, 1.0, 0.0).astype(BF16)
    out_ref[pl.ds(0, ghosts), :] = contract_first(pick, feat_ref[...]).astype(BF16)
    pos = jnp.concatenate([pos_ref[...].astype(F32), jnp.zeros((13, atoms), F32)], axis=0)
    coords = jnp.dot(pos.astype(BF16), pick, preferred_element_type=F32)
    tail = [coords[:8, h * LANES : (h + 1) * LANES] for h in range(ghosts // LANES)]
    out_ref[pl.ds(ghosts, EXTRA), :] = jnp.concatenate(tail, axis=0).astype(BF16)
    weights = jnp.broadcast_to(wq_ref[...].astype(F32), (16, LANES)).astype(BF16)
    charge = contract_last(weights, feat_ref[...])[:1]
    live = lax.broadcasted_iota(jnp.int32, (1, atoms), 1) < count_ref[0, 0]
    qc_ref[...] = jnp.concatenate(
        [jnp.where(live, charge, 0.0), cell_ref[...].astype(F32)], axis=0
    )


def prepare(count, feat, pos, exports, cells, w_charge):
    atoms, ghosts = (feat.shape[0], exports.shape[0])
    vmem = pl.BlockSpec(memory_space=pltpu.VMEM)
    return pl.pallas_call(
        prepare_kernel,
        in_specs=[pl.BlockSpec(memory_space=pltpu.SMEM)] + [vmem] * 5,
        out_specs=[vmem, vmem],
        out_shape=[
            jax.ShapeDtypeStruct((ghosts + EXTRA, feat.shape[1]), BF16),
            jax.ShapeDtypeStruct((2, atoms), F32),
        ],
        name="prepare",
    )(count, feat, pos, exports[None], cells[None], w_charge[None])


def real_tables(count):
    half = count // 2
    index = np.arange(count)
    freq = np.where(index <= half, index, index - half)
    place = np.arange(count)
    angle = 2.0 * np.pi * (freq[:, None] * place[None, :] % count) / count
    is_cos = (index <= half)[:, None]
    basis = np.where(is_cos, np.cos(angle), np.sin(angle))
    weight = np.where((index == 0) | (index == half), 1.0, 2.0)[:, None] / count
    wave = np.where(index == half, 0.0, 2.0 * np.pi * freq / count)[:, None]
    slope = np.where(is_cos, np.sin(angle), -np.cos(angle)) * wave
    return (basis, (weight * basis).T, (weight * slope).T)


def split_table(table, copies):
    whole = np.kron(np.eye(copies), table).astype(np.float32)
    high = whole.astype(BF16)
    low = (whole - high.astype(np.float32)).astype(BF16)
    return np.concatenate([high, low], axis=1)


def sine_half(t):
    x = t * (math.pi / 512.0)
    s = x * x
    p = -2.50521084e-08
    p = p * s + 2.75573192e-06
    p = p * s - 1.98412698e-04
    p = p * s + 8.33333333e-03
    p = p * s - 1.66666667e-01
    return x + x * (s * p)


def grid_kernel(
    cycle_x, cycle_y, place_ref, qc_ref, fy_ref, fx_ref, ix_ref, iy_ref, dy_ref, out_ref,
    buf_a, buf_b, buf_c, buf_d, buf_e, trig_ref,
):
    mesh_x, mesh_y, mesh_z = (GRID_X * cycle_x, GRID_Y * cycle_y, GRID_Z)
    devices = cycle_x * cycle_y
    modes = mesh_z // 2 // devices
    coefs = 2 * modes
    first = place_ref[0] * modes
    columns = GRID_X * GRID_Y
    group_y = max(1, 256 // mesh_y)
    group_x = max(1, 256 // mesh_x)
    atoms = qc_ref.shape[2]

    row = lax.broadcasted_iota(jnp.int32, (ROWS, 1), 0) % coefs
    row_mode = first + row % modes
    row_sine = row >= modes
    row_edge = row_sine & (row_mode == 0)
    row_factor = jnp.where(row_edge, mesh_z // 2, row_mode)
    row_shift = jnp.where(row_sine & (row_mode != 0), mesh_z // 4, 0)
    column_iota = lax.broadcasted_iota(jnp.int32, (columns, atoms), 0)

    def columns_of(device):
        cell = qc_ref[device, 1:2, :].astype(jnp.int32)
        return cell, column_iota == lax.shift_right_logical(cell, 10)

    def spread(device, carry):
        cell, match = columns_of(device)
        depth = cell & (mesh_z - 1)
        turn = (row_factor * depth - row_shift) & (mesh_z - 1)
        trig = sine_half((jnp.abs(turn - mesh_z // 2) - mesh_z // 4).astype(F32))
        high = trig.astype(BF16)
        trig_ref[device, pl.ds(0, ROWS), :] = high
        trig_ref[device, pl.ds(ROWS, ROWS), :] = (trig - high.astype(F32)).astype(BF16)
        charged = trig * qc_ref[device, 0:1, :]
        high = charged.astype(BF16)
        low = (charged - high.astype(F32)).astype(BF16)
        pick = jnp.where(match, 1.0, 0.0).astype(BF16)
        copies = LANES // ROWS
        total = contract_last(pick, jnp.concatenate([high] * copies, axis=0))
        total += contract_last(pick, jnp.concatenate([low] * copies, axis=0))
        buf_a[pl.ds(device * columns, columns), :] = total
        return carry

    lax.fori_loop(0, devices, spread, 0)

    lane = lax.broadcasted_iota(jnp.int32, (1, LANES), 1)
    low_half = lane >= LANES // 2

    def apply(table_ref, data):
        high = data.astype(BF16).astype(F32)
        mixed = jnp.where(low_half, data - high, high).astype(BF16)
        both = jnp.concatenate([mixed, mixed], axis=0)
        result = jnp.dot(table_ref[...], both, preferred_element_type=F32)
        return result + pltpu.roll(result, LANES // 2, 1)

    def forward_y(step, carry):
        parts = []
        for i in range(group_y):
            place = step * group_y + i
            for sy in range(cycle_y):
                start = ((place // GRID_X) * cycle_y + sy) * columns + (place % GRID_X) * GRID_Y
                parts.append(buf_a[pl.ds(pl.multiple_of(start, 8), GRID_Y), :])
        size = group_y * mesh_y
        start = pl.multiple_of(step * size, 8)
        buf_b[pl.ds(start, size), :] = apply(fy_ref, jnp.concatenate(parts, axis=0))
        return carry

    lax.fori_loop(0, mesh_x // group_y, forward_y, 0)

    size_x = group_x * mesh_x
    lane_coef = lane % coefs
    lane_mode = first + lane_coef % modes
    lane_sine = lane_coef >= modes
    lane_freq = jnp.where(lane_sine & (lane_mode == 0), mesh_z // 2, lane_mode)
    wave_z = lane_freq.astype(F32) * (2.0 * math.pi / mesh_z)
    lane_weight = jnp.where(lane_mode == 0, 1.0, 2.0) / mesh_z
    slope_z = jnp.where(lane_mode == 0, 0.0, wave_z) * jnp.where(lane_sine, 1.0, -1.0)
    index_x = lax.broadcasted_iota(jnp.int32, (size_x, 1), 0)
    freq_x = index_x % mesh_x
    freq_x = jnp.where(freq_x <= mesh_x // 2, freq_x, freq_x - mesh_x // 2)
    wave_x = freq_x.astype(F32) * (2.0 * math.pi / mesh_x)
    near = wave_x * wave_x + wave_z * wave_z

    def middle(step, carry):
        parts = []
        for i in range(group_x):
            parts.append(buf_b[pl.ds(step * group_x + i, mesh_x, stride=mesh_y), :])
        spectrum = apply(fx_ref, jnp.concatenate(parts, axis=0))
        freq_y = step * group_x + index_x // mesh_x
        freq_y = jnp.where(freq_y <= mesh_y // 2, freq_y, freq_y - mesh_y // 2)
        wave_y = freq_y.astype(F32) * (2.0 * math.pi / mesh_y)
        wave_sq = near + wave_y * wave_y
        zero = wave_sq == 0.0
        green = jnp.exp(-0.5 * SMEARING * SMEARING * wave_sq) / jnp.where(zero, 1.0, wave_sq)
        green = jnp.where(zero, 0.0, 4.0 * math.pi * green)
        both = apply(ix_ref, spectrum * (green * lane_weight))
        start = pl.multiple_of(step * size_x, 8)
        buf_a[pl.ds(start, size_x), :] = both[:size_x]
        buf_c[pl.ds(start, size_x), :] = both[size_x:]
        return carry

    lax.fori_loop(0, mesh_y // group_x, middle, 0)

    def backward_y(step, carry):
        plain, sloped = ([], [])
        for i in range(group_y):
            place = step * group_y + i
            plain.append(buf_a[pl.ds(place, mesh_y, stride=mesh_x), :])
            sloped.append(buf_c[pl.ds(place, mesh_y, stride=mesh_x), :])
        plain = jnp.concatenate(plain, axis=0)
        size = group_y * mesh_y
        start = pl.multiple_of(step * size, 8)
        potential = apply(iy_ref, plain)
        buf_b[pl.ds(start, size), :] = apply(iy_ref, jnp.concatenate(sloped, axis=0))
        buf_d[pl.ds(start, size), :] = apply(dy_ref, plain)
        buf_e[pl.ds(start, size), :] = pltpu.roll(potential, modes, 1) * slope_z
        return carry

    lax.fori_loop(0, mesh_x // group_y, backward_y, 0)

    use_low = (lane // ROWS) == 1
    use_none = (lane % ROWS) >= coefs

    def sample(device, carry):
        _, match = columns_of(device)
        rows = []
        for buf in (buf_b, buf_d, buf_e):
            for lx in range(GRID_X):
                place = (device // cycle_y) * GRID_X + lx
                start = place * mesh_y + (device % cycle_y) * GRID_Y
                rows.append(buf[pl.ds(pl.multiple_of(start, 8), GRID_Y), :])
        data = jnp.concatenate(rows, axis=0)
        high = data.astype(BF16).astype(F32)
        mixed = jnp.where(use_low, data - high, high)
        mixed = jnp.where(use_none, 0.0, mixed).astype(BF16)
        high = trig_ref[device, pl.ds(0, ROWS), :]
        low = trig_ref[device, pl.ds(ROWS, ROWS), :]
        waves = jnp.concatenate([high, high, low, jnp.zeros_like(low)], axis=0)
        fields = jnp.dot(mixed, waves, preferred_element_type=F32)
        picked = []
        for a in range(3):
            part = jnp.where(match, fields[a * columns : (a + 1) * columns], 0.0)
            picked.append(jnp.sum(part, axis=0, keepdims=True))
        out_ref[device] = jnp.concatenate(picked, axis=0)
        return carry

    lax.fori_loop(0, devices, sample, 0)


def grid_fields(place, gathered, cycle_x, cycle_y):
    mesh_x, mesh_y = (GRID_X * cycle_x, GRID_Y * cycle_y)
    devices, _, atoms = gathered.shape
    group_y = max(1, 256 // mesh_y)
    group_x = max(1, 256 // mesh_x)
    ax, bx, cx = real_tables(mesh_x)
    ay, by, cy = real_tables(mesh_y)
    tables = [
        split_table(ay, group_y),
        split_table(ax, group_x),
        np.concatenate([split_table(bx, group_x), split_table(cx, group_x)], axis=0),
        split_table(by, group_y),
        split_table(cy, group_y),
    ]
    plane = pltpu.VMEM((mesh_x * mesh_y, LANES), F32)
    vmem = pl.BlockSpec(memory_space=pltpu.VMEM)
    return pl.pallas_call(
        functools.partial(grid_kernel, cycle_x, cycle_y),
        in_specs=[pl.BlockSpec(memory_space=pltpu.SMEM)] + [vmem] * 6,
        out_specs=vmem,
        out_shape=jax.ShapeDtypeStruct((devices, 3, atoms), F32),
        scratch_shapes=[plane] * 5 + [pltpu.VMEM((devices, 2 * ROWS, atoms), BF16)],
        compiler_params=pltpu.CompilerParams(vmem_limit_bytes=60 << 20),
        cost_estimate=pl.CostEstimate(
            flops=8_000_000_000, bytes_accessed=4_000_000, transcendentals=100_000
        ),
        name="grid_fields",
    )(place, gathered, *[jnp.asarray(t) for t in tables])


def edge_kernel(
    list_ref, feat_ref, pos_ref, mid_ref, up_ref, down_ref, w_self_ref, w_pair_ref, w_radial_ref,
    w_expand_ref, w_contract_ref, w_final_ref, out_ref,
    table, near_a, near_b, own_ref, sums_ref,
):
    atoms, channels = feat_ref.shape
    ghosts = mid_ref.shape[1] - EXTRA
    per_atom = list_ref.shape[0] // atoms
    chunk = CHUNK_ATOMS * per_atom
    chunks = atoms // CHUNK_ATOMS
    basis_count = w_radial_ref.shape[0]
    spacing = CUTOFF_SQ / (basis_count - 1)

    def column_of(index, size):
        rows = lax.broadcasted_iota(jnp.int32, (8, 3 * LANES), 0)
        cols = lax.broadcasted_iota(jnp.int32, (8, 3 * LANES), 1) // LANES
        return jnp.where(rows == cols, 1.0, 0.0)

    spread = column_of(0, 0)

    def fill(start, rows, coords, shift):
        projected = jnp.dot(rows, w_pair_ref[...], preferred_element_type=F32)
        projected = projected.astype(BF16).astype(F32)
        count = rows.shape[0]
        wide = contract_first(coords, spread, HIGHEST)
        parts = [projected[:, :channels] * 0.5, projected[:, channels:]]
        for a in range(3):
            part = wide[:, a * LANES : (a + 1) * LANES]
            parts.append(part + shift[a] if shift[a] != 0.0 else part)
        for s, part in enumerate(parts):
            table[pl.ds(start * 8 + s, count, stride=8), :] = part
        return parts

    pos = jnp.concatenate([pos_ref[...].astype(F32), jnp.zeros((5, atoms), F32)], axis=0)
    for i in range(atoms // LANES):
        rows = feat_ref[pl.ds(i * LANES, LANES), :]
        parts = fill(i * LANES, rows, pos[:, i * LANES : (i + 1) * LANES], (0.0, 0.0, 0.0))
        own = jnp.dot(rows, w_self_ref[...], preferred_element_type=F32)
        own_ref[0, pl.ds(i * LANES, LANES), :] = own * 0.5
        for a in range(3):
            own_ref[1 + a, pl.ds(i * LANES, LANES), :] = parts[2 + a]
    for sx in range(3):
        for sy, ref in enumerate((up_ref, mid_ref, down_ref)):
            block = 3 * sx + sy
            if block == 4:
                continue
            tail = ref[sx, pl.ds(ghosts, EXTRA), :].astype(F32)
            shift = ((sx - 1) * BOX, (sy - 1) * BOX, 0.0)
            for h in range(ghosts // LANES):
                rows = ref[sx, pl.ds(h * LANES, LANES), :]
                start = atoms + block * ghosts + h * LANES
                fill(start, rows, tail[h * 8 : (h + 1) * 8], shift)

    w_radial = w_radial_ref[...] * 0.5
    high = w_radial.astype(BF16).astype(F32)
    w_basis = jnp.concatenate(
        [high, high, w_radial - high, jnp.zeros((LANES - 3 * basis_count, channels), F32)], axis=0
    ).astype(BF16)
    lane = lax.broadcasted_iota(jnp.int32, (1, LANES), 1)
    center = (lane % basis_count).astype(F32)
    use_low = (lane // basis_count) == 1

    def gather(index, near):
        for a in range(CHUNK_ATOMS):
            for k in range(per_atom):
                j = pl.multiple_of(list_ref[(index * CHUNK_ATOMS + a) * per_atom + k], 8)
                e = k * CHUNK_ATOMS + a
                near[pl.ds(e * 8, 8), :] = table[pl.ds(j, 8), :]

    def work(index, near):
        first = pl.multiple_of(index * CHUNK_ATOMS, 8)

        def per_edge(s):
            return near[pl.ds(s, chunk, stride=8), :].reshape(per_atom, CHUNK_ATOMS, LANES)

        def own(s):
            return own_ref[s, pl.ds(first, CHUNK_ATOMS), :][None]

        disp = [per_edge(2 + a) - own(1 + a) for a in range(3)]
        d2 = disp[0] * disp[0] + disp[1] * disp[1] + disp[2] * disp[2]
        t = (d2 * (1.0 / spacing)).reshape(chunk, LANES) - center
        basis = jnp.exp(-(t * t))
        basis_high = basis.astype(BF16).astype(F32)
        mixed = jnp.where(use_low, basis - basis_high, basis_high).astype(BF16)
        radial = jnp.dot(mixed, w_basis, preferred_element_type=F32)
        half = radial.reshape(per_atom, CHUNK_ATOMS, LANES) + own(0) + per_edge(0)
        edge_in = (half + half * jnp.tanh(half)).astype(BF16).reshape(chunk, LANES)
        half = jnp.dot(edge_in, w_expand_ref[...], preferred_element_type=F32)
        latent = (half + half * jnp.tanh(half)).astype(BF16)
        out = jnp.dot(latent, w_contract_ref[...], preferred_element_type=F32)
        envelope = jnp.maximum(0.0, 1.0 - d2 * (1.0 / CUTOFF_SQ))
        envelope = envelope * envelope
        weight = out.reshape(per_atom, CHUNK_ATOMS, LANES) * envelope * per_edge(1)
        sums_ref[0, pl.ds(first, CHUNK_ATOMS), :] = jnp.sum(weight, axis=0)
        for a in range(3):
            sums_ref[1 + a, pl.ds(first, CHUNK_ATOMS), :] = jnp.sum(disp[a] * weight, axis=0)

    gather(0, near_a)

    def pair(step, carry):
        gather(2 * step + 1, near_b)
        work(2 * step, near_a)
        gather(jnp.minimum(2 * step + 2, chunks - 1), near_a)
        work(2 * step + 1, near_b)
        return carry

    lax.fori_loop(0, chunks // 2, pair, 0)

    scale = 1.0 / math.sqrt(per_atom)
    vector = [sums_ref[1 + a] * scale for a in range(3)]
    square = vector[0] * vector[0] + vector[1] * vector[1] + vector[2] * vector[2]
    invariant = (sums_ref[0] * scale + square * (1.0 / 3.0)).astype(BF16)
    gate = jnp.dot(invariant, w_final_ref[...], preferred_element_type=F32)
    gate = gate * (0.5 + 0.5 * jnp.tanh(0.5 * gate)) * (1.0 / math.sqrt(channels))
    ones = jnp.ones((8, channels), F32)
    short = [contract_last(ones, vector[a] * gate, HIGHEST)[:1] for a in range(3)]
    out_ref[...] = jnp.concatenate(short, axis=0)


def edge_forces(lists, feat, pos, mid, up, down, w_self, w_pair, w_radial, w_expand, w_contract, w_final):
    atoms, channels = feat.shape
    per_atom = lists.shape[1]
    ghosts = mid.shape[1] - EXTRA
    chunk = CHUNK_ATOMS * per_atom
    vmem = pl.BlockSpec(memory_space=pltpu.VMEM)
    near = pltpu.VMEM((chunk * 8, LANES), F32)
    edges = atoms * per_atom
    latent = w_expand.shape[1]
    return pl.pallas_call(
        edge_kernel,
        in_specs=[pl.BlockSpec(memory_space=pltpu.SMEM)] + [vmem] * 11,
        out_specs=vmem,
        out_shape=jax.ShapeDtypeStruct((3, atoms), F32),
        scratch_shapes=[
            pltpu.VMEM(((atoms + 9 * ghosts) * 8, LANES), F32),
            near,
            near,
            pltpu.VMEM((4, atoms, LANES), F32),
            pltpu.VMEM((4, atoms, LANES), F32),
        ],
        compiler_params=pltpu.CompilerParams(vmem_limit_bytes=56 << 20),
        cost_estimate=pl.CostEstimate(
            flops=4 * edges * channels * latent,
            bytes_accessed=4_000_000,
            transcendentals=edges * latent,
        ),
        name="edge_forces",
    )(
        (lists * 8).reshape(-1), feat, pos, mid, up, down, w_self, w_pair, w_radial,
        w_expand * 0.5, w_contract, w_final,
    )


def ring(array, axis, step):
    size = lax.axis_size(axis)
    return lax.ppermute(array, axis, [(i, (i + step) % size) for i in range(size)])


def shards(
    features, positions, atom_count, ghost_index, neighbour_list, cell_index, w_self, w_pair,
    w_radial, w_expand, w_contract, w_final, w_charge,
):
    feat = features[0, 0]
    pos = positions[0, 0]
    cycle_x, cycle_y = (lax.axis_size("dx"), lax.axis_size("dy"))
    exported, charge_cell = prepare(
        atom_count, feat, pos, ghost_index[0, 0], cell_index[0, 0], w_charge
    )
    gathered = lax.all_gather(charge_cell, ("dx", "dy"))
    mid = jnp.stack([ring(exported, "dx", 1), exported, ring(exported, "dx", -1)])
    up = ring(mid, "dy", 1)
    down = ring(mid, "dy", -1)
    place = lax.axis_index("dx") * cycle_y + lax.axis_index("dy")
    partial = grid_fields(place[None].astype(jnp.int32), gathered, cycle_x, cycle_y)
    received = lax.all_to_all(partial, ("dx", "dy"), split_axis=0, concat_axis=0, tiled=True)
    short = edge_forces(
        neighbour_list[0, 0], feat, pos, mid, up, down, w_self, w_pair, w_radial, w_expand,
        w_contract, w_final,
    )
    field = jnp.sum(received, axis=0)
    total = short + charge_cell[:1] * field
    live = lax.broadcasted_iota(jnp.int32, (1, feat.shape[0]), 1) < atom_count[0, 0]
    return jnp.where(live, total, jnp.zeros_like(total))[None, None]


def solution(mesh):
    placed = (
        P("dx", "dy", None, None),
        P("dx", "dy", None, None),
        P("dx", "dy"),
        P("dx", "dy", None),
        P("dx", "dy", None, None),
        P("dx", "dy", None),
    ) + (P(),) * 7
    return jax.shard_map(
        shards, mesh=mesh, in_specs=placed, out_specs=P("dx", "dy", None, None), check_vma=False
    )
```

time: 438 us -> 162 us (0.37); the launches traced: 432 us -> 162 us
  local copies, waits for them, and re-layouts: 190 us -> 2.93 us
  matrix products: 133 us -> 0 us
  blocking collectives: 0 us -> 73.4 us
  Pallas kernels: 0 us -> 65.1 us
  other arithmetic: 52.1 us -> 0.82 us
  starting transfers between devices: 32.3 us -> 9.92 us
  waiting for transfers between devices: 22.5 us -> 8.68 us
    dot_general x49 -> x0, matrix products: 133 us -> none  [the longest x28 79.2 us: apply_table(): return jnp.einsum(formula, values, table, precision=lax.Precision.HIGHEST)]
    gather x15 -> x0, local copies, waits for them, and re-layouts: 99.9 us -> none  [the longest x6 44.9 us: one_block(): gathered = jnp.take(projected, flat_list, axis=0)]
    all_gather x0 -> x1, blocking collectives: none -> 73.4 us  [shards(): gathered = lax.all_gather(charge_cell, ('dx', 'dy'))]
    pallas_call x0 -> x3, Pallas kernels: none -> 65.1 us  [the longest x1 34.6 us: edge_forces(): pl.pallas_call(edge_kernel, in_specs=[pl.BlockSpec(memory_space=pltpu.SME...]
    reduce_sum x24 -> x1, other arithmetic: 21.3 us -> 0.05 us  [shards(): field = jnp.sum(received, axis=0)]
    another operation x9 -> x0, local copies, waits for them, and re-layouts: 20.5 us -> none  [the longest x3 9.55 us: shards(): stacked = jnp.stack([real_z, imag_z])]
    mul x1 -> x2, local copies, waits for them, and re-layouts: 18.3 us -> 0.84 us  [edge_forces(): lists * 8]
    unnamed x45 -> x16, local copies, waits for them, and re-layouts: 18.5 us -> 1.47 us
  transfers between devices with their start and end apart: 12 -> 5, of which waited for: 5 -> 2; matrix products, arithmetic and copies ran while one was open for 65% -> 1% of each run, Pallas kernels for 0% -> 39%
where the time goes in v1:
time: 162 us
  blocking collectives  73.4 us (45%)
  Pallas kernels  65.1 us (40%)
  starting transfers between devices  9.92 us (6%)
  waiting for transfers between devices  8.68 us (5%)
  local copies, waits for them, and re-layouts  2.93 us (2%)
    all_gather x1, blocking collectives, shards(): gathered = lax.all_gather(charge_cell, ('dx', 'dy'))  73.4 us
    pallas_call x1, Pallas kernels, edge_forces(): pl.pallas_call(edge_kernel, in_specs=[pl.BlockSpec(memory_space=pltpu.SME...  34.6 us
    pallas_call x1, Pallas kernels, grid_fields(): pl.pallas_call(functools.partial(grid_kernel, cycle_x, cycle_y), in_specs...  28.7 us
    ppermute x4, waiting for transfers between devices, ring(): lax.ppermute(array, axis, [(i, (i + step) % size) for i in range(size)])  8.67 us
    ppermute x4, starting transfers between devices, ring(): lax.ppermute(array, axis, [(i, (i + step) % size) for i in range(size)])  7.21 us
  transfers between devices with their start and end apart: 5, of which 2 were waited for; matrix products, arithmetic and copies ran while one was open for 1% of the time, Pallas kernels for 39%

profile of v1, /device:TPU:0, one launch (start us, length us, event | category | flops | bytes accessed | tf_op | source)
XLA Modules:
  0.0 161.6 jit_solution(30743285715834969)
XLA Ops:
  0.7 1.8 %prepare.1 = (bf16[272,128]{1,0:T(8,128)(2,1)}, f32[2,384]{1,0:T(2,128)}) custom-call(s32[1,1]{1,0:T(1,128)} %copy.24.count_ref, bf16[384,128]{1,0:T(8,128)(2,1)} %bitcast.16, bf16[3,384]{1,0:T(4,128)(2,1)} %bitcast.22, s32[1,256]{1,0:T(1,128)} %bitcast.25, s32[1,384]{1,0:T(1,128)} %bitcast.24, bf16[1,128]{1,0:T(2,128)(2,1)} %bitcast.26), custom_call_target="tpu_custom_call" | custom-call | tf_op jit(solution)/shard_map/prepare/pallas_call | solution.py:61
  2.5 0.0 copy-start.4
  2.5 0.5 collective-permute-start
  2.9 2.0 %collective-permute-start.1 = (bf16[272,128]{1,0:T(8,128)(2,1)}, bf16[272,128]{1,0:T(8,128)(2,1)S(1)}, u32[]{:S(2)}, u32[]{:S(2)}) collective-permute-start(bf16[272,128]{1,0:T(8,128)(2,1)} %get-tuple-element.7), channel_id=1, source_target_pairs={{0,24},{8,0},{16,8},{24,16},{1,25},{9,1},{17,9},{25,17},{2,26},{10... | collective-permute-start | bytes 208904 | tf_op jit(solution)/shard_map/ppermute | solution.py:440
  4.9 0.0 copy-done.4
  4.9 73.4 %all-gather.1.qc_ref = f32[32,2,384]{2,1,0:T(2,128)} all-gather(f32[1,2,384]{2,1,0:T(2,128)S(1)} %bitcast.21), channel_id=2, replica_groups=mesh['dx'=4,'dy'=8] {'dx','dy'}, dimensions={0}, use_global_device_ids=true | all-gather | bytes 101376 | tf_op jit(solution)/shard_map/all_gather | solution.py:453
  78.3 28.7 %grid_fields.1 = f32[32,3,384]{2,1,0:T(4,128)} custom-call(s32[1]{0:T(128)} %bitcast.9.place_ref, f32[32,2,384]{2,1,0:T(2,128)} %all-gather.1.qc_ref, bf16[256,512]{1,0:T(8,128)(2,1)} %constant.26.clone.fy_ref, bf16[256,512]{1,0:T(8,128)(2,1)} %constant.27.clone.fx_ref, bf16[512,512]{1,0:T(8,128)(2,1)} %constant.28.clone.ix_ref, ...), custom_call_target="tpu_custom_call" | custom-call | flops 8000000000 | bytes 4000000 | tf_op jit(solution)/shard_map/grid_fields/pallas_call | solution.py:271
  107.0 0.0 copy-start.3
  107.0 2.7 %all-to-all-start = ((f32[32,3,384]{2,1,0:T(4,128)}), f32[32,3,384]{2,1,0:T(4,128)S(1)}, u32[]{:S(2)}, u32[]{:S(2)}) async-start(f32[32,3,384]{2,1,0:T(4,128)} %grid_fields.1), calls=%async_computation | async-start | bytes 393216 | tf_op jit(solution)/shard_map/all_to_all | solution.py:459
  109.8 0.0 copy-done.3
  109.8 0.1 copy.22
  109.9 0.0 copy-start.2
  109.9 0.7 mul.31.list_ref
  110.6 0.0 copy-start
  110.6 0.0 collective-permute-done
  110.6 0.0 collective-permute-done.1
  110.7 0.1 copy-done.2
  110.8 0.0 copy-start.1
  110.8 1.7 %collective-permute-start.2 = (bf16[3,272,128]{2,1,0:T(8,128)(2,1)S(1)}, bf16[3,272,128]{2,1,0:T(8,128)(2,1)S(1)}, u32[]{:S(2)}, u32[]{:S(2)}) collective-permute-start(bf16[3,272,128]{2,1,0:T(8,128)(2,1)S(1)} %pad_maximum_fusion.mid_ref), channel_id=1, source_target_pairs={{0,1},{1,2},{2,3},{3,4},{4,5},{5,6},{6,7},{7,0},{8,9},{9,10},{10,1... | collective-permute-start | bytes 626696 | tf_op jit(solution)/shard_map/ppermute | solution.py:440
  112.5 3.1 %collective-permute-start.3 = (bf16[3,272,128]{2,1,0:T(8,128)(2,1)S(1)}, bf16[3,272,128]{2,1,0:T(8,128)(2,1)S(1)}, u32[]{:S(2)}, u32[]{:S(2)}) collective-permute-start(bf16[3,272,128]{2,1,0:T(8,128)(2,1)S(1)} %pad_maximum_fusion.mid_ref), channel_id=1, source_target_pairs={{0,7},{1,0},{2,1},{3,2},{4,3},{5,4},{6,5},{7,6},{8,15},{9,8},{10,9... | collective-permute-start | bytes 626696 | tf_op jit(solution)/shard_map/ppermute | solution.py:440
  115.6 0.0 copy-done
  115.6 0.7 broadcast_multiply_fusion.w_expand_ref
  116.3 0.0 copy-done.1
  116.3 6.7 %collective-permute-done.2.up_ref = bf16[3,272,128]{2,1,0:T(8,128)(2,1)S(1)} collective-permute-done((bf16[3,272,128]{2,1,0:T(8,128)(2,1)S(1)}, bf16[3,272,128]{2,1,0:T(8,128)(2,1)S(1)}, u32[]{:S(2)}, u32[]{:S(2)}) %collective-permute-start.2) | collective-permute-done | bytes 208928 | tf_op jit(solution)/shard_map/ppermute | solution.py:440
  123.1 0.0 copy-start.6
  123.1 1.9 %collective-permute-done.3.down_ref = bf16[3,272,128]{2,1,0:T(8,128)(2,1)S(1)} collective-permute-done((bf16[3,272,128]{2,1,0:T(8,128)(2,1)S(1)}, bf16[3,272,128]{2,1,0:T(8,128)(2,1)S(1)}, u32[]{:S(2)}, u32[]{:S(2)}) %collective-permute-start.3) | collective-permute-done | bytes 208928 | tf_op jit(solution)/shard_map/ppermute | solution.py:440
  125.0 0.0 copy-done.6
  125.0 0.0 copy-start.7
  125.0 0.7 copy-done.7
  125.7 34.6 %edge_forces.1 = f32[3,384]{1,0:T(4,128)} custom-call(s32[12288]{0:T(1024)} %mul.31.list_ref, bf16[384,128]{1,0:T(8,128)(2,1)} %bitcast.17, bf16[3,384]{1,0:T(4,128)(2,1)} %bitcast.23, bf16[3,272,128]{2,1,0:T(8,128)(2,1)} %copy-done.1, bf16[3,272,128]{2,1,0:T(8,128)(2,1)} %copy-done.6, bf16[3,272,128]{2,1,0:T(8,128)(2,1)} %copy-done.7, ...), custom_call_target="tpu_custom_call" | custom-call | flops 6442450944 | bytes 4000000 | tf_op jit(solution)/shard_map/edge_forces/pallas_call | solution.py:413
  160.3 0.0 copy-start.5
  160.3 0.0 all-to-all-done
  160.3 0.1 reduce_sum.9
  160.4 0.6 copy-done.5
  161.0 0.6 copy.23
  (5 shorter events, 0.1 us)
Async XLA Ops:
  2.5 2.4 %copy-start.4 = (f32[2,384]{1,0:T(2,128)S(1)}, f32[2,384]{1,0:T(2,128)}, u32[]{:S(2)}) copy-start(f32[2,384]{1,0:T(2,128)} %get-tuple-element.8) | copy-start | bytes 9220
  2.5 108.2 %collective-permute-start = (bf16[272,128]{1,0:T(8,128)(2,1)}, bf16[272,128]{1,0:T(8,128)(2,1)S(1)}, u32[]{:S(2)}, u32[]{:S(2)}) collective-permute-start(bf16[272,128]{1,0:T(8,128)(2,1)} %get-tuple-element.7), channel_id=1, source_target_pairs={{0,8},{8,16},{16,24},{24,0},{1,9},{9,17},{17,25},{25,1},{2,10},{10... | collective-permute-start | bytes 208904 | tf_op jit(solution)/shard_map/ppermute | solution.py:440
  2.9 107.7 %collective-permute-start.1 = (bf16[272,128]{1,0:T(8,128)(2,1)}, bf16[272,128]{1,0:T(8,128)(2,1)S(1)}, u32[]{:S(2)}, u32[]{:S(2)}) collective-permute-start(bf16[272,128]{1,0:T(8,128)(2,1)} %get-tuple-element.7), channel_id=1, source_target_pairs={{0,24},{8,0},{16,8},{24,16},{1,25},{9,1},{17,9},{25,17},{2,26},{10... | collective-permute-start | bytes 208904 | tf_op jit(solution)/shard_map/ppermute | solution.py:440
  107.0 2.7 %copy-start.3 = (s32[1,1,384,32]{2,3,1,0:T(8,128)S(1)}, s32[1,1,384,32]{2,3,1,0:T(8,128)}, u32[]{:S(2)}) copy-start(s32[1,1,384,32]{2,3,1,0:T(8,128)} %param.22) | copy-start | bytes 147460
  107.0 53.3 %all-to-all-start = ((f32[32,3,384]{2,1,0:T(4,128)}), f32[32,3,384]{2,1,0:T(4,128)S(1)}, u32[]{:S(2)}, u32[]{:S(2)}) async-start(f32[32,3,384]{2,1,0:T(4,128)} %grid_fields.1), calls=%async_computation | async-start | bytes 393216 | tf_op jit(solution)/shard_map/all_to_all | solution.py:459
  109.9 0.9 copy-start.2
  110.6 5.0 %copy-start = (bf16[128,1024]{1,0:T(8,128)(2,1)S(1)}, bf16[128,1024]{1,0:T(8,128)(2,1)}, u32[]{:S(2)}) copy-start(bf16[128,1024]{1,0:T(8,128)(2,1)} %param.27) | copy-start | bytes 786436
  110.8 5.5 %copy-start.1 = (bf16[3,272,128]{2,1,0:T(8,128)(2,1)}, bf16[3,272,128]{2,1,0:T(8,128)(2,1)S(1)}, u32[]{:S(2)}) copy-start(bf16[3,272,128]{2,1,0:T(8,128)(2,1)S(1)} %pad_maximum_fusion.mid_ref) | copy-start | bytes 626692
  110.8 12.2 %collective-permute-start.2 = (bf16[3,272,128]{2,1,0:T(8,128)(2,1)S(1)}, bf16[3,272,128]{2,1,0:T(8,128)(2,1)S(1)}, u32[]{:S(2)}, u32[]{:S(2)}) collective-permute-start(bf16[3,272,128]{2,1,0:T(8,128)(2,1)S(1)} %pad_maximum_fusion.mid_ref), channel_id=1, source_target_pairs={{0,1},{1,2},{2,3},{3,4},{4,5},{5,6},{6,7},{7,0},{8,9},{9,10},{10,1... | collective-permute-start | bytes 626696 | tf_op jit(solution)/shard_map/ppermute | solution.py:440
  112.5 12.5 %collective-permute-start.3 = (bf16[3,272,128]{2,1,0:T(8,128)(2,1)S(1)}, bf16[3,272,128]{2,1,0:T(8,128)(2,1)S(1)}, u32[]{:S(2)}, u32[]{:S(2)}) collective-permute-start(bf16[3,272,128]{2,1,0:T(8,128)(2,1)S(1)} %pad_maximum_fusion.mid_ref), channel_id=1, source_target_pairs={{0,7},{1,0},{2,1},{3,2},{4,3},{5,4},{6,5},{7,6},{8,15},{9,8},{10,9... | collective-permute-start | bytes 626696 | tf_op jit(solution)/shard_map/ppermute | solution.py:440
  123.1 1.9 %copy-start.6 = (bf16[3,272,128]{2,1,0:T(8,128)(2,1)}, bf16[3,272,128]{2,1,0:T(8,128)(2,1)S(1)}, u32[]{:S(2)}) copy-start(bf16[3,272,128]{2,1,0:T(8,128)(2,1)S(1)} %collective-permute-done.2.up_ref) | copy-start | bytes 626692
  125.0 0.7 copy-start.7
  160.3 0.7 copy-start.5

commit v2 on v1

--- a/solution.py
+++ b/solution.py
@@ -20,6 +20,7 @@
 EXTRA = 16
 ROWS = 32
 CHUNK_ATOMS = 16
+PIECES = 4
 HIGHEST = lax.Precision.HIGHEST
 F32 = jnp.float32
 BF16 = jnp.bfloat16
@@ -84,11 +85,8 @@
     return (basis, (weight * basis).T, (weight * slope).T)
 
 
-def split_table(table, copies):
-    whole = np.kron(np.eye(copies), table).astype(np.float32)
-    high = whole.astype(BF16)
-    low = (whole - high.astype(np.float32)).astype(BF16)
-    return np.concatenate([high, low], axis=1)
+def block_table(table, copies):
+    return np.kron(np.eye(copies), table).astype(np.float32)
 
 
 def sine_half(t):
@@ -103,9 +101,14 @@
 
 
 def grid_kernel(
-    cycle_x, cycle_y, place_ref, qc_ref, fy_ref, fx_ref, ix_ref, iy_ref, dy_ref, out_ref,
-    buf_a, buf_b, buf_c, buf_d, buf_e, trig_ref,
+    cycle_x, cycle_y, place_ref, qc_ref, fy_table, fx_table, ix_table, iy_table, dy_table, out_ref,
+    buf_a, buf_b, buf_c, buf_d, buf_e, trig_ref, fy_ref, fx_ref, ix_ref, iy_ref, dy_ref,
 ):
+    tables = (fy_table, fx_table, ix_table, iy_table, dy_table)
+    for whole, halves in zip(tables, (fy_ref, fx_ref, ix_ref, iy_ref, dy_ref)):
+        high = whole[...].astype(BF16)
+        halves[:, : whole.shape[1]] = high
+        halves[:, whole.shape[1] :] = (whole[...] - high.astype(F32)).astype(BF16)
     mesh_x, mesh_y, mesh_z = (GRID_X * cycle_x, GRID_Y * cycle_y, GRID_Z)
     devices = cycle_x * cycle_y
     modes = mesh_z // 2 // devices
@@ -140,13 +143,12 @@
         high = charged.astype(BF16)
         low = (charged - high.astype(F32)).astype(BF16)
         pick = jnp.where(match, 1.0, 0.0).astype(BF16)
-        copies = LANES // ROWS
-        total = contract_last(pick, jnp.concatenate([high] * copies, axis=0))
-        total += contract_last(pick, jnp.concatenate([low] * copies, axis=0))
-        buf_a[pl.ds(device * columns, columns), :] = total
+        total = contract_last(pick, jnp.concatenate([high, low] * (LANES // ROWS // 2), axis=0))
+        total = total + pltpu.roll(total, ROWS, 1)
+        buf_a[pl.ds(pl.multiple_of(device * columns, 8), columns), :] = total
         return carry
 
-    lax.fori_loop(0, devices, spread, 0)
+    lax.fori_loop(0, devices, spread, 0, unroll=4)
 
     lane = lax.broadcasted_iota(jnp.int32, (1, LANES), 1)
     low_half = lane >= LANES // 2
@@ -170,7 +172,7 @@
         buf_b[pl.ds(start, size), :] = apply(fy_ref, jnp.concatenate(parts, axis=0))
         return carry
 
-    lax.fori_loop(0, mesh_x // group_y, forward_y, 0)
+    lax.fori_loop(0, mesh_x // group_y, forward_y, 0, unroll=2)
 
     size_x = group_x * mesh_x
     lane_coef = lane % coefs
@@ -204,7 +206,7 @@
         buf_c[pl.ds(start, size_x), :] = both[size_x:]
         return carry
 
-    lax.fori_loop(0, mesh_y // group_x, middle, 0)
+    lax.fori_loop(0, mesh_y // group_x, middle, 0, unroll=2)
 
     def backward_y(step, carry):
         plain, sloped = ([], [])
@@ -221,7 +223,7 @@
         buf_e[pl.ds(start, size), :] = pltpu.roll(potential, modes, 1) * slope_z
         return carry
 
-    lax.fori_loop(0, mesh_x // group_y, backward_y, 0)
+    lax.fori_loop(0, mesh_x // group_y, backward_y, 0, unroll=2)
 
     use_low = (lane // ROWS) == 1
     use_none = (lane % ROWS) >= coefs
@@ -249,7 +251,7 @@
         out_ref[device] = jnp.concatenate(picked, axis=0)
         return carry
 
-    lax.fori_loop(0, devices, sample, 0)
+    lax.fori_loop(0, devices, sample, 0, unroll=4)
 
 
 def grid_fields(place, gathered, cycle_x, cycle_y):
@@ -260,11 +262,11 @@
     ax, bx, cx = real_tables(mesh_x)
     ay, by, cy = real_tables(mesh_y)
     tables = [
-        split_table(ay, group_y),
-        split_table(ax, group_x),
-        np.concatenate([split_table(bx, group_x), split_table(cx, group_x)], axis=0),
-        split_table(by, group_y),
-        split_table(cy, group_y),
+        block_table(ay, group_y),
+        block_table(ax, group_x),
+        np.concatenate([block_table(bx, group_x), block_table(cx, group_x)], axis=0),
+        block_table(by, group_y),
+        block_table(cy, group_y),
     ]
     plane = pltpu.VMEM((mesh_x * mesh_y, LANES), F32)
     vmem = pl.BlockSpec(memory_space=pltpu.VMEM)
@@ -273,7 +275,9 @@
         in_specs=[pl.BlockSpec(memory_space=pltpu.SMEM)] + [vmem] * 6,
         out_specs=vmem,
         out_shape=jax.ShapeDtypeStruct((devices, 3, atoms), F32),
-        scratch_shapes=[plane] * 5 + [pltpu.VMEM((devices, 2 * ROWS, atoms), BF16)],
+        scratch_shapes=[plane] * 5
+        + [pltpu.VMEM((devices, 2 * ROWS, atoms), BF16)]
+        + [pltpu.VMEM((t.shape[0], 2 * t.shape[1]), BF16) for t in tables],
         compiler_params=pltpu.CompilerParams(vmem_limit_bytes=60 << 20),
         cost_estimate=pl.CostEstimate(
             flops=8_000_000_000, bytes_accessed=4_000_000, transcendentals=100_000
@@ -285,7 +289,7 @@
 def edge_kernel(
     list_ref, feat_ref, pos_ref, mid_ref, up_ref, down_ref, w_self_ref, w_pair_ref, w_radial_ref,
     w_expand_ref, w_contract_ref, w_final_ref, out_ref,
-    table, near_a, near_b, own_ref, sums_ref,
+    table, near_a, near_b, edge_a, edge_b, aux_a, aux_b, own_ref, sums_ref, w_half,
 ):
     atoms, channels = feat_ref.shape
     ghosts = mid_ref.shape[1] - EXTRA
@@ -344,48 +348,79 @@
     center = (lane % basis_count).astype(F32)
     use_low = (lane // basis_count) == 1
 
-    def gather(index, near):
-        for a in range(CHUNK_ATOMS):
-            for k in range(per_atom):
-                j = pl.multiple_of(list_ref[(index * CHUNK_ATOMS + a) * per_atom + k], 8)
+    piece = chunk // PIECES
+    slots = per_atom // PIECES
+    latent = w_expand_ref.shape[1]
+    width = latent // PIECES
+    w_half[...] = w_expand_ref[...] * 0.5
+
+    def gather(index, near, part):
+        for k in range(part * slots, (part + 1) * slots):
+            for a in range(CHUNK_ATOMS):
+                j = pl.multiple_of(list_ref[k * atoms + index * CHUNK_ATOMS + a], 8)
                 e = k * CHUNK_ATOMS + a
                 near[pl.ds(e * 8, 8), :] = table[pl.ds(j, 8), :]
 
-    def work(index, near):
+    def geometry(index, near, edge_in, aux, part):
         first = pl.multiple_of(index * CHUNK_ATOMS, 8)
+        rows = pl.ds(part * piece, piece)
 
         def per_edge(s):
-            return near[pl.ds(s, chunk, stride=8), :].reshape(per_atom, CHUNK_ATOMS, LANES)
+            start = part * piece * 8 + s
+            return near[pl.ds(start, piece, stride=8), :].reshape(slots, CHUNK_ATOMS, LANES)
 
         def own(s):
             return own_ref[s, pl.ds(first, CHUNK_ATOMS), :][None]
 
         disp = [per_edge(2 + a) - own(1 + a) for a in range(3)]
         d2 = disp[0] * disp[0] + disp[1] * disp[1] + disp[2] * disp[2]
-        t = (d2 * (1.0 / spacing)).reshape(chunk, LANES) - center
+        t = (d2 * (1.0 / spacing)).reshape(piece, LANES) - center
         basis = jnp.exp(-(t * t))
         basis_high = basis.astype(BF16).astype(F32)
         mixed = jnp.where(use_low, basis - basis_high, basis_high).astype(BF16)
         radial = jnp.dot(mixed, w_basis, preferred_element_type=F32)
-        half = radial.reshape(per_atom, CHUNK_ATOMS, LANES) + own(0) + per_edge(0)
-        edge_in = (half + half * jnp.tanh(half)).astype(BF16).reshape(chunk, LANES)
-        half = jnp.dot(edge_in, w_expand_ref[...], preferred_element_type=F32)
-        latent = (half + half * jnp.tanh(half)).astype(BF16)
-        out = jnp.dot(latent, w_contract_ref[...], preferred_element_type=F32)
+        half = radial.reshape(slots, CHUNK_ATOMS, LANES) + own(0) + per_edge(0)
+        edge_in[rows, :] = (half + half * jnp.tanh(half)).astype(BF16).reshape(piece, LANES)
         envelope = jnp.maximum(0.0, 1.0 - d2 * (1.0 / CUTOFF_SQ))
-        envelope = envelope * envelope
-        weight = out.reshape(per_atom, CHUNK_ATOMS, LANES) * envelope * per_edge(1)
+        aux[0, rows, :] = (envelope * envelope * per_edge(1)).reshape(piece, LANES)
+        for a in range(3):
+            aux[1 + a, rows, :] = disp[a].reshape(piece, LANES)
+
+    def network(edge_in, part):
+        cols = pl.ds(part * width, width)
+        half = jnp.dot(edge_in[...], w_half[:, cols], preferred_element_type=F32)
+        hidden = (half + half * jnp.tanh(half)).astype(BF16)
+        return jnp.dot(hidden, w_contract_ref[cols, :], preferred_element_type=F32)
+
+    def collect(index, mixed, aux):
+        first = pl.multiple_of(index * CHUNK_ATOMS, 8)
+        shape = (per_atom, CHUNK_ATOMS, LANES)
+        weight = (mixed * aux[0]).reshape(shape)
         sums_ref[0, pl.ds(first, CHUNK_ATOMS), :] = jnp.sum(weight, axis=0)
         for a in range(3):
-            sums_ref[1 + a, pl.ds(first, CHUNK_ATOMS), :] = jnp.sum(disp[a] * weight, axis=0)
-
-    gather(0, near_a)
+            moment = jnp.sum(aux[1 + a].reshape(shape) * weight, axis=0)
+            sums_ref[1 + a, pl.ds(first, CHUNK_ATOMS), :] = moment
+
+    def stage(index, near, near_next, edge_in, edge_next, aux, aux_next):
+        after = jnp.minimum(index + 1, chunks - 1)
+        later = jnp.minimum(index + 2, chunks - 1)
+        mixed = None
+        for part in range(PIECES):
+            gather(later, near, part)
+            geometry(after, near_next, edge_next, aux_next, part)
+            term = network(edge_in, part)
+            mixed = term if mixed is None else mixed + term
+        collect(index, mixed, aux)
+
+    for part in range(PIECES):
+        gather(0, near_a, part)
+    for part in range(PIECES):
+        gather(1, near_b, part)
+        geometry(0, near_a, edge_a, aux_a, part)
 
     def pair(step, carry):
-        gather(2 * step + 1, near_b)
-        work(2 * step, near_a)
-        gather(jnp.minimum(2 * step + 2, chunks - 1), near_a)
-        work(2 * step + 1, near_b)
+        stage(2 * step, near_a, near_b, edge_a, edge_b, aux_a, aux_b)
+        stage(2 * step + 1, near_b, near_a, edge_b, edge_a, aux_b, aux_a)
         return carry
 
     lax.fori_loop(0, chunks // 2, pair, 0)
@@ -401,13 +436,14 @@
     out_ref[...] = jnp.concatenate(short, axis=0)
 
 
-def edge_forces(lists, feat, pos, mid, up, down, w_self, w_pair, w_radial, w_expand, w_contract, w_final):
+def edge_forces(per_atom, lists, feat, pos, mid, up, down, w_self, w_pair, w_radial, w_expand, w_contract, w_final):
     atoms, channels = feat.shape
-    per_atom = lists.shape[1]
     ghosts = mid.shape[1] - EXTRA
     chunk = CHUNK_ATOMS * per_atom
     vmem = pl.BlockSpec(memory_space=pltpu.VMEM)
     near = pltpu.VMEM((chunk * 8, LANES), F32)
+    edge = pltpu.VMEM((chunk, LANES), BF16)
+    aux = pltpu.VMEM((4, chunk, LANES), F32)
     edges = atoms * per_atom
     latent = w_expand.shape[1]
     return pl.pallas_call(
@@ -419,8 +455,13 @@
             pltpu.VMEM(((atoms + 9 * ghosts) * 8, LANES), F32),
             near,
             near,
+            edge,
+            edge,
+            aux,
+            aux,
             pltpu.VMEM((4, atoms, LANES), F32),
             pltpu.VMEM((4, atoms, LANES), F32),
+            pltpu.VMEM(w_expand.shape, BF16),
         ],
         compiler_params=pltpu.CompilerParams(vmem_limit_bytes=56 << 20),
         cost_estimate=pl.CostEstimate(
@@ -430,8 +471,8 @@
         ),
         name="edge_forces",
     )(
-        (lists * 8).reshape(-1), feat, pos, mid, up, down, w_self, w_pair, w_radial,
-        w_expand * 0.5, w_contract, w_final,
+        lists, feat, pos, mid, up, down, w_self, w_pair, w_radial,
+        w_expand, w_contract, w_final,
     )
 
 
@@ -450,15 +491,18 @@
     exported, charge_cell = prepare(
         atom_count, feat, pos, ghost_index[0, 0], cell_index[0, 0], w_charge
     )
-    gathered = lax.all_gather(charge_cell, ("dx", "dy"))
+    spread = jnp.broadcast_to(charge_cell, (cycle_x * cycle_y,) + charge_cell.shape)
+    gathered = lax.all_to_all(spread, ("dx", "dy"), split_axis=0, concat_axis=0, tiled=True)
     mid = jnp.stack([ring(exported, "dx", 1), exported, ring(exported, "dx", -1)])
+    lists = (neighbour_list[0, 0] * 8).T.reshape(-1)
+    gathered, mid, lists = lax.optimization_barrier((gathered, mid, lists))
     up = ring(mid, "dy", 1)
     down = ring(mid, "dy", -1)
     place = lax.axis_index("dx") * cycle_y + lax.axis_index("dy")
     partial = grid_fields(place[None].astype(jnp.int32), gathered, cycle_x, cycle_y)
     received = lax.all_to_all(partial, ("dx", "dy"), split_axis=0, concat_axis=0, tiled=True)
     short = edge_forces(
-        neighbour_list[0, 0], feat, pos, mid, up, down, w_self, w_pair, w_radial, w_expand,
+        neighbour_list.shape[3], lists, feat, pos, mid, up, down, w_self, w_pair, w_radial, w_expand,
         w_contract, w_final,
     )
     field = jnp.sum(received, axis=0)

time: 162 us -> 81.3 us (0.50)
  blocking collectives: 73.4 us -> 0 us
  Pallas kernels: 65.1 us -> 54.1 us
  starting transfers between devices: 9.92 us -> 15.1 us
  waiting for transfers between devices: 8.68 us -> 6.58 us
    all_gather x1 -> x0, blocking collectives: 73.4 us -> none  [shards(): gathered = lax.all_gather(charge_cell, ('dx', 'dy'))]
    pallas_call x1, Pallas kernels: 28.7 us -> 17.4 us  [grid_fields(): pl.pallas_call(functools.partial(grid_kernel, cycle_x, cycle_y), in_specs...]
    ppermute x4, waiting for transfers between devices: 8.67 us -> 0.01 us  [ring(): lax.ppermute(array, axis, [(i, (i + step) % size) for i in range(size)])]
    all_to_all x0 -> x1, waiting for transfers between devices: none -> 6.57 us  [shards(): lax.all_to_all(spread, ('dx', 'dy'), split_axis=0, concat_axis=0, tiled=T...]
    all_to_all x0 -> x1, starting transfers between devices: none -> 6.1 us  [shards(): lax.all_to_all(spread, ('dx', 'dy'), split_axis=0, concat_axis=0, tiled=T...]
    ppermute x4, starting transfers between devices: 7.21 us -> 4.41 us  [ring(): lax.ppermute(array, axis, [(i, (i + step) % size) for i in range(size)])]
    all_to_all x1, starting transfers between devices: 2.71 us -> 4.6 us  [shards(): lax.all_to_all(partial, ('dx', 'dy'), split_axis=0, concat_axis=0, tiled=...]
  transfers between devices with their start and end apart: 5 -> 6, of which waited for: 2 -> 1; matrix products, arithmetic and copies ran while one was open for 1% -> 2% of each run, Pallas kernels for 39% -> 65%
where the time goes in v2:
time: 81.3 us; the launch traced here: 80.8 us
  Pallas kernels  54.1 us (67%)
  starting transfers between devices  15.1 us (19%)
  waiting for transfers between devices  6.58 us (8%)
  local copies, waits for them, and re-layouts  4.14 us (5%)
    pallas_call x1, Pallas kernels, edge_forces(): pl.pallas_call(edge_kernel, in_specs=[pl.BlockSpec(memory_space=pltpu.SME...  34.9 us
    pallas_call x1, Pallas kernels, grid_fields(): pl.pallas_call(functools.partial(grid_kernel, cycle_x, cycle_y), in_specs...  17.4 us
    all_to_all x1, waiting for transfers between devices, shards(): lax.all_to_all(spread, ('dx', 'dy'), split_axis=0, concat_axis=0, tiled=T...  6.57 us
    all_to_all x1, starting transfers between devices, shards(): lax.all_to_all(spread, ('dx', 'dy'), split_axis=0, concat_axis=0, tiled=T...  6.1 us
    all_to_all x1, starting transfers between devices, shards(): lax.all_to_all(partial, ('dx', 'dy'), split_axis=0, concat_axis=0, tiled=...  4.6 us
    ppermute x4, starting transfers between devices, ring(): lax.ppermute(array, axis, [(i, (i + step) % size) for i in range(size)])  4.41 us
    unnamed x16, local copies, waits for them, and re-layouts  2.25 us
    pallas_call x1, Pallas kernels, prepare(): pl.pallas_call(prepare_kernel, in_specs=[pl.BlockSpec(memory_space=pltpu....  1.84 us
  transfers between devices with their start and end apart: 6, of which 1 were waited for; matrix products, arithmetic and copies ran while one was open for 2% of the time, Pallas kernels for 65%

profile of v2, /device:TPU:0, one launch (start us, length us, event | category | flops | bytes accessed | tf_op | source)
XLA Modules:
  0.0 80.8 jit_solution(14038250183490232474)
XLA Ops:
  0.7 1.8 %prepare.1 = (bf16[272,128]{1,0:T(8,128)(2,1)}, f32[2,384]{1,0:T(2,128)}) custom-call(s32[1,1]{1,0:T(1,128)} %copy.20.count_ref, bf16[384,128]{1,0:T(8,128)(2,1)} %bitcast.17, bf16[3,384]{1,0:T(4,128)(2,1)} %bitcast.22, s32[1,256]{1,0:T(1,128)} %bitcast.25, s32[1,384]{1,0:T(1,128)} %bitcast.24, bf16[1,128]{1,0:T(2,128)(2,1)} %bitcast.26), custom_call_target="tpu_custom_call" | custom-call | tf_op jit(solution)/shard_map/prepare/pallas_call | solution.py:62
  2.5 0.0 copy-start.4
  2.5 2.4 %collective-permute-start.1 = (bf16[272,128]{1,0:T(8,128)(2,1)}, bf16[272,128]{1,0:T(8,128)(2,1)S(1)}, u32[]{:S(2)}, u32[]{:S(2)}) collective-permute-start(bf16[272,128]{1,0:T(8,128)(2,1)} %get-tuple-element.11), channel_id=1, source_target_pairs={{0,24},{8,0},{16,8},{24,16},{1,25},{9,1},{17,9},{25,17},{2,26},{10... | collective-permute-start | bytes 208904 | tf_op jit(solution)/shard_map/ppermute | solution.py:481
  4.9 0.0 collective-permute-start
  4.9 0.0 copy-done.4
  4.9 0.7 broadcast_in_dim.25
  5.5 0.0 copy-start.3
  5.5 6.1 %all-to-all-start = ((f32[32,2,384]{2,1,0:T(2,128)}), f32[32,2,384]{2,1,0:T(2,128)S(1)}, u32[]{:S(2)}, u32[]{:S(2)}) async-start(f32[32,2,384]{2,1,0:T(2,128)} %broadcast_in_dim.25), calls=%async_computation | async-start | bytes 196608 | tf_op jit(solution)/shard_map/all_to_all | solution.py:495
  11.7 0.0 copy-done.3
  11.7 0.0 copy-start.2
  11.7 0.6 reshape.10.list_ref
  12.3 0.0 collective-permute-done.1
  12.3 0.0 collective-permute-done
  12.3 0.3 copy-done.2
  12.6 0.0 copy-start
  12.6 6.6 %all-to-all-done.qc_ref = f32[32,2,384]{2,1,0:T(2,128)S(1)} async-done(((f32[32,2,384]{2,1,0:T(2,128)}), f32[32,2,384]{2,1,0:T(2,128)S(1)}, u32[]{:S(2)}, u32[]{:S(2)}) %all-to-all-start) | async-done | bytes 98336 | tf_op jit(solution)/shard_map/all_to_all | solution.py:495
  19.2 0.0 copy-start.1
  19.2 1.5 %collective-permute-start.3 = (bf16[3,272,128]{2,1,0:T(8,128)(2,1)S(1)}, bf16[3,272,128]{2,1,0:T(8,128)(2,1)S(1)}, u32[]{:S(2)}, u32[]{:S(2)}) collective-permute-start(bf16[3,272,128]{2,1,0:T(8,128)(2,1)S(1)} %pad_maximum_fusion.mid_ref), channel_id=1, source_target_pairs={{0,7},{1,0},{2,1},{3,2},{4,3},{5,4},{6,5},{7,6},{8,15},{9,8},{10,9... | collective-permute-start | bytes 626696 | tf_op jit(solution)/shard_map/ppermute | solution.py:481
  20.8 0.5 collective-permute-start.2
  21.2 0.0 copy-done.1
  21.2 17.4 %grid_fields.1 = f32[32,3,384]{2,1,0:T(4,128)} custom-call(s32[1]{0:T(128)} %bitcast.11.place_ref, f32[32,2,384]{2,1,0:T(2,128)} %copy-done.1, f32[256,256]{1,0:T(8,128)} %constant.24.clone.fy_table, f32[256,256]{1,0:T(8,128)} %constant.25.clone.fx_table, f32[512,256]{1,0:T(8,128)} %constant.26.clone.ix_table, f32[256,256]{1,0:T(8,128)} %constant.27.clone.iy_table, ...), custom_call_target="tpu_custom_call" | custom-call | flops 8000000000 | bytes 4000000 | tf_op jit(solution)/shard_map/grid_fields/pallas_call | solution.py:273
  38.7 0.0 copy-done
  38.7 4.6 %all-to-all-start.1 = ((f32[32,3,384]{2,1,0:T(4,128)}), f32[32,3,384]{2,1,0:T(4,128)S(1)}, u32[]{:S(2)}, u32[]{:S(2)}) async-start(f32[32,3,384]{2,1,0:T(4,128)} %grid_fields.1), calls=%async_computation.1 | async-start | bytes 393216 | tf_op jit(solution)/shard_map/all_to_all | solution.py:503
  43.3 0.0 collective-permute-done.3.down_ref
  43.3 0.0 copy-start.6
  43.3 0.0 collective-permute-done.2.up_ref
  43.3 0.6 copy-done.6
  43.9 0.0 copy-start.7
  43.9 0.7 copy-done.7
  44.6 34.9 %edge_forces.1 = f32[3,384]{1,0:T(4,128)} custom-call(s32[12288]{0:T(1024)} %reshape.10.list_ref, bf16[384,128]{1,0:T(8,128)(2,1)} %bitcast.18, bf16[3,384]{1,0:T(4,128)(2,1)} %bitcast.23, bf16[3,272,128]{2,1,0:T(8,128)(2,1)} %copy-done, bf16[3,272,128]{2,1,0:T(8,128)(2,1)} %copy-done.7, bf16[3,272,128]{2,1,0:T(8,128)(2,1)} %copy-done.6, ...), custom_call_target="tpu_custom_call" | custom-call | flops 6442450944 | bytes 4000000 | tf_op jit(solution)/shard_map/edge_forces/pallas_call | solution.py:449
  79.5 0.0 copy-start.5
  79.5 0.0 all-to-all-done.1
  79.5 0.1 reduce_sum.9
  79.6 0.6 copy-done.5
  80.2 0.6 copy.19
  (5 shorter events, 0.1 us)
Async XLA Ops:
  2.5 2.4 %copy-start.4 = (f32[2,384]{1,0:T(2,128)S(1)}, f32[2,384]{1,0:T(2,128)}, u32[]{:S(2)}) copy-start(f32[2,384]{1,0:T(2,128)} %get-tuple-element.10) | copy-start | bytes 9220
  2.5 9.8 %collective-permute-start.1 = (bf16[272,128]{1,0:T(8,128)(2,1)}, bf16[272,128]{1,0:T(8,128)(2,1)S(1)}, u32[]{:S(2)}, u32[]{:S(2)}) collective-permute-start(bf16[272,128]{1,0:T(8,128)(2,1)} %get-tuple-element.11), channel_id=1, source_target_pairs={{0,24},{8,0},{16,8},{24,16},{1,25},{9,1},{17,9},{25,17},{2,26},{10... | collective-permute-start | bytes 208904 | tf_op jit(solution)/shard_map/ppermute | solution.py:481
  4.9 7.5 %collective-permute-start = (bf16[272,128]{1,0:T(8,128)(2,1)}, bf16[272,128]{1,0:T(8,128)(2,1)S(1)}, u32[]{:S(2)}, u32[]{:S(2)}) collective-permute-start(bf16[272,128]{1,0:T(8,128)(2,1)} %get-tuple-element.11), channel_id=1, source_target_pairs={{0,8},{8,16},{16,24},{24,0},{1,9},{9,17},{17,25},{25,1},{2,10},{10... | collective-permute-start | bytes 208904 | tf_op jit(solution)/shard_map/ppermute | solution.py:481
  5.5 6.1 %copy-start.3 = (s32[1,1,384,32]{2,3,1,0:T(8,128)S(1)}, s32[1,1,384,32]{2,3,1,0:T(8,128)}, u32[]{:S(2)}) copy-start(s32[1,1,384,32]{2,3,1,0:T(8,128)} %param.22) | copy-start | bytes 147460
  5.5 13.7 %all-to-all-start = ((f32[32,2,384]{2,1,0:T(2,128)}), f32[32,2,384]{2,1,0:T(2,128)S(1)}, u32[]{:S(2)}, u32[]{:S(2)}) async-start(f32[32,2,384]{2,1,0:T(2,128)} %broadcast_in_dim.25), calls=%async_computation | async-start | bytes 196608 | tf_op jit(solution)/shard_map/all_to_all | solution.py:495
  11.7 0.9 %copy-start.2 = (bf16[272,128]{1,0:T(8,128)(2,1)S(1)}, bf16[272,128]{1,0:T(8,128)(2,1)}, u32[]{:S(2)}) copy-start(bf16[272,128]{1,0:T(8,128)(2,1)} %get-tuple-element.11) | copy-start | bytes 208900
  12.6 26.0 %copy-start = (bf16[3,272,128]{2,1,0:T(8,128)(2,1)}, bf16[3,272,128]{2,1,0:T(8,128)(2,1)S(1)}, u32[]{:S(2)}) copy-start(bf16[3,272,128]{2,1,0:T(8,128)(2,1)S(1)} %pad_maximum_fusion.mid_ref) | copy-start | bytes 626692
  19.2 2.0 %copy-start.1 = (f32[32,2,384]{2,1,0:T(2,128)}, f32[32,2,384]{2,1,0:T(2,128)S(1)}, u32[]{:S(2)}) copy-start(f32[32,2,384]{2,1,0:T(2,128)S(1)} %all-to-all-done.qc_ref) | copy-start | bytes 294916
  19.2 24.0 %collective-permute-start.3 = (bf16[3,272,128]{2,1,0:T(8,128)(2,1)S(1)}, bf16[3,272,128]{2,1,0:T(8,128)(2,1)S(1)}, u32[]{:S(2)}, u32[]{:S(2)}) collective-permute-start(bf16[3,272,128]{2,1,0:T(8,128)(2,1)S(1)} %pad_maximum_fusion.mid_ref), channel_id=1, source_target_pairs={{0,7},{1,0},{2,1},{3,2},{4,3},{5,4},{6,5},{7,6},{8,15},{9,8},{10,9... | collective-permute-start | bytes 626696 | tf_op jit(solution)/shard_map/ppermute | solution.py:481
  20.8 22.5 %collective-permute-start.2 = (bf16[3,272,128]{2,1,0:T(8,128)(2,1)S(1)}, bf16[3,272,128]{2,1,0:T(8,128)(2,1)S(1)}, u32[]{:S(2)}, u32[]{:S(2)}) collective-permute-start(bf16[3,272,128]{2,1,0:T(8,128)(2,1)S(1)} %pad_maximum_fusion.mid_ref), channel_id=1, source_target_pairs={{0,1},{1,2},{2,3},{3,4},{4,5},{5,6},{6,7},{7,0},{8,9},{9,10},{10,1... | collective-permute-start | bytes 626696 | tf_op jit(solution)/shard_map/ppermute | solution.py:481
  38.7 40.9 %all-to-all-start.1 = ((f32[32,3,384]{2,1,0:T(4,128)}), f32[32,3,384]{2,1,0:T(4,128)S(1)}, u32[]{:S(2)}, u32[]{:S(2)}) async-start(f32[32,3,384]{2,1,0:T(4,128)} %grid_fields.1), calls=%async_computation.1 | async-start | bytes 393216 | tf_op jit(solution)/shard_map/all_to_all | solution.py:503
  43.3 0.7 copy-start.6
  43.9 0.7 copy-start.7
  79.5 0.7 copy-start.5

commit v3 on v2

--- a/solution.py
+++ b/solution.py
@@ -287,104 +287,108 @@
 
 
 def edge_kernel(
-    list_ref, feat_ref, pos_ref, mid_ref, up_ref, down_ref, w_self_ref, w_pair_ref, w_radial_ref,
-    w_expand_ref, w_contract_ref, w_final_ref, out_ref,
-    table, near_a, near_b, edge_a, edge_b, aux_a, aux_b, own_ref, sums_ref, w_half,
+    list_ref, index_ref, feat_ref, pos_ref, mid_ref, up_ref, down_ref, w_self_ref, w_pair_ref,
+    w_radial_ref, w_expand_ref, w_contract_ref, w_final_ref, out_ref,
+    table, places, near_a, near_b, near_c, edge_a, edge_b, edge_c, marks, own_ref, sums_ref, w_half,
 ):
     atoms, channels = feat_ref.shape
     ghosts = mid_ref.shape[1] - EXTRA
-    per_atom = list_ref.shape[0] // atoms
+    slots_all = atoms + 9 * ghosts
+    per_atom = index_ref.shape[0]
     chunk = CHUNK_ATOMS * per_atom
     chunks = atoms // CHUNK_ATOMS
     basis_count = w_radial_ref.shape[0]
     spacing = CUTOFF_SQ / (basis_count - 1)
-
-    def column_of(index, size):
-        rows = lax.broadcasted_iota(jnp.int32, (8, 3 * LANES), 0)
-        cols = lax.broadcasted_iota(jnp.int32, (8, 3 * LANES), 1) // LANES
-        return jnp.where(rows == cols, 1.0, 0.0)
-
-    spread = column_of(0, 0)
+    latent = w_expand_ref.shape[1]
+    width = latent // PIECES
+    slots = per_atom // PIECES
+    w_half[...] = w_expand_ref[...] * 0.5
 
     def fill(start, rows, coords, shift):
+        count = rows.shape[0]
         projected = jnp.dot(rows, w_pair_ref[...], preferred_element_type=F32)
         projected = projected.astype(BF16).astype(F32)
-        count = rows.shape[0]
-        wide = contract_first(coords, spread, HIGHEST)
-        parts = [projected[:, :channels] * 0.5, projected[:, channels:]]
-        for a in range(3):
-            part = wide[:, a * LANES : (a + 1) * LANES]
-            parts.append(part + shift[a] if shift[a] != 0.0 else part)
-        for s, part in enumerate(parts):
-            table[pl.ds(start * 8 + s, count, stride=8), :] = part
-        return parts
+        table[pl.ds(start, count), :] = projected[:, :channels] * 0.5
+        table[pl.ds(slots_all + start, count), :] = projected[:, channels:]
+        row = lax.broadcasted_iota(jnp.int32, (8, LANES), 0)
+        offset = jnp.where(row == 0, shift[0], jnp.where(row == 1, shift[1], 0.0))
+        places[start // LANES] = coords + offset
 
     pos = jnp.concatenate([pos_ref[...].astype(F32), jnp.zeros((5, atoms), F32)], axis=0)
     for i in range(atoms // LANES):
         rows = feat_ref[pl.ds(i * LANES, LANES), :]
-        parts = fill(i * LANES, rows, pos[:, i * LANES : (i + 1) * LANES], (0.0, 0.0, 0.0))
+        fill(i * LANES, rows, pos[:, i * LANES : (i + 1) * LANES], (0.0, 0.0))
         own = jnp.dot(rows, w_self_ref[...], preferred_element_type=F32)
-        own_ref[0, pl.ds(i * LANES, LANES), :] = own * 0.5
-        for a in range(3):
-            own_ref[1 + a, pl.ds(i * LANES, LANES), :] = parts[2 + a]
+        own_ref[pl.ds(i * LANES, LANES), :] = own * 0.5
     for sx in range(3):
         for sy, ref in enumerate((up_ref, mid_ref, down_ref)):
             block = 3 * sx + sy
             if block == 4:
                 continue
             tail = ref[sx, pl.ds(ghosts, EXTRA), :].astype(F32)
-            shift = ((sx - 1) * BOX, (sy - 1) * BOX, 0.0)
             for h in range(ghosts // LANES):
                 rows = ref[sx, pl.ds(h * LANES, LANES), :]
                 start = atoms + block * ghosts + h * LANES
-                fill(start, rows, tail[h * 8 : (h + 1) * 8], shift)
+                fill(start, rows, tail[h * 8 : (h + 1) * 8], ((sx - 1) * BOX, (sy - 1) * BOX))
+
+    feature = lax.broadcasted_iota(jnp.int32, (8, LANES), 0)
+    skipped = range((atoms + 4 * ghosts) // LANES, (atoms + 5 * ghosts) // LANES)
+    for i in range(atoms // LANES):
+        columns = slice(i * LANES, (i + 1) * LANES)
+        index = index_ref[:, columns]
+        inside = index & (LANES - 1)
+        outside = lax.shift_right_logical(index, 7)
+        found = [jnp.zeros((per_atom, LANES), F32)] * 3
+        for c in range(slots_all // LANES):
+            if c in skipped:
+                continue
+            tile = places[c]
+            here = outside == c
+            for a in range(3):
+                source = jnp.broadcast_to(tile[a : a + 1], (per_atom, LANES))
+                value = jnp.take_along_axis(source, inside, axis=1)
+                found[a] = jnp.where(here, value, found[a])
+        disp = [found[a] - pos[a : a + 1, columns] for a in range(3)]
+        d2 = disp[0] * disp[0] + disp[1] * disp[1] + disp[2] * disp[2]
+        envelope = jnp.maximum(0.0, 1.0 - d2 * (1.0 / CUTOFF_SQ))
+        envelope = envelope * envelope
+        moments = [envelope] + [envelope * disp[a] for a in range(3)]
+        for k in range(per_atom):
+            def wide(value):
+                return jnp.broadcast_to(value[k : k + 1], (8, LANES))
+
+            t = wide(d2) * (1.0 / spacing) - feature.astype(F32)
+            basis = jnp.exp(-(t * t))
+            high = basis.astype(BF16).astype(F32)
+            tail = jnp.where(feature == 0, wide(moments[0]), 0.0)
+            for a in range(3):
+                tail = jnp.where(feature == 1 + a, wide(moments[1 + a]), tail)
+            stacked = jnp.concatenate([high, basis - high, high, tail], axis=0)
+            marks[k, pl.ds(i * LANES, LANES), :] = stacked.T
 
     w_radial = w_radial_ref[...] * 0.5
     high = w_radial.astype(BF16).astype(F32)
     w_basis = jnp.concatenate(
-        [high, high, w_radial - high, jnp.zeros((LANES - 3 * basis_count, channels), F32)], axis=0
+        [high, high, w_radial - high, jnp.zeros((8, channels), F32)], axis=0
     ).astype(BF16)
-    lane = lax.broadcasted_iota(jnp.int32, (1, LANES), 1)
-    center = (lane % basis_count).astype(F32)
-    use_low = (lane // basis_count) == 1
-
-    piece = chunk // PIECES
-    slots = per_atom // PIECES
-    latent = w_expand_ref.shape[1]
-    width = latent // PIECES
-    w_half[...] = w_expand_ref[...] * 0.5
 
     def gather(index, near, part):
         for k in range(part * slots, (part + 1) * slots):
             for a in range(CHUNK_ATOMS):
-                j = pl.multiple_of(list_ref[k * atoms + index * CHUNK_ATOMS + a], 8)
+                j = list_ref[k * atoms + index * CHUNK_ATOMS + a]
                 e = k * CHUNK_ATOMS + a
-                near[pl.ds(e * 8, 8), :] = table[pl.ds(j, 8), :]
-
-    def geometry(index, near, edge_in, aux, part):
+                near[pl.ds(e, 2, stride=chunk), :] = table[pl.ds(j, 2, stride=slots_all), :]
+
+    def enter(index, near, edge_in, part):
         first = pl.multiple_of(index * CHUNK_ATOMS, 8)
-        rows = pl.ds(part * piece, piece)
-
-        def per_edge(s):
-            start = part * piece * 8 + s
-            return near[pl.ds(start, piece, stride=8), :].reshape(slots, CHUNK_ATOMS, LANES)
-
-        def own(s):
-            return own_ref[s, pl.ds(first, CHUNK_ATOMS), :][None]
-
-        disp = [per_edge(2 + a) - own(1 + a) for a in range(3)]
-        d2 = disp[0] * disp[0] + disp[1] * disp[1] + disp[2] * disp[2]
-        t = (d2 * (1.0 / spacing)).reshape(piece, LANES) - center
-        basis = jnp.exp(-(t * t))
-        basis_high = basis.astype(BF16).astype(F32)
-        mixed = jnp.where(use_low, basis - basis_high, basis_high).astype(BF16)
-        radial = jnp.dot(mixed, w_basis, preferred_element_type=F32)
-        half = radial.reshape(slots, CHUNK_ATOMS, LANES) + own(0) + per_edge(0)
-        edge_in[rows, :] = (half + half * jnp.tanh(half)).astype(BF16).reshape(piece, LANES)
-        envelope = jnp.maximum(0.0, 1.0 - d2 * (1.0 / CUTOFF_SQ))
-        aux[0, rows, :] = (envelope * envelope * per_edge(1)).reshape(piece, LANES)
-        for a in range(3):
-            aux[1 + a, rows, :] = disp[a].reshape(piece, LANES)
+        rows = pl.ds(part * slots * CHUNK_ATOMS, slots * CHUNK_ATOMS)
+        shape = (slots, CHUNK_ATOMS, LANES)
+        basis = marks[pl.ds(part * slots, slots), pl.ds(first, CHUNK_ATOMS), :]
+        basis = basis.reshape(slots * CHUNK_ATOMS, basis.shape[2]).astype(BF16)
+        radial = jnp.dot(basis, w_basis, preferred_element_type=F32).reshape(shape)
+        own = own_ref[pl.ds(first, CHUNK_ATOMS), :][None]
+        half = radial + own + near[rows, :].reshape(shape)
+        edge_in[rows, :] = (half + half * jnp.tanh(half)).astype(BF16).reshape(-1, LANES)
 
     def network(edge_in, part):
         cols = pl.ds(part * width, width)
@@ -392,38 +396,39 @@
         hidden = (half + half * jnp.tanh(half)).astype(BF16)
         return jnp.dot(hidden, w_contract_ref[cols, :], preferred_element_type=F32)
 
-    def collect(index, mixed, aux):
+    def collect(index, mixed, near):
         first = pl.multiple_of(index * CHUNK_ATOMS, 8)
-        shape = (per_atom, CHUNK_ATOMS, LANES)
-        weight = (mixed * aux[0]).reshape(shape)
-        sums_ref[0, pl.ds(first, CHUNK_ATOMS), :] = jnp.sum(weight, axis=0)
-        for a in range(3):
-            moment = jnp.sum(aux[1 + a].reshape(shape) * weight, axis=0)
-            sums_ref[1 + a, pl.ds(first, CHUNK_ATOMS), :] = moment
-
-    def stage(index, near, near_next, edge_in, edge_next, aux, aux_next):
+        weight = (mixed * near[pl.ds(chunk, chunk), :]).reshape(per_atom, CHUNK_ATOMS, LANES)
+        for s in range(4):
+            mark = marks[:, pl.ds(first, CHUNK_ATOMS), 3 * basis_count + s : 3 * basis_count + s + 1]
+            sums_ref[s, pl.ds(first, CHUNK_ATOMS), :] = jnp.sum(weight * mark, axis=0)
+
+    def stage(index, nears, edges):
         after = jnp.minimum(index + 1, chunks - 1)
         later = jnp.minimum(index + 2, chunks - 1)
         mixed = None
         for part in range(PIECES):
-            gather(later, near, part)
-            geometry(after, near_next, edge_next, aux_next, part)
-            term = network(edge_in, part)
+            gather(later, nears[2], part)
+            enter(after, nears[1], edges[1], part)
+            term = network(edges[0], part)
             mixed = term if mixed is None else mixed + term
-        collect(index, mixed, aux)
-
+        collect(index, mixed, nears[0])
+
+    nears = (near_a, near_b, near_c)
+    edges = (edge_a, edge_b, edge_c)
     for part in range(PIECES):
         gather(0, near_a, part)
     for part in range(PIECES):
         gather(1, near_b, part)
-        geometry(0, near_a, edge_a, aux_a, part)
-
-    def pair(step, carry):
-        stage(2 * step, near_a, near_b, edge_a, edge_b, aux_a, aux_b)
-        stage(2 * step + 1, near_b, near_a, edge_b, edge_a, aux_b, aux_a)
+        enter(0, near_a, edge_a, part)
+
+    def triple(step, carry):
+        for i in range(3):
+            order = (i, (i + 1) % 3, (i + 2) % 3)
+            stage(3 * step + i, [nears[o] for o in order], [edges[o] for o in order])
         return carry
 
-    lax.fori_loop(0, chunks // 2, pair, 0)
+    lax.fori_loop(0, chunks // 3, triple, 0)
 
     scale = 1.0 / math.sqrt(per_atom)
     vector = [sums_ref[1 + a] * scale for a in range(3)]
@@ -436,30 +441,29 @@
     out_ref[...] = jnp.concatenate(short, axis=0)
 
 
-def edge_forces(per_atom, lists, feat, pos, mid, up, down, w_self, w_pair, w_radial, w_expand, w_contract, w_final):
+def edge_forces(index, feat, pos, mid, up, down, w_self, w_pair, w_radial, w_expand, w_contract, w_final):
     atoms, channels = feat.shape
+    per_atom = index.shape[0]
     ghosts = mid.shape[1] - EXTRA
+    slots_all = atoms + 9 * ghosts
     chunk = CHUNK_ATOMS * per_atom
     vmem = pl.BlockSpec(memory_space=pltpu.VMEM)
-    near = pltpu.VMEM((chunk * 8, LANES), F32)
-    edge = pltpu.VMEM((chunk, LANES), BF16)
-    aux = pltpu.VMEM((4, chunk, LANES), F32)
     edges = atoms * per_atom
     latent = w_expand.shape[1]
     return pl.pallas_call(
         edge_kernel,
-        in_specs=[pl.BlockSpec(memory_space=pltpu.SMEM)] + [vmem] * 11,
+        in_specs=[pl.BlockSpec(memory_space=pltpu.SMEM)] + [vmem] * 12,
         out_specs=vmem,
         out_shape=jax.ShapeDtypeStruct((3, atoms), F32),
         scratch_shapes=[
-            pltpu.VMEM(((atoms + 9 * ghosts) * 8, LANES), F32),
-            near,
-            near,
-            edge,
-            edge,
-            aux,
-            aux,
-            pltpu.VMEM((4, atoms, LANES), F32),
+            pltpu.VMEM((2 * slots_all, LANES), F32),
+            pltpu.VMEM((slots_all // LANES, 8, LANES), F32),
+        ]
+        + [pltpu.VMEM((2 * chunk, LANES), F32)] * 3
+        + [pltpu.VMEM((chunk, LANES), BF16)] * 3
+        + [
+            pltpu.VMEM((per_atom, atoms, 32), F32),
+            pltpu.VMEM((atoms, LANES), F32),
             pltpu.VMEM((4, atoms, LANES), F32),
             pltpu.VMEM(w_expand.shape, BF16),
         ],
@@ -471,7 +475,7 @@
         ),
         name="edge_forces",
     )(
-        lists, feat, pos, mid, up, down, w_self, w_pair, w_radial,
+        index.reshape(-1), index, feat, pos, mid, up, down, w_self, w_pair, w_radial,
         w_expand, w_contract, w_final,
     )
 
@@ -494,7 +498,7 @@
     spread = jnp.broadcast_to(charge_cell, (cycle_x * cycle_y,) + charge_cell.shape)
     gathered = lax.all_to_all(spread, ("dx", "dy"), split_axis=0, concat_axis=0, tiled=True)
     mid = jnp.stack([ring(exported, "dx", 1), exported, ring(exported, "dx", -1)])
-    lists = (neighbour_list[0, 0] * 8).T.reshape(-1)
+    lists = neighbour_list[0, 0].T
     gathered, mid, lists = lax.optimization_barrier((gathered, mid, lists))
     up = ring(mid, "dy", 1)
     down = ring(mid, "dy", -1)
@@ -502,7 +506,7 @@
     partial = grid_fields(place[None].astype(jnp.int32), gathered, cycle_x, cycle_y)
     received = lax.all_to_all(partial, ("dx", "dy"), split_axis=0, concat_axis=0, tiled=True)
     short = edge_forces(
-        neighbour_list.shape[3], lists, feat, pos, mid, up, down, w_self, w_pair, w_radial, w_expand,
+        lists, feat, pos, mid, up, down, w_self, w_pair, w_radial, w_expand,
         w_contract, w_final,
     )
     field = jnp.sum(received, axis=0)

time: 81.3 us -> 84.1 us (1.034)
  Pallas kernels: 54.1 us -> 56.2 us
  waiting for transfers between devices: 6.58 us -> 7.46 us
    pallas_call x1, Pallas kernels: 34.9 us -> 37 us  [edge_forces(): pl.pallas_call(edge_kernel, in_specs=[pl.BlockSpec(memory_space=pltpu.SME...]
    all_to_all x1, waiting for transfers between devices: 6.57 us -> 7.44 us  [shards(): lax.all_to_all(spread, ('dx', 'dy'), split_axis=0, concat_axis=0, tiled=T...]
where the time goes in v3:
time: 84.1 us; the launch traced here: 83.7 us
  Pallas kernels  56.2 us (67%)
  starting transfers between devices  15.3 us (18%)
  waiting for transfers between devices  7.46 us (9%)
  local copies, waits for them, and re-layouts  3.88 us (5%)
    pallas_call x1, Pallas kernels, edge_forces(): pl.pallas_call(edge_kernel, in_specs=[pl.BlockSpec(memory_space=pltpu.SME...  37 us
    pallas_call x1, Pallas kernels, grid_fields(): pl.pallas_call(functools.partial(grid_kernel, cycle_x, cycle_y), in_specs...  17.4 us
    all_to_all x1, waiting for transfers between devices, shards(): lax.all_to_all(spread, ('dx', 'dy'), split_axis=0, concat_axis=0, tiled=T...  7.44 us
    all_to_all x1, starting transfers between devices, shards(): lax.all_to_all(spread, ('dx', 'dy'), split_axis=0, concat_axis=0, tiled=T...  6.1 us
    all_to_all x1, starting transfers between devices, shards(): lax.all_to_all(partial, ('dx', 'dy'), split_axis=0, concat_axis=0, tiled=...  4.78 us
    ppermute x4, starting transfers between devices, ring(): lax.ppermute(array, axis, [(i, (i + step) % size) for i in range(size)])  4.41 us
    unnamed x16, local copies, waits for them, and re-layouts  1.98 us
    pallas_call x1, Pallas kernels, prepare(): pl.pallas_call(prepare_kernel, in_specs=[pl.BlockSpec(memory_space=pltpu....  1.84 us
  transfers between devices with their start and end apart: 6, of which 1 were waited for; matrix products, arithmetic and copies ran while one was open for 2% of the time, Pallas kernels for 65%

profile of v3, /device:TPU:0, one launch (start us, length us, event | category | flops | bytes accessed | tf_op | source)
XLA Modules:
  0.0 83.7 jit_solution(17839618768181846412)
XLA Ops:
  0.7 1.8 %prepare.1 = (bf16[272,128]{1,0:T(8,128)(2,1)}, f32[2,384]{1,0:T(2,128)}) custom-call(s32[1,1]{1,0:T(1,128)} %copy.20.count_ref, bf16[384,128]{1,0:T(8,128)(2,1)} %bitcast.16, bf16[3,384]{1,0:T(4,128)(2,1)} %bitcast.23, s32[1,256]{1,0:T(1,128)} %bitcast.26, s32[1,384]{1,0:T(1,128)} %bitcast.25, bf16[1,128]{1,0:T(2,128)(2,1)} %bitcast.27), custom_call_target="tpu_custom_call" | custom-call | tf_op jit(solution)/shard_map/prepare/pallas_call | solution.py:62
  2.5 0.0 copy-start.4
  2.5 2.4 %collective-permute-start.1 = (bf16[272,128]{1,0:T(8,128)(2,1)}, bf16[272,128]{1,0:T(8,128)(2,1)S(1)}, u32[]{:S(2)}, u32[]{:S(2)}) collective-permute-start(bf16[272,128]{1,0:T(8,128)(2,1)} %get-tuple-element.11), channel_id=1, source_target_pairs={{0,24},{8,0},{16,8},{24,16},{1,25},{9,1},{17,9},{25,17},{2,26},{10... | collective-permute-start | bytes 208904 | tf_op jit(solution)/shard_map/ppermute | solution.py:485
  4.9 0.0 collective-permute-start
  4.9 0.0 copy-done.4
  4.9 0.7 broadcast_in_dim.25
  5.5 0.0 copy-start.2
  5.5 6.1 %all-to-all-start = ((f32[32,2,384]{2,1,0:T(2,128)}), f32[32,2,384]{2,1,0:T(2,128)S(1)}, u32[]{:S(2)}, u32[]{:S(2)}) async-start(f32[32,2,384]{2,1,0:T(2,128)} %broadcast_in_dim.25), calls=%async_computation | async-start | bytes 196608 | tf_op jit(solution)/shard_map/all_to_all | solution.py:499
  11.7 0.0 collective-permute-done.1
  11.7 0.0 collective-permute-done
  11.7 0.0 copy-done.2
  11.8 0.0 copy-start
  11.8 7.4 %all-to-all-done.qc_ref = f32[32,2,384]{2,1,0:T(2,128)S(1)} async-done(((f32[32,2,384]{2,1,0:T(2,128)}), f32[32,2,384]{2,1,0:T(2,128)S(1)}, u32[]{:S(2)}, u32[]{:S(2)}) %all-to-all-start) | async-done | bytes 98336 | tf_op jit(solution)/shard_map/all_to_all | solution.py:499
  19.2 0.0 copy-start.1
  19.2 1.5 %collective-permute-start.3 = (bf16[3,272,128]{2,1,0:T(8,128)(2,1)S(1)}, bf16[3,272,128]{2,1,0:T(8,128)(2,1)S(1)}, u32[]{:S(2)}, u32[]{:S(2)}) collective-permute-start(bf16[3,272,128]{2,1,0:T(8,128)(2,1)S(1)} %pad_maximum_fusion.mid_ref), channel_id=1, source_target_pairs={{0,7},{1,0},{2,1},{3,2},{4,3},{5,4},{6,5},{7,6},{8,15},{9,8},{10,9... | collective-permute-start | bytes 626696 | tf_op jit(solution)/shard_map/ppermute | solution.py:485
  20.8 0.5 collective-permute-start.2
  21.2 0.0 copy-done.1
  21.2 0.0 copy-start.3
  21.3 17.4 %grid_fields.1 = f32[32,3,384]{2,1,0:T(4,128)} custom-call(s32[1]{0:T(128)} %bitcast.11.place_ref, f32[32,2,384]{2,1,0:T(2,128)} %copy-done.1, f32[256,256]{1,0:T(8,128)} %constant.23.clone.fy_table, f32[256,256]{1,0:T(8,128)} %constant.24.clone.fx_table, f32[512,256]{1,0:T(8,128)} %constant.25.clone.ix_table, f32[256,256]{1,0:T(8,128)} %constant.26.clone.iy_table, ...), custom_call_target="tpu_custom_call" | custom-call | flops 8000000000 | bytes 4000000 | tf_op jit(solution)/shard_map/grid_fields/pallas_call | solution.py:273
  38.7 0.0 copy-done
  38.7 0.0 copy-done.3
  38.7 0.6 reshape.8.list_ref
  39.3 4.8 %all-to-all-start.1 = ((f32[32,3,384]{2,1,0:T(4,128)}), f32[32,3,384]{2,1,0:T(4,128)S(1)}, u32[]{:S(2)}, u32[]{:S(2)}) async-start(f32[32,3,384]{2,1,0:T(4,128)} %grid_fields.1), calls=%async_computation.1 | async-start | bytes 393216 | tf_op jit(solution)/shard_map/all_to_all | solution.py:507
  44.1 0.0 collective-permute-done.3.down_ref
  44.1 0.0 copy-start.6
  44.1 0.0 collective-permute-done.2.up_ref
  44.1 0.6 copy-done.6
  44.8 0.0 copy-start.7
  44.8 0.7 copy-done.7
  45.4 37.0 %edge_forces.1 = f32[3,384]{1,0:T(4,128)} custom-call(s32[12288]{0:T(1024)} %reshape.8.list_ref, s32[32,384]{1,0:T(8,128)} %bitcast.21, bf16[384,128]{1,0:T(8,128)(2,1)} %bitcast.17, bf16[3,384]{1,0:T(4,128)(2,1)} %bitcast.24, bf16[3,272,128]{2,1,0:T(8,128)(2,1)} %copy-done, bf16[3,272,128]{2,1,0:T(8,128)(2,1)} %copy-done.7, bf16[3,272,128]{2,1,0:T(8,128)(2,1)} %copy-done.6, ...), custom_call_target="tpu_custom_call" | custom-call | flops 6442450944 | bytes 4000000 | tf_op jit(solution)/shard_map/edge_forces/pallas_call | solution.py:453
  82.4 0.0 copy-start.5
  82.4 0.0 all-to-all-done.1
  82.4 0.1 reduce_sum.9
  82.5 0.6 copy-done.5
  83.1 0.6 copy.19
  (4 shorter events, 0.1 us)
Async XLA Ops:
  2.5 2.4 %copy-start.4 = (f32[2,384]{1,0:T(2,128)S(1)}, f32[2,384]{1,0:T(2,128)}, u32[]{:S(2)}) copy-start(f32[2,384]{1,0:T(2,128)} %get-tuple-element.10) | copy-start | bytes 9220
  2.5 9.2 %collective-permute-start.1 = (bf16[272,128]{1,0:T(8,128)(2,1)}, bf16[272,128]{1,0:T(8,128)(2,1)S(1)}, u32[]{:S(2)}, u32[]{:S(2)}) collective-permute-start(bf16[272,128]{1,0:T(8,128)(2,1)} %get-tuple-element.11), channel_id=1, source_target_pairs={{0,24},{8,0},{16,8},{24,16},{1,25},{9,1},{17,9},{25,17},{2,26},{10... | collective-permute-start | bytes 208904 | tf_op jit(solution)/shard_map/ppermute | solution.py:485
  4.9 6.8 %collective-permute-start = (bf16[272,128]{1,0:T(8,128)(2,1)}, bf16[272,128]{1,0:T(8,128)(2,1)S(1)}, u32[]{:S(2)}, u32[]{:S(2)}) collective-permute-start(bf16[272,128]{1,0:T(8,128)(2,1)} %get-tuple-element.11), channel_id=1, source_target_pairs={{0,8},{8,16},{16,24},{24,0},{1,9},{9,17},{17,25},{25,1},{2,10},{10... | collective-permute-start | bytes 208904 | tf_op jit(solution)/shard_map/ppermute | solution.py:485
  5.5 6.2 %copy-start.2 = (bf16[272,128]{1,0:T(8,128)(2,1)S(1)}, bf16[272,128]{1,0:T(8,128)(2,1)}, u32[]{:S(2)}) copy-start(bf16[272,128]{1,0:T(8,128)(2,1)} %get-tuple-element.11) | copy-start | bytes 208900
  5.5 13.7 %all-to-all-start = ((f32[32,2,384]{2,1,0:T(2,128)}), f32[32,2,384]{2,1,0:T(2,128)S(1)}, u32[]{:S(2)}, u32[]{:S(2)}) async-start(f32[32,2,384]{2,1,0:T(2,128)} %broadcast_in_dim.25), calls=%async_computation | async-start | bytes 196608 | tf_op jit(solution)/shard_map/all_to_all | solution.py:499
  11.8 26.9 %copy-start = (bf16[3,272,128]{2,1,0:T(8,128)(2,1)}, bf16[3,272,128]{2,1,0:T(8,128)(2,1)S(1)}, u32[]{:S(2)}) copy-start(bf16[3,272,128]{2,1,0:T(8,128)(2,1)S(1)} %pad_maximum_fusion.mid_ref) | copy-start | bytes 626692
  19.2 2.0 %copy-start.1 = (f32[32,2,384]{2,1,0:T(2,128)}, f32[32,2,384]{2,1,0:T(2,128)S(1)}, u32[]{:S(2)}) copy-start(f32[32,2,384]{2,1,0:T(2,128)S(1)} %all-to-all-done.qc_ref) | copy-start | bytes 294916
  19.2 24.9 %collective-permute-start.3 = (bf16[3,272,128]{2,1,0:T(8,128)(2,1)S(1)}, bf16[3,272,128]{2,1,0:T(8,128)(2,1)S(1)}, u32[]{:S(2)}, u32[]{:S(2)}) collective-permute-start(bf16[3,272,128]{2,1,0:T(8,128)(2,1)S(1)} %pad_maximum_fusion.mid_ref), channel_id=1, source_target_pairs={{0,7},{1,0},{2,1},{3,2},{4,3},{5,4},{6,5},{7,6},{8,15},{9,8},{10,9... | collective-permute-start | bytes 626696 | tf_op jit(solution)/shard_map/ppermute | solution.py:485
  20.8 23.3 %collective-permute-start.2 = (bf16[3,272,128]{2,1,0:T(8,128)(2,1)S(1)}, bf16[3,272,128]{2,1,0:T(8,128)(2,1)S(1)}, u32[]{:S(2)}, u32[]{:S(2)}) collective-permute-start(bf16[3,272,128]{2,1,0:T(8,128)(2,1)S(1)} %pad_maximum_fusion.mid_ref), channel_id=1, source_target_pairs={{0,1},{1,2},{2,3},{3,4},{4,5},{5,6},{6,7},{7,0},{8,9},{9,10},{10,1... | collective-permute-start | bytes 626696 | tf_op jit(solution)/shard_map/ppermute | solution.py:485
  21.2 17.4 %copy-start.3 = (s32[1,1,384,32]{2,3,1,0:T(8,128)S(1)}, s32[1,1,384,32]{2,3,1,0:T(8,128)}, u32[]{:S(2)}) copy-start(s32[1,1,384,32]{2,3,1,0:T(8,128)} %param.22) | copy-start | bytes 147460
  39.3 43.1 %all-to-all-start.1 = ((f32[32,3,384]{2,1,0:T(4,128)}), f32[32,3,384]{2,1,0:T(4,128)S(1)}, u32[]{:S(2)}, u32[]{:S(2)}) async-start(f32[32,3,384]{2,1,0:T(4,128)} %grid_fields.1), calls=%async_computation.1 | async-start | bytes 393216 | tf_op jit(solution)/shard_map/all_to_all | solution.py:507
  44.1 0.7 copy-start.6
  44.8 0.7 copy-start.7
  82.4 0.7 copy-start.5

commit v4 on v3

--- a/solution.py
+++ b/solution.py
@@ -388,12 +388,13 @@
         radial = jnp.dot(basis, w_basis, preferred_element_type=F32).reshape(shape)
         own = own_ref[pl.ds(first, CHUNK_ATOMS), :][None]
         half = radial + own + near[rows, :].reshape(shape)
-        edge_in[rows, :] = (half + half * jnp.tanh(half)).astype(BF16).reshape(-1, LANES)
+        turn = jnp.tanh(half.astype(BF16)).astype(F32)
+        edge_in[rows, :] = (half + half * turn).astype(BF16).reshape(-1, LANES)
 
     def network(edge_in, part):
         cols = pl.ds(part * width, width)
-        half = jnp.dot(edge_in[...], w_half[:, cols], preferred_element_type=F32)
-        hidden = (half + half * jnp.tanh(half)).astype(BF16)
+        half = jnp.dot(edge_in[...], w_half[:, cols], preferred_element_type=F32).astype(BF16)
+        hidden = half + half * jnp.tanh(half)
         return jnp.dot(hidden, w_contract_ref[cols, :], preferred_element_type=F32)
 
     def collect(index, mixed, near):

time: 84.1 us -> 82.7 us (0.983)
  Pallas kernels: 56.2 us -> 54.9 us
    pallas_call x1, Pallas kernels: 37 us -> 35.6 us  [edge_forces(): pl.pallas_call(edge_kernel, in_specs=[pl.BlockSpec(memory_space=pltpu.SME...]
  transfers between devices with their start and end apart: 6 -> 6, of which waited for: 1 -> 1; matrix products, arithmetic and copies ran while one was open for 2% -> 2% of each run, Pallas kernels for 65% -> 64%
where the time goes in v4:
time: 82.7 us; the launch traced here: 82.3 us
  Pallas kernels  54.9 us (66%)
  starting transfers between devices  15.3 us (19%)
  waiting for transfers between devices  7.46 us (9%)
  local copies, waits for them, and re-layouts  3.88 us (5%)
    pallas_call x1, Pallas kernels, edge_forces(): pl.pallas_call(edge_kernel, in_specs=[pl.BlockSpec(memory_space=pltpu.SME...  35.6 us
    pallas_call x1, Pallas kernels, grid_fields(): pl.pallas_call(functools.partial(grid_kernel, cycle_x, cycle_y), in_specs...  17.4 us
    all_to_all x1, waiting for transfers between devices, shards(): lax.all_to_all(spread, ('dx', 'dy'), split_axis=0, concat_axis=0, tiled=T...  7.44 us
    all_to_all x1, starting transfers between devices, shards(): lax.all_to_all(spread, ('dx', 'dy'), split_axis=0, concat_axis=0, tiled=T...  6.1 us
    all_to_all x1, starting transfers between devices, shards(): lax.all_to_all(partial, ('dx', 'dy'), split_axis=0, concat_axis=0, tiled=...  4.78 us
    ppermute x4, starting transfers between devices, ring(): lax.ppermute(array, axis, [(i, (i + step) % size) for i in range(size)])  4.41 us
    unnamed x16, local copies, waits for them, and re-layouts  1.98 us
    pallas_call x1, Pallas kernels, prepare(): pl.pallas_call(prepare_kernel, in_specs=[pl.BlockSpec(memory_space=pltpu....  1.84 us
  transfers between devices with their start and end apart: 6, of which 1 were waited for; matrix products, arithmetic and copies ran while one was open for 2% of the time, Pallas kernels for 64%

profile of v4, /device:TPU:0, one launch (start us, length us, event | category | flops | bytes accessed | tf_op | source)
XLA Modules:
  0.0 82.3 jit_solution(263874794980854306)
XLA Ops:
  0.7 1.8 %prepare.1 = (bf16[272,128]{1,0:T(8,128)(2,1)}, f32[2,384]{1,0:T(2,128)}) custom-call(s32[1,1]{1,0:T(1,128)} %copy.20.count_ref, bf16[384,128]{1,0:T(8,128)(2,1)} %bitcast.16, bf16[3,384]{1,0:T(4,128)(2,1)} %bitcast.23, s32[1,256]{1,0:T(1,128)} %bitcast.26, s32[1,384]{1,0:T(1,128)} %bitcast.25, bf16[1,128]{1,0:T(2,128)(2,1)} %bitcast.27), custom_call_target="tpu_custom_call" | custom-call | tf_op jit(solution)/shard_map/prepare/pallas_call | solution.py:62
  2.5 0.0 copy-start.4
  2.5 2.4 %collective-permute-start.1 = (bf16[272,128]{1,0:T(8,128)(2,1)}, bf16[272,128]{1,0:T(8,128)(2,1)S(1)}, u32[]{:S(2)}, u32[]{:S(2)}) collective-permute-start(bf16[272,128]{1,0:T(8,128)(2,1)} %get-tuple-element.11), channel_id=1, source_target_pairs={{0,24},{8,0},{16,8},{24,16},{1,25},{9,1},{17,9},{25,17},{2,26},{10... | collective-permute-start | bytes 208904 | tf_op jit(solution)/shard_map/ppermute | solution.py:486
  4.9 0.0 collective-permute-start
  4.9 0.0 copy-done.4
  4.9 0.7 broadcast_in_dim.25
  5.5 0.0 copy-start.2
  5.5 6.1 %all-to-all-start = ((f32[32,2,384]{2,1,0:T(2,128)}), f32[32,2,384]{2,1,0:T(2,128)S(1)}, u32[]{:S(2)}, u32[]{:S(2)}) async-start(f32[32,2,384]{2,1,0:T(2,128)} %broadcast_in_dim.25), calls=%async_computation | async-start | bytes 196608 | tf_op jit(solution)/shard_map/all_to_all | solution.py:500
  11.7 0.0 collective-permute-done.1
  11.7 0.0 collective-permute-done
  11.7 0.0 copy-done.2
  11.8 0.0 copy-start
  11.8 7.4 %all-to-all-done.qc_ref = f32[32,2,384]{2,1,0:T(2,128)S(1)} async-done(((f32[32,2,384]{2,1,0:T(2,128)}), f32[32,2,384]{2,1,0:T(2,128)S(1)}, u32[]{:S(2)}, u32[]{:S(2)}) %all-to-all-start) | async-done | bytes 98336 | tf_op jit(solution)/shard_map/all_to_all | solution.py:500
  19.2 0.0 copy-start.1
  19.2 1.5 %collective-permute-start.3 = (bf16[3,272,128]{2,1,0:T(8,128)(2,1)S(1)}, bf16[3,272,128]{2,1,0:T(8,128)(2,1)S(1)}, u32[]{:S(2)}, u32[]{:S(2)}) collective-permute-start(bf16[3,272,128]{2,1,0:T(8,128)(2,1)S(1)} %pad_maximum_fusion.mid_ref), channel_id=1, source_target_pairs={{0,7},{1,0},{2,1},{3,2},{4,3},{5,4},{6,5},{7,6},{8,15},{9,8},{10,9... | collective-permute-start | bytes 626696 | tf_op jit(solution)/shard_map/ppermute | solution.py:486
  20.8 0.5 collective-permute-start.2
  21.2 0.0 copy-done.1
  21.2 0.0 copy-start.3
  21.3 17.4 %grid_fields.1 = f32[32,3,384]{2,1,0:T(4,128)} custom-call(s32[1]{0:T(128)} %bitcast.11.place_ref, f32[32,2,384]{2,1,0:T(2,128)} %copy-done.1, f32[256,256]{1,0:T(8,128)} %constant.23.clone.fy_table, f32[256,256]{1,0:T(8,128)} %constant.24.clone.fx_table, f32[512,256]{1,0:T(8,128)} %constant.25.clone.ix_table, f32[256,256]{1,0:T(8,128)} %constant.26.clone.iy_table, ...), custom_call_target="tpu_custom_call" | custom-call | flops 8000000000 | bytes 4000000 | tf_op jit(solution)/shard_map/grid_fields/pallas_call | solution.py:273
  38.7 0.0 copy-done
  38.7 0.0 copy-done.3
  38.7 0.6 reshape.8.list_ref
  39.3 4.8 %all-to-all-start.1 = ((f32[32,3,384]{2,1,0:T(4,128)}), f32[32,3,384]{2,1,0:T(4,128)S(1)}, u32[]{:S(2)}, u32[]{:S(2)}) async-start(f32[32,3,384]{2,1,0:T(4,128)} %grid_fields.1), calls=%async_computation.1 | async-start | bytes 393216 | tf_op jit(solution)/shard_map/all_to_all | solution.py:508
  44.1 0.0 collective-permute-done.3.down_ref
  44.1 0.0 copy-start.6
  44.1 0.0 collective-permute-done.2.up_ref
  44.1 0.6 copy-done.6
  44.8 0.0 copy-start.7
  44.8 0.7 copy-done.7
  45.4 35.6 %edge_forces.1 = f32[3,384]{1,0:T(4,128)} custom-call(s32[12288]{0:T(1024)} %reshape.8.list_ref, s32[32,384]{1,0:T(8,128)} %bitcast.21, bf16[384,128]{1,0:T(8,128)(2,1)} %bitcast.17, bf16[3,384]{1,0:T(4,128)(2,1)} %bitcast.24, bf16[3,272,128]{2,1,0:T(8,128)(2,1)} %copy-done, bf16[3,272,128]{2,1,0:T(8,128)(2,1)} %copy-done.7, bf16[3,272,128]{2,1,0:T(8,128)(2,1)} %copy-done.6, ...), custom_call_target="tpu_custom_call" | custom-call | flops 6442450944 | bytes 4000000 | tf_op jit(solution)/shard_map/edge_forces/pallas_call | solution.py:454
  81.0 0.0 copy-start.5
  81.0 0.0 all-to-all-done.1
  81.0 0.1 reduce_sum.9
  81.1 0.6 copy-done.5
  81.7 0.6 copy.19
  (4 shorter events, 0.1 us)
Async XLA Ops:
  2.5 2.4 %copy-start.4 = (f32[2,384]{1,0:T(2,128)S(1)}, f32[2,384]{1,0:T(2,128)}, u32[]{:S(2)}) copy-start(f32[2,384]{1,0:T(2,128)} %get-tuple-element.10) | copy-start | bytes 9220
  2.5 9.2 %collective-permute-start.1 = (bf16[272,128]{1,0:T(8,128)(2,1)}, bf16[272,128]{1,0:T(8,128)(2,1)S(1)}, u32[]{:S(2)}, u32[]{:S(2)}) collective-permute-start(bf16[272,128]{1,0:T(8,128)(2,1)} %get-tuple-element.11), channel_id=1, source_target_pairs={{0,24},{8,0},{16,8},{24,16},{1,25},{9,1},{17,9},{25,17},{2,26},{10... | collective-permute-start | bytes 208904 | tf_op jit(solution)/shard_map/ppermute | solution.py:486
  4.9 6.8 %collective-permute-start = (bf16[272,128]{1,0:T(8,128)(2,1)}, bf16[272,128]{1,0:T(8,128)(2,1)S(1)}, u32[]{:S(2)}, u32[]{:S(2)}) collective-permute-start(bf16[272,128]{1,0:T(8,128)(2,1)} %get-tuple-element.11), channel_id=1, source_target_pairs={{0,8},{8,16},{16,24},{24,0},{1,9},{9,17},{17,25},{25,1},{2,10},{10... | collective-permute-start | bytes 208904 | tf_op jit(solution)/shard_map/ppermute | solution.py:486
  5.5 6.2 %copy-start.2 = (bf16[272,128]{1,0:T(8,128)(2,1)S(1)}, bf16[272,128]{1,0:T(8,128)(2,1)}, u32[]{:S(2)}) copy-start(bf16[272,128]{1,0:T(8,128)(2,1)} %get-tuple-element.11) | copy-start | bytes 208900
  5.5 13.7 %all-to-all-start = ((f32[32,2,384]{2,1,0:T(2,128)}), f32[32,2,384]{2,1,0:T(2,128)S(1)}, u32[]{:S(2)}, u32[]{:S(2)}) async-start(f32[32,2,384]{2,1,0:T(2,128)} %broadcast_in_dim.25), calls=%async_computation | async-start | bytes 196608 | tf_op jit(solution)/shard_map/all_to_all | solution.py:500
  11.8 26.9 %copy-start = (bf16[3,272,128]{2,1,0:T(8,128)(2,1)}, bf16[3,272,128]{2,1,0:T(8,128)(2,1)S(1)}, u32[]{:S(2)}) copy-start(bf16[3,272,128]{2,1,0:T(8,128)(2,1)S(1)} %pad_maximum_fusion.mid_ref) | copy-start | bytes 626692
  19.2 2.0 %copy-start.1 = (f32[32,2,384]{2,1,0:T(2,128)}, f32[32,2,384]{2,1,0:T(2,128)S(1)}, u32[]{:S(2)}) copy-start(f32[32,2,384]{2,1,0:T(2,128)S(1)} %all-to-all-done.qc_ref) | copy-start | bytes 294916
  19.2 24.9 %collective-permute-start.3 = (bf16[3,272,128]{2,1,0:T(8,128)(2,1)S(1)}, bf16[3,272,128]{2,1,0:T(8,128)(2,1)S(1)}, u32[]{:S(2)}, u32[]{:S(2)}) collective-permute-start(bf16[3,272,128]{2,1,0:T(8,128)(2,1)S(1)} %pad_maximum_fusion.mid_ref), channel_id=1, source_target_pairs={{0,7},{1,0},{2,1},{3,2},{4,3},{5,4},{6,5},{7,6},{8,15},{9,8},{10,9... | collective-permute-start | bytes 626696 | tf_op jit(solution)/shard_map/ppermute | solution.py:486
  20.8 23.3 %collective-permute-start.2 = (bf16[3,272,128]{2,1,0:T(8,128)(2,1)S(1)}, bf16[3,272,128]{2,1,0:T(8,128)(2,1)S(1)}, u32[]{:S(2)}, u32[]{:S(2)}) collective-permute-start(bf16[3,272,128]{2,1,0:T(8,128)(2,1)S(1)} %pad_maximum_fusion.mid_ref), channel_id=1, source_target_pairs={{0,1},{1,2},{2,3},{3,4},{4,5},{5,6},{6,7},{7,0},{8,9},{9,10},{10,1... | collective-permute-start | bytes 626696 | tf_op jit(solution)/shard_map/ppermute | solution.py:486
  21.2 17.4 %copy-start.3 = (s32[1,1,384,32]{2,3,1,0:T(8,128)S(1)}, s32[1,1,384,32]{2,3,1,0:T(8,128)}, u32[]{:S(2)}) copy-start(s32[1,1,384,32]{2,3,1,0:T(8,128)} %param.22) | copy-start | bytes 147460
  39.3 41.8 %all-to-all-start.1 = ((f32[32,3,384]{2,1,0:T(4,128)}), f32[32,3,384]{2,1,0:T(4,128)S(1)}, u32[]{:S(2)}, u32[]{:S(2)}) async-start(f32[32,3,384]{2,1,0:T(4,128)} %grid_fields.1), calls=%async_computation.1 | async-start | bytes 393216 | tf_op jit(solution)/shard_map/all_to_all | solution.py:508
  44.1 0.7 copy-start.6
  44.8 0.7 copy-start.7
  81.0 0.7 copy-start.5

commit v5 on v4

--- a/solution.py
+++ b/solution.py
@@ -374,10 +374,13 @@
 
     def gather(index, near, part):
         for k in range(part * slots, (part + 1) * slots):
-            for a in range(CHUNK_ATOMS):
-                j = list_ref[k * atoms + index * CHUNK_ATOMS + a]
-                e = k * CHUNK_ATOMS + a
-                near[pl.ds(e, 2, stride=chunk), :] = table[pl.ds(j, 2, stride=slots_all), :]
+            start = k * atoms + index * CHUNK_ATOMS
+            loaded = [
+                table[pl.ds(list_ref[start + a], 2, stride=slots_all), :]
+                for a in range(CHUNK_ATOMS)
+            ]
+            for a, pair in enumerate(loaded):
+                near[pl.ds(k * CHUNK_ATOMS + a, 2, stride=chunk), :] = pair
 
     def enter(index, near, edge_in, part):
         first = pl.multiple_of(index * CHUNK_ATOMS, 8)

time: 82.7 us -> 83 us (level)
  no operation moved by 1% of the time
where the time goes in v5:
time: 83 us; the launch traced here: 82.6 us
  Pallas kernels  55.1 us (66%)
  starting transfers between devices  15.3 us (18%)
  waiting for transfers between devices  7.46 us (9%)
  local copies, waits for them, and re-layouts  3.88 us (5%)
    pallas_call x1, Pallas kernels, edge_forces(): pl.pallas_call(edge_kernel, in_specs=[pl.BlockSpec(memory_space=pltpu.SME...  35.8 us
    pallas_call x1, Pallas kernels, grid_fields(): pl.pallas_call(functools.partial(grid_kernel, cycle_x, cycle_y), in_specs...  17.4 us
    all_to_all x1, waiting for transfers between devices, shards(): lax.all_to_all(spread, ('dx', 'dy'), split_axis=0, concat_axis=0, tiled=T...  7.44 us
    all_to_all x1, starting transfers between devices, shards(): lax.all_to_all(spread, ('dx', 'dy'), split_axis=0, concat_axis=0, tiled=T...  6.1 us
    all_to_all x1, starting transfers between devices, shards(): lax.all_to_all(partial, ('dx', 'dy'), split_axis=0, concat_axis=0, tiled=...  4.78 us
    ppermute x4, starting transfers between devices, ring(): lax.ppermute(array, axis, [(i, (i + step) % size) for i in range(size)])  4.41 us
    unnamed x16, local copies, waits for them, and re-layouts  1.98 us
    pallas_call x1, Pallas kernels, prepare(): pl.pallas_call(prepare_kernel, in_specs=[pl.BlockSpec(memory_space=pltpu....  1.84 us
  transfers between devices with their start and end apart: 6, of which 1 were waited for; matrix products, arithmetic and copies ran while one was open for 2% of the time, Pallas kernels for 64%

profile of v5, /device:TPU:0, one launch (start us, length us, event | category | flops | bytes accessed | tf_op | source)
XLA Modules:
  0.0 82.6 jit_solution(10194224905221362907)
XLA Ops:
  0.7 1.8 %prepare.1 = (bf16[272,128]{1,0:T(8,128)(2,1)}, f32[2,384]{1,0:T(2,128)}) custom-call(s32[1,1]{1,0:T(1,128)} %copy.20.count_ref, bf16[384,128]{1,0:T(8,128)(2,1)} %bitcast.16, bf16[3,384]{1,0:T(4,128)(2,1)} %bitcast.23, s32[1,256]{1,0:T(1,128)} %bitcast.26, s32[1,384]{1,0:T(1,128)} %bitcast.25, bf16[1,128]{1,0:T(2,128)(2,1)} %bitcast.27), custom_call_target="tpu_custom_call" | custom-call | tf_op jit(solution)/shard_map/prepare/pallas_call | solution.py:62
  2.5 0.0 copy-start.4
  2.5 2.4 %collective-permute-start.1 = (bf16[272,128]{1,0:T(8,128)(2,1)}, bf16[272,128]{1,0:T(8,128)(2,1)S(1)}, u32[]{:S(2)}, u32[]{:S(2)}) collective-permute-start(bf16[272,128]{1,0:T(8,128)(2,1)} %get-tuple-element.11), channel_id=1, source_target_pairs={{0,24},{8,0},{16,8},{24,16},{1,25},{9,1},{17,9},{25,17},{2,26},{10... | collective-permute-start | bytes 208904 | tf_op jit(solution)/shard_map/ppermute | solution.py:489
  4.9 0.0 collective-permute-start
  4.9 0.0 copy-done.4
  4.9 0.7 broadcast_in_dim.25
  5.5 0.0 copy-start.2
  5.5 6.1 %all-to-all-start = ((f32[32,2,384]{2,1,0:T(2,128)}), f32[32,2,384]{2,1,0:T(2,128)S(1)}, u32[]{:S(2)}, u32[]{:S(2)}) async-start(f32[32,2,384]{2,1,0:T(2,128)} %broadcast_in_dim.25), calls=%async_computation | async-start | bytes 196608 | tf_op jit(solution)/shard_map/all_to_all | solution.py:503
  11.7 0.0 collective-permute-done.1
  11.7 0.0 collective-permute-done
  11.7 0.0 copy-done.2
  11.8 0.0 copy-start
  11.8 7.4 %all-to-all-done.qc_ref = f32[32,2,384]{2,1,0:T(2,128)S(1)} async-done(((f32[32,2,384]{2,1,0:T(2,128)}), f32[32,2,384]{2,1,0:T(2,128)S(1)}, u32[]{:S(2)}, u32[]{:S(2)}) %all-to-all-start) | async-done | bytes 98336 | tf_op jit(solution)/shard_map/all_to_all | solution.py:503
  19.2 0.0 copy-start.1
  19.2 1.5 %collective-permute-start.3 = (bf16[3,272,128]{2,1,0:T(8,128)(2,1)S(1)}, bf16[3,272,128]{2,1,0:T(8,128)(2,1)S(1)}, u32[]{:S(2)}, u32[]{:S(2)}) collective-permute-start(bf16[3,272,128]{2,1,0:T(8,128)(2,1)S(1)} %pad_maximum_fusion.mid_ref), channel_id=1, source_target_pairs={{0,7},{1,0},{2,1},{3,2},{4,3},{5,4},{6,5},{7,6},{8,15},{9,8},{10,9... | collective-permute-start | bytes 626696 | tf_op jit(solution)/shard_map/ppermute | solution.py:489
  20.8 0.5 collective-permute-start.2
  21.2 0.0 copy-done.1
  21.2 0.0 copy-start.3
  21.3 17.4 %grid_fields.1 = f32[32,3,384]{2,1,0:T(4,128)} custom-call(s32[1]{0:T(128)} %bitcast.11.place_ref, f32[32,2,384]{2,1,0:T(2,128)} %copy-done.1, f32[256,256]{1,0:T(8,128)} %constant.23.clone.fy_table, f32[256,256]{1,0:T(8,128)} %constant.24.clone.fx_table, f32[512,256]{1,0:T(8,128)} %constant.25.clone.ix_table, f32[256,256]{1,0:T(8,128)} %constant.26.clone.iy_table, ...), custom_call_target="tpu_custom_call" | custom-call | flops 8000000000 | bytes 4000000 | tf_op jit(solution)/shard_map/grid_fields/pallas_call | solution.py:273
  38.7 0.0 copy-done
  38.7 0.0 copy-done.3
  38.7 0.6 reshape.8.list_ref
  39.3 4.8 %all-to-all-start.1 = ((f32[32,3,384]{2,1,0:T(4,128)}), f32[32,3,384]{2,1,0:T(4,128)S(1)}, u32[]{:S(2)}, u32[]{:S(2)}) async-start(f32[32,3,384]{2,1,0:T(4,128)} %grid_fields.1), calls=%async_computation.1 | async-start | bytes 393216 | tf_op jit(solution)/shard_map/all_to_all | solution.py:511
  44.1 0.0 collective-permute-done.3.down_ref
  44.1 0.0 copy-start.6
  44.1 0.0 collective-permute-done.2.up_ref
  44.1 0.6 copy-done.6
  44.8 0.0 copy-start.7
  44.8 0.7 copy-done.7
  45.4 35.8 %edge_forces.1 = f32[3,384]{1,0:T(4,128)} custom-call(s32[12288]{0:T(1024)} %reshape.8.list_ref, s32[32,384]{1,0:T(8,128)} %bitcast.21, bf16[384,128]{1,0:T(8,128)(2,1)} %bitcast.17, bf16[3,384]{1,0:T(4,128)(2,1)} %bitcast.24, bf16[3,272,128]{2,1,0:T(8,128)(2,1)} %copy-done, bf16[3,272,128]{2,1,0:T(8,128)(2,1)} %copy-done.7, bf16[3,272,128]{2,1,0:T(8,128)(2,1)} %copy-done.6, ...), custom_call_target="tpu_custom_call" | custom-call | flops 6442450944 | bytes 4000000 | tf_op jit(solution)/shard_map/edge_forces/pallas_call | solution.py:457
  81.3 0.0 copy-start.5
  81.3 0.0 all-to-all-done.1
  81.3 0.1 reduce_sum.9
  81.3 0.6 copy-done.5
  82.0 0.6 copy.19
  (4 shorter events, 0.1 us)
Async XLA Ops:
  2.5 2.4 %copy-start.4 = (f32[2,384]{1,0:T(2,128)S(1)}, f32[2,384]{1,0:T(2,128)}, u32[]{:S(2)}) copy-start(f32[2,384]{1,0:T(2,128)} %get-tuple-element.10) | copy-start | bytes 9220
  2.5 9.2 %collective-permute-start.1 = (bf16[272,128]{1,0:T(8,128)(2,1)}, bf16[272,128]{1,0:T(8,128)(2,1)S(1)}, u32[]{:S(2)}, u32[]{:S(2)}) collective-permute-start(bf16[272,128]{1,0:T(8,128)(2,1)} %get-tuple-element.11), channel_id=1, source_target_pairs={{0,24},{8,0},{16,8},{24,16},{1,25},{9,1},{17,9},{25,17},{2,26},{10... | collective-permute-start | bytes 208904 | tf_op jit(solution)/shard_map/ppermute | solution.py:489
  4.9 6.8 %collective-permute-start = (bf16[272,128]{1,0:T(8,128)(2,1)}, bf16[272,128]{1,0:T(8,128)(2,1)S(1)}, u32[]{:S(2)}, u32[]{:S(2)}) collective-permute-start(bf16[272,128]{1,0:T(8,128)(2,1)} %get-tuple-element.11), channel_id=1, source_target_pairs={{0,8},{8,16},{16,24},{24,0},{1,9},{9,17},{17,25},{25,1},{2,10},{10... | collective-permute-start | bytes 208904 | tf_op jit(solution)/shard_map/ppermute | solution.py:489
  5.5 6.2 %copy-start.2 = (bf16[272,128]{1,0:T(8,128)(2,1)S(1)}, bf16[272,128]{1,0:T(8,128)(2,1)}, u32[]{:S(2)}) copy-start(bf16[272,128]{1,0:T(8,128)(2,1)} %get-tuple-element.11) | copy-start | bytes 208900
  5.5 13.7 %all-to-all-start = ((f32[32,2,384]{2,1,0:T(2,128)}), f32[32,2,384]{2,1,0:T(2,128)S(1)}, u32[]{:S(2)}, u32[]{:S(2)}) async-start(f32[32,2,384]{2,1,0:T(2,128)} %broadcast_in_dim.25), calls=%async_computation | async-start | bytes 196608 | tf_op jit(solution)/shard_map/all_to_all | solution.py:503
  11.8 26.9 %copy-start = (bf16[3,272,128]{2,1,0:T(8,128)(2,1)}, bf16[3,272,128]{2,1,0:T(8,128)(2,1)S(1)}, u32[]{:S(2)}) copy-start(bf16[3,272,128]{2,1,0:T(8,128)(2,1)S(1)} %pad_maximum_fusion.mid_ref) | copy-start | bytes 626692
  19.2 2.0 %copy-start.1 = (f32[32,2,384]{2,1,0:T(2,128)}, f32[32,2,384]{2,1,0:T(2,128)S(1)}, u32[]{:S(2)}) copy-start(f32[32,2,384]{2,1,0:T(2,128)S(1)} %all-to-all-done.qc_ref) | copy-start | bytes 294916
  19.2 24.9 %collective-permute-start.3 = (bf16[3,272,128]{2,1,0:T(8,128)(2,1)S(1)}, bf16[3,272,128]{2,1,0:T(8,128)(2,1)S(1)}, u32[]{:S(2)}, u32[]{:S(2)}) collective-permute-start(bf16[3,272,128]{2,1,0:T(8,128)(2,1)S(1)} %pad_maximum_fusion.mid_ref), channel_id=1, source_target_pairs={{0,7},{1,0},{2,1},{3,2},{4,3},{5,4},{6,5},{7,6},{8,15},{9,8},{10,9... | collective-permute-start | bytes 626696 | tf_op jit(solution)/shard_map/ppermute | solution.py:489
  20.8 23.3 %collective-permute-start.2 = (bf16[3,272,128]{2,1,0:T(8,128)(2,1)S(1)}, bf16[3,272,128]{2,1,0:T(8,128)(2,1)S(1)}, u32[]{:S(2)}, u32[]{:S(2)}) collective-permute-start(bf16[3,272,128]{2,1,0:T(8,128)(2,1)S(1)} %pad_maximum_fusion.mid_ref), channel_id=1, source_target_pairs={{0,1},{1,2},{2,3},{3,4},{4,5},{5,6},{6,7},{7,0},{8,9},{9,10},{10,1... | collective-permute-start | bytes 626696 | tf_op jit(solution)/shard_map/ppermute | solution.py:489
  21.2 17.4 %copy-start.3 = (s32[1,1,384,32]{2,3,1,0:T(8,128)S(1)}, s32[1,1,384,32]{2,3,1,0:T(8,128)}, u32[]{:S(2)}) copy-start(s32[1,1,384,32]{2,3,1,0:T(8,128)} %param.22) | copy-start | bytes 147460
  39.3 42.0 %all-to-all-start.1 = ((f32[32,3,384]{2,1,0:T(4,128)}), f32[32,3,384]{2,1,0:T(4,128)S(1)}, u32[]{:S(2)}, u32[]{:S(2)}) async-start(f32[32,3,384]{2,1,0:T(4,128)} %grid_fields.1), calls=%async_computation.1 | async-start | bytes 393216 | tf_op jit(solution)/shard_map/all_to_all | solution.py:511
  44.1 0.7 copy-start.6
  44.8 0.7 copy-start.7
  81.3 0.7 copy-start.5

commit v6 on v4

--- a/solution.py
+++ b/solution.py
@@ -21,6 +21,7 @@
 ROWS = 32
 CHUNK_ATOMS = 16
 PIECES = 4
+TILES = 2
 HIGHEST = lax.Precision.HIGHEST
 F32 = jnp.float32
 BF16 = jnp.bfloat16
@@ -300,7 +301,7 @@
     basis_count = w_radial_ref.shape[0]
     spacing = CUTOFF_SQ / (basis_count - 1)
     latent = w_expand_ref.shape[1]
-    width = latent // PIECES
+    width = latent // TILES
     slots = per_atom // PIECES
     w_half[...] = w_expand_ref[...] * 0.5
 
@@ -308,8 +309,9 @@
         count = rows.shape[0]
         projected = jnp.dot(rows, w_pair_ref[...], preferred_element_type=F32)
         projected = projected.astype(BF16).astype(F32)
-        table[pl.ds(start, count), :] = projected[:, :channels] * 0.5
-        table[pl.ds(slots_all + start, count), :] = projected[:, channels:]
+        rows_of = table.reshape(slots_all * 8, LANES)
+        rows_of[pl.ds(start * 8, count, stride=8), :] = projected[:, :channels] * 0.5
+        rows_of[pl.ds(start * 8 + 1, count, stride=8), :] = projected[:, channels:]
         row = lax.broadcasted_iota(jnp.int32, (8, LANES), 0)
         offset = jnp.where(row == 0, shift[0], jnp.where(row == 1, shift[1], 0.0))
         places[start // LANES] = coords + offset
@@ -374,10 +376,10 @@
 
     def gather(index, near, part):
         for k in range(part * slots, (part + 1) * slots):
-            for a in range(CHUNK_ATOMS):
-                j = list_ref[k * atoms + index * CHUNK_ATOMS + a]
-                e = k * CHUNK_ATOMS + a
-                near[pl.ds(e, 2, stride=chunk), :] = table[pl.ds(j, 2, stride=slots_all), :]
+            start = k * atoms + index * CHUNK_ATOMS
+            loaded = [table[list_ref[start + a]] for a in range(CHUNK_ATOMS)]
+            for a, tile in enumerate(loaded):
+                near[pl.ds(k * CHUNK_ATOMS + a, 2, stride=chunk), :] = tile[:2]
 
     def enter(index, near, edge_in, part):
         first = pl.multiple_of(index * CHUNK_ATOMS, 8)
@@ -411,8 +413,9 @@
         for part in range(PIECES):
             gather(later, nears[2], part)
             enter(after, nears[1], edges[1], part)
-            term = network(edges[0], part)
-            mixed = term if mixed is None else mixed + term
+            if part % (PIECES // TILES) == PIECES // TILES - 1:
+                term = network(edges[0], part // (PIECES // TILES))
+                mixed = term if mixed is None else mixed + term
         collect(index, mixed, nears[0])
 
     nears = (near_a, near_b, near_c)
@@ -457,7 +460,7 @@
         out_specs=vmem,
         out_shape=jax.ShapeDtypeStruct((3, atoms), F32),
         scratch_shapes=[
-            pltpu.VMEM((2 * slots_all, LANES), F32),
+            pltpu.VMEM((slots_all, 8, LANES), F32),
             pltpu.VMEM((slots_all // LANES, 8, LANES), F32),
         ]
         + [pltpu.VMEM((2 * chunk, LANES), F32)] * 3

time: 82.7 us -> 80 us (0.967)
  Pallas kernels: 54.9 us -> 52.3 us
    pallas_call x1, Pallas kernels: 35.6 us -> 33 us  [edge_forces(): pl.pallas_call(edge_kernel, in_specs=[pl.BlockSpec(memory_space=pltpu.SME...]
  transfers between devices with their start and end apart: 6 -> 6, of which waited for: 1 -> 1; matrix products, arithmetic and copies ran while one was open for 2% -> 2% of each run, Pallas kernels for 64% -> 63%
where the time goes in v6:
time: 80 us; the launch traced here: 79.6 us
  Pallas kernels  52.3 us (65%)
  starting transfers between devices  15.1 us (19%)
  waiting for transfers between devices  7.46 us (9%)
  local copies, waits for them, and re-layouts  3.88 us (5%)
    pallas_call x1, Pallas kernels, edge_forces(): pl.pallas_call(edge_kernel, in_specs=[pl.BlockSpec(memory_space=pltpu.SME...  33 us
    pallas_call x1, Pallas kernels, grid_fields(): pl.pallas_call(functools.partial(grid_kernel, cycle_x, cycle_y), in_specs...  17.4 us
    all_to_all x1, waiting for transfers between devices, shards(): lax.all_to_all(spread, ('dx', 'dy'), split_axis=0, concat_axis=0, tiled=T...  7.44 us
    all_to_all x1, starting transfers between devices, shards(): lax.all_to_all(spread, ('dx', 'dy'), split_axis=0, concat_axis=0, tiled=T...  6.1 us
    all_to_all x1, starting transfers between devices, shards(): lax.all_to_all(partial, ('dx', 'dy'), split_axis=0, concat_axis=0, tiled=...  4.6 us
    ppermute x4, starting transfers between devices, ring(): lax.ppermute(array, axis, [(i, (i + step) % size) for i in range(size)])  4.41 us
    unnamed x16, local copies, waits for them, and re-layouts  1.98 us
    pallas_call x1, Pallas kernels, prepare(): pl.pallas_call(prepare_kernel, in_specs=[pl.BlockSpec(memory_space=pltpu....  1.84 us
  transfers between devices with their start and end apart: 6, of which 1 were waited for; matrix products, arithmetic and copies ran while one was open for 2% of the time, Pallas kernels for 63%

profile of v6, /device:TPU:0, one launch (start us, length us, event | category | flops | bytes accessed | tf_op | source)
XLA Modules:
  0.0 79.6 jit_solution(13099708054076073074)
XLA Ops:
  0.7 1.8 %prepare.1 = (bf16[272,128]{1,0:T(8,128)(2,1)}, f32[2,384]{1,0:T(2,128)}) custom-call(s32[1,1]{1,0:T(1,128)} %copy.20.count_ref, bf16[384,128]{1,0:T(8,128)(2,1)} %bitcast.16, bf16[3,384]{1,0:T(4,128)(2,1)} %bitcast.23, s32[1,256]{1,0:T(1,128)} %bitcast.26, s32[1,384]{1,0:T(1,128)} %bitcast.25, bf16[1,128]{1,0:T(2,128)(2,1)} %bitcast.27), custom_call_target="tpu_custom_call" | custom-call | tf_op jit(solution)/shard_map/prepare/pallas_call | solution.py:63
  2.5 0.0 copy-start.4
  2.5 2.4 %collective-permute-start.1 = (bf16[272,128]{1,0:T(8,128)(2,1)}, bf16[272,128]{1,0:T(8,128)(2,1)S(1)}, u32[]{:S(2)}, u32[]{:S(2)}) collective-permute-start(bf16[272,128]{1,0:T(8,128)(2,1)} %get-tuple-element.11), channel_id=1, source_target_pairs={{0,24},{8,0},{16,8},{24,16},{1,25},{9,1},{17,9},{25,17},{2,26},{10... | collective-permute-start | bytes 208904 | tf_op jit(solution)/shard_map/ppermute | solution.py:489
  4.9 0.0 collective-permute-start
  4.9 0.0 copy-done.4
  4.9 0.7 broadcast_in_dim.25
  5.5 0.0 copy-start.2
  5.5 6.1 %all-to-all-start = ((f32[32,2,384]{2,1,0:T(2,128)}), f32[32,2,384]{2,1,0:T(2,128)S(1)}, u32[]{:S(2)}, u32[]{:S(2)}) async-start(f32[32,2,384]{2,1,0:T(2,128)} %broadcast_in_dim.25), calls=%async_computation | async-start | bytes 196608 | tf_op jit(solution)/shard_map/all_to_all | solution.py:503
  11.7 0.0 collective-permute-done.1
  11.7 0.0 collective-permute-done
  11.7 0.0 copy-done.2
  11.8 0.0 copy-start
  11.8 7.4 %all-to-all-done.qc_ref = f32[32,2,384]{2,1,0:T(2,128)S(1)} async-done(((f32[32,2,384]{2,1,0:T(2,128)}), f32[32,2,384]{2,1,0:T(2,128)S(1)}, u32[]{:S(2)}, u32[]{:S(2)}) %all-to-all-start) | async-done | bytes 98336 | tf_op jit(solution)/shard_map/all_to_all | solution.py:503
  19.2 0.0 copy-start.1
  19.2 1.5 %collective-permute-start.3 = (bf16[3,272,128]{2,1,0:T(8,128)(2,1)S(1)}, bf16[3,272,128]{2,1,0:T(8,128)(2,1)S(1)}, u32[]{:S(2)}, u32[]{:S(2)}) collective-permute-start(bf16[3,272,128]{2,1,0:T(8,128)(2,1)S(1)} %pad_maximum_fusion.mid_ref), channel_id=1, source_target_pairs={{0,7},{1,0},{2,1},{3,2},{4,3},{5,4},{6,5},{7,6},{8,15},{9,8},{10,9... | collective-permute-start | bytes 626696 | tf_op jit(solution)/shard_map/ppermute | solution.py:489
  20.8 0.5 collective-permute-start.2
  21.2 0.0 copy-done.1
  21.2 0.0 copy-start.3
  21.2 17.4 %grid_fields.1 = f32[32,3,384]{2,1,0:T(4,128)} custom-call(s32[1]{0:T(128)} %bitcast.11.place_ref, f32[32,2,384]{2,1,0:T(2,128)} %copy-done.1, f32[256,256]{1,0:T(8,128)} %constant.23.clone.fy_table, f32[256,256]{1,0:T(8,128)} %constant.24.clone.fx_table, f32[512,256]{1,0:T(8,128)} %constant.25.clone.ix_table, f32[256,256]{1,0:T(8,128)} %constant.26.clone.iy_table, ...), custom_call_target="tpu_custom_call" | custom-call | flops 8000000000 | bytes 4000000 | tf_op jit(solution)/shard_map/grid_fields/pallas_call | solution.py:274
  38.7 0.0 copy-done
  38.7 0.0 copy-done.3
  38.7 0.6 reshape.8.list_ref
  39.3 4.6 %all-to-all-start.1 = ((f32[32,3,384]{2,1,0:T(4,128)}), f32[32,3,384]{2,1,0:T(4,128)S(1)}, u32[]{:S(2)}, u32[]{:S(2)}) async-start(f32[32,3,384]{2,1,0:T(4,128)} %grid_fields.1), calls=%async_computation.1 | async-start | bytes 393216 | tf_op jit(solution)/shard_map/all_to_all | solution.py:511
  43.9 0.0 collective-permute-done.3.down_ref
  43.9 0.0 copy-start.6
  43.9 0.0 collective-permute-done.2.up_ref
  43.9 0.6 copy-done.6
  44.6 0.0 copy-start.7
  44.6 0.7 copy-done.7
  45.3 33.0 %edge_forces.1 = f32[3,384]{1,0:T(4,128)} custom-call(s32[12288]{0:T(1024)} %reshape.8.list_ref, s32[32,384]{1,0:T(8,128)} %bitcast.21, bf16[384,128]{1,0:T(8,128)(2,1)} %bitcast.17, bf16[3,384]{1,0:T(4,128)(2,1)} %bitcast.24, bf16[3,272,128]{2,1,0:T(8,128)(2,1)} %copy-done, bf16[3,272,128]{2,1,0:T(8,128)(2,1)} %copy-done.7, bf16[3,272,128]{2,1,0:T(8,128)(2,1)} %copy-done.6, ...), custom_call_target="tpu_custom_call" | custom-call | flops 6442450944 | bytes 4000000 | tf_op jit(solution)/shard_map/edge_forces/pallas_call | solution.py:457
  78.3 0.0 copy-start.5
  78.3 0.0 all-to-all-done.1
  78.3 0.1 reduce_sum.9
  78.3 0.6 copy-done.5
  79.0 0.6 copy.19
  (4 shorter events, 0.1 us)
Async XLA Ops:
  2.5 2.4 %copy-start.4 = (f32[2,384]{1,0:T(2,128)S(1)}, f32[2,384]{1,0:T(2,128)}, u32[]{:S(2)}) copy-start(f32[2,384]{1,0:T(2,128)} %get-tuple-element.10) | copy-start | bytes 9220
  2.5 9.2 %collective-permute-start.1 = (bf16[272,128]{1,0:T(8,128)(2,1)}, bf16[272,128]{1,0:T(8,128)(2,1)S(1)}, u32[]{:S(2)}, u32[]{:S(2)}) collective-permute-start(bf16[272,128]{1,0:T(8,128)(2,1)} %get-tuple-element.11), channel_id=1, source_target_pairs={{0,24},{8,0},{16,8},{24,16},{1,25},{9,1},{17,9},{25,17},{2,26},{10... | collective-permute-start | bytes 208904 | tf_op jit(solution)/shard_map/ppermute | solution.py:489
  4.9 6.8 %collective-permute-start = (bf16[272,128]{1,0:T(8,128)(2,1)}, bf16[272,128]{1,0:T(8,128)(2,1)S(1)}, u32[]{:S(2)}, u32[]{:S(2)}) collective-permute-start(bf16[272,128]{1,0:T(8,128)(2,1)} %get-tuple-element.11), channel_id=1, source_target_pairs={{0,8},{8,16},{16,24},{24,0},{1,9},{9,17},{17,25},{25,1},{2,10},{10... | collective-permute-start | bytes 208904 | tf_op jit(solution)/shard_map/ppermute | solution.py:489
  5.5 6.2 %copy-start.2 = (bf16[272,128]{1,0:T(8,128)(2,1)S(1)}, bf16[272,128]{1,0:T(8,128)(2,1)}, u32[]{:S(2)}) copy-start(bf16[272,128]{1,0:T(8,128)(2,1)} %get-tuple-element.11) | copy-start | bytes 208900
  5.5 13.7 %all-to-all-start = ((f32[32,2,384]{2,1,0:T(2,128)}), f32[32,2,384]{2,1,0:T(2,128)S(1)}, u32[]{:S(2)}, u32[]{:S(2)}) async-start(f32[32,2,384]{2,1,0:T(2,128)} %broadcast_in_dim.25), calls=%async_computation | async-start | bytes 196608 | tf_op jit(solution)/shard_map/all_to_all | solution.py:503
  11.8 26.9 %copy-start = (bf16[3,272,128]{2,1,0:T(8,128)(2,1)}, bf16[3,272,128]{2,1,0:T(8,128)(2,1)S(1)}, u32[]{:S(2)}) copy-start(bf16[3,272,128]{2,1,0:T(8,128)(2,1)S(1)} %pad_maximum_fusion.mid_ref) | copy-start | bytes 626692
  19.2 2.0 %copy-start.1 = (f32[32,2,384]{2,1,0:T(2,128)}, f32[32,2,384]{2,1,0:T(2,128)S(1)}, u32[]{:S(2)}) copy-start(f32[32,2,384]{2,1,0:T(2,128)S(1)} %all-to-all-done.qc_ref) | copy-start | bytes 294916
  19.2 24.7 %collective-permute-start.3 = (bf16[3,272,128]{2,1,0:T(8,128)(2,1)S(1)}, bf16[3,272,128]{2,1,0:T(8,128)(2,1)S(1)}, u32[]{:S(2)}, u32[]{:S(2)}) collective-permute-start(bf16[3,272,128]{2,1,0:T(8,128)(2,1)S(1)} %pad_maximum_fusion.mid_ref), channel_id=1, source_target_pairs={{0,7},{1,0},{2,1},{3,2},{4,3},{5,4},{6,5},{7,6},{8,15},{9,8},{10,9... | collective-permute-start | bytes 626696 | tf_op jit(solution)/shard_map/ppermute | solution.py:489
  20.8 23.2 %collective-permute-start.2 = (bf16[3,272,128]{2,1,0:T(8,128)(2,1)S(1)}, bf16[3,272,128]{2,1,0:T(8,128)(2,1)S(1)}, u32[]{:S(2)}, u32[]{:S(2)}) collective-permute-start(bf16[3,272,128]{2,1,0:T(8,128)(2,1)S(1)} %pad_maximum_fusion.mid_ref), channel_id=1, source_target_pairs={{0,1},{1,2},{2,3},{3,4},{4,5},{5,6},{6,7},{7,0},{8,9},{9,10},{10,1... | collective-permute-start | bytes 626696 | tf_op jit(solution)/shard_map/ppermute | solution.py:489
  21.2 17.4 %copy-start.3 = (s32[1,1,384,32]{2,3,1,0:T(8,128)S(1)}, s32[1,1,384,32]{2,3,1,0:T(8,128)}, u32[]{:S(2)}) copy-start(s32[1,1,384,32]{2,3,1,0:T(8,128)} %param.22) | copy-start | bytes 147460
  39.3 39.0 %all-to-all-start.1 = ((f32[32,3,384]{2,1,0:T(4,128)}), f32[32,3,384]{2,1,0:T(4,128)S(1)}, u32[]{:S(2)}, u32[]{:S(2)}) async-start(f32[32,3,384]{2,1,0:T(4,128)} %grid_fields.1), calls=%async_computation.1 | async-start | bytes 393216 | tf_op jit(solution)/shard_map/all_to_all | solution.py:511
  43.9 0.7 copy-start.6
  44.6 0.7 copy-start.7
  78.3 0.7 copy-start.5

commit v7 on v6

--- a/solution.py
+++ b/solution.py
@@ -19,6 +19,7 @@
 LANES = 128
 EXTRA = 16
 ROWS = 32
+GROUPS = LANES // ROWS
 CHUNK_ATOMS = 16
 PIECES = 4
 TILES = 2
@@ -52,12 +53,11 @@
     weights = jnp.broadcast_to(wq_ref[...].astype(F32), (16, LANES)).astype(BF16)
     charge = contract_last(weights, feat_ref[...])[:1]
     live = lax.broadcasted_iota(jnp.int32, (1, atoms), 1) < count_ref[0, 0]
-    qc_ref[...] = jnp.concatenate(
-        [jnp.where(live, charge, 0.0), cell_ref[...].astype(F32)], axis=0
-    )
-
-
-def prepare(count, feat, pos, exports, cells, w_charge):
+    both = jnp.concatenate([jnp.where(live, charge, 0.0), cell_ref[...].astype(F32)], axis=0)
+    qc_ref[...] = jnp.broadcast_to(both[None], qc_ref.shape)
+
+
+def prepare(devices, count, feat, pos, exports, cells, w_charge):
     atoms, ghosts = (feat.shape[0], exports.shape[0])
     vmem = pl.BlockSpec(memory_space=pltpu.VMEM)
     return pl.pallas_call(
@@ -66,7 +66,7 @@
         out_specs=[vmem, vmem],
         out_shape=[
             jax.ShapeDtypeStruct((ghosts + EXTRA, feat.shape[1]), BF16),
-            jax.ShapeDtypeStruct((2, atoms), F32),
+            jax.ShapeDtypeStruct((devices, 2, atoms), F32),
         ],
         name="prepare",
     )(count, feat, pos, exports[None], cells[None], w_charge[None])
@@ -86,8 +86,11 @@
     return (basis, (weight * basis).T, (weight * slope).T)
 
 
-def block_table(table, copies):
-    return np.kron(np.eye(copies), table).astype(np.float32)
+def thirds(table):
+    whole = table.astype(np.float32)
+    high = whole.astype(BF16).astype(np.float32)
+    low = (whole - high).astype(BF16).astype(np.float32)
+    return np.concatenate([high, high, low], axis=1)
 
 
 def sine_half(t):
@@ -102,22 +105,15 @@
 
 
 def grid_kernel(
-    cycle_x, cycle_y, place_ref, qc_ref, fy_table, fx_table, ix_table, iy_table, dy_table, out_ref,
-    buf_a, buf_b, buf_c, buf_d, buf_e, trig_ref, fy_ref, fx_ref, ix_ref, iy_ref, dy_ref,
+    cycle_x, cycle_y, place_ref, qc_ref, fy_ref, fx_ref, ix_ref, iy_ref, out_ref,
+    buf_a, buf_b, buf_c, buf_d, buf_e, trig_ref,
 ):
-    tables = (fy_table, fx_table, ix_table, iy_table, dy_table)
-    for whole, halves in zip(tables, (fy_ref, fx_ref, ix_ref, iy_ref, dy_ref)):
-        high = whole[...].astype(BF16)
-        halves[:, : whole.shape[1]] = high
-        halves[:, whole.shape[1] :] = (whole[...] - high.astype(F32)).astype(BF16)
     mesh_x, mesh_y, mesh_z = (GRID_X * cycle_x, GRID_Y * cycle_y, GRID_Z)
     devices = cycle_x * cycle_y
     modes = mesh_z // 2 // devices
     coefs = 2 * modes
     first = place_ref[0] * modes
     columns = GRID_X * GRID_Y
-    group_y = max(1, 256 // mesh_y)
-    group_x = max(1, 256 // mesh_x)
     atoms = qc_ref.shape[2]
 
     row = lax.broadcasted_iota(jnp.int32, (ROWS, 1), 0) % coefs
@@ -152,49 +148,56 @@
     lax.fori_loop(0, devices, spread, 0, unroll=4)
 
     lane = lax.broadcasted_iota(jnp.int32, (1, LANES), 1)
-    low_half = lane >= LANES // 2
-
-    def apply(table_ref, data):
-        high = data.astype(BF16).astype(F32)
-        mixed = jnp.where(low_half, data - high, high).astype(BF16)
-        both = jnp.concatenate([mixed, mixed], axis=0)
-        result = jnp.dot(table_ref[...], both, preferred_element_type=F32)
-        return result + pltpu.roll(result, LANES // 2, 1)
-
-    def forward_y(step, carry):
-        parts = []
-        for i in range(group_y):
-            place = step * group_y + i
+    lane_group = lane // ROWS
+
+    def pack(copied):
+        wide = copied[0]
+        for g in range(1, GROUPS):
+            wide = jnp.where(lane_group == g, copied[g], wide)
+        return wide
+
+    def unpack(wide):
+        turned = [wide] + [pltpu.roll(wide, g * ROWS, 1) for g in range(1, GROUPS)]
+        copied = []
+        for i in range(GROUPS):
+            copied.append(pack([turned[(g - i) % GROUPS] for g in range(GROUPS)]))
+        return copied
+
+    def apply(table_ref, wide):
+        high = wide.astype(BF16)
+        low = (wide - high.astype(F32)).astype(BF16)
+        data = jnp.concatenate([high, low, high], axis=0)
+        return jnp.dot(table_ref[...].astype(BF16), data, preferred_element_type=F32)
+
+    for first_x in range(0, mesh_x, GROUPS):
+        copied = []
+        for place in range(first_x, first_x + GROUPS):
+            rows = []
             for sy in range(cycle_y):
                 start = ((place // GRID_X) * cycle_y + sy) * columns + (place % GRID_X) * GRID_Y
-                parts.append(buf_a[pl.ds(pl.multiple_of(start, 8), GRID_Y), :])
-        size = group_y * mesh_y
-        start = pl.multiple_of(step * size, 8)
-        buf_b[pl.ds(start, size), :] = apply(fy_ref, jnp.concatenate(parts, axis=0))
-        return carry
-
-    lax.fori_loop(0, mesh_x // group_y, forward_y, 0, unroll=2)
-
-    size_x = group_x * mesh_x
-    lane_coef = lane % coefs
+                rows.append(buf_a[pl.ds(start, GRID_Y), :])
+            copied.append(jnp.concatenate(rows, axis=0))
+        for i, part in enumerate(unpack(apply(fy_ref, pack(copied)))):
+            buf_b[pl.ds((first_x + i) * mesh_y, mesh_y), :] = part
+
+    lane_coef = lane % ROWS % coefs
     lane_mode = first + lane_coef % modes
     lane_sine = lane_coef >= modes
     lane_freq = jnp.where(lane_sine & (lane_mode == 0), mesh_z // 2, lane_mode)
     wave_z = lane_freq.astype(F32) * (2.0 * math.pi / mesh_z)
     lane_weight = jnp.where(lane_mode == 0, 1.0, 2.0) / mesh_z
     slope_z = jnp.where(lane_mode == 0, 0.0, wave_z) * jnp.where(lane_sine, 1.0, -1.0)
-    index_x = lax.broadcasted_iota(jnp.int32, (size_x, 1), 0)
-    freq_x = index_x % mesh_x
+    freq_x = lax.broadcasted_iota(jnp.int32, (mesh_x, 1), 0)
     freq_x = jnp.where(freq_x <= mesh_x // 2, freq_x, freq_x - mesh_x // 2)
     wave_x = freq_x.astype(F32) * (2.0 * math.pi / mesh_x)
     near = wave_x * wave_x + wave_z * wave_z
 
-    def middle(step, carry):
-        parts = []
-        for i in range(group_x):
-            parts.append(buf_b[pl.ds(step * group_x + i, mesh_x, stride=mesh_y), :])
-        spectrum = apply(fx_ref, jnp.concatenate(parts, axis=0))
-        freq_y = step * group_x + index_x // mesh_x
+    for first_y in range(0, mesh_y, GROUPS):
+        copied = [
+            buf_b[pl.ds(first_y + i, mesh_x, stride=mesh_y), :] for i in range(GROUPS)
+        ]
+        spectrum = apply(fx_ref, pack(copied))
+        freq_y = first_y + lane_group
         freq_y = jnp.where(freq_y <= mesh_y // 2, freq_y, freq_y - mesh_y // 2)
         wave_y = freq_y.astype(F32) * (2.0 * math.pi / mesh_y)
         wave_sq = near + wave_y * wave_y
@@ -202,29 +205,28 @@
         green = jnp.exp(-0.5 * SMEARING * SMEARING * wave_sq) / jnp.where(zero, 1.0, wave_sq)
         green = jnp.where(zero, 0.0, 4.0 * math.pi * green)
         both = apply(ix_ref, spectrum * (green * lane_weight))
-        start = pl.multiple_of(step * size_x, 8)
-        buf_a[pl.ds(start, size_x), :] = both[:size_x]
-        buf_c[pl.ds(start, size_x), :] = both[size_x:]
-        return carry
-
-    lax.fori_loop(0, mesh_y // group_x, middle, 0, unroll=2)
-
-    def backward_y(step, carry):
-        plain, sloped = ([], [])
-        for i in range(group_y):
-            place = step * group_y + i
-            plain.append(buf_a[pl.ds(place, mesh_y, stride=mesh_x), :])
-            sloped.append(buf_c[pl.ds(place, mesh_y, stride=mesh_x), :])
-        plain = jnp.concatenate(plain, axis=0)
-        size = group_y * mesh_y
-        start = pl.multiple_of(step * size, 8)
-        potential = apply(iy_ref, plain)
-        buf_b[pl.ds(start, size), :] = apply(iy_ref, jnp.concatenate(sloped, axis=0))
-        buf_d[pl.ds(start, size), :] = apply(dy_ref, plain)
-        buf_e[pl.ds(start, size), :] = pltpu.roll(potential, modes, 1) * slope_z
-        return carry
-
-    lax.fori_loop(0, mesh_x // group_y, backward_y, 0, unroll=2)
+        for i, part in enumerate(unpack(both)):
+            rows = pl.ds((first_y + i) * mesh_x, mesh_x)
+            buf_a[rows, :] = part[:mesh_x]
+            buf_c[rows, :] = part[mesh_x:]
+
+    for first_x in range(0, mesh_x, GROUPS):
+        plain, sloped = (
+            pack([buf[pl.ds(first_x + i, mesh_y, stride=mesh_x), :] for i in range(GROUPS)])
+            for buf in (buf_a, buf_c)
+        )
+        both = apply(iy_ref, plain)
+        along_x = apply(iy_ref.at[pl.ds(0, mesh_y), :], sloped)
+        potential = both[:mesh_y]
+        partner = jnp.where(
+            lane % ROWS >= modes,
+            pltpu.roll(potential, modes, 1),
+            pltpu.roll(potential, LANES - modes, 1),
+        )
+        fields = (along_x, both[mesh_y:], partner * slope_z)
+        for buf, wide in zip((buf_b, buf_d, buf_e), fields):
+            for i, part in enumerate(unpack(wide)):
+                buf[pl.ds((first_x + i) * mesh_y, mesh_y), :] = part
 
     use_low = (lane // ROWS) == 1
     use_none = (lane % ROWS) >= coefs
@@ -258,27 +260,23 @@
 def grid_fields(place, gathered, cycle_x, cycle_y):
     mesh_x, mesh_y = (GRID_X * cycle_x, GRID_Y * cycle_y)
     devices, _, atoms = gathered.shape
-    group_y = max(1, 256 // mesh_y)
-    group_x = max(1, 256 // mesh_x)
     ax, bx, cx = real_tables(mesh_x)
     ay, by, cy = real_tables(mesh_y)
     tables = [
-        block_table(ay, group_y),
-        block_table(ax, group_x),
-        np.concatenate([block_table(bx, group_x), block_table(cx, group_x)], axis=0),
-        block_table(by, group_y),
-        block_table(cy, group_y),
+        thirds(ay),
+        thirds(ax),
+        np.concatenate([thirds(bx), thirds(cx)], axis=0),
+        np.concatenate([thirds(by), thirds(cy)], axis=0),
     ]
     plane = pltpu.VMEM((mesh_x * mesh_y, LANES), F32)
     vmem = pl.BlockSpec(memory_space=pltpu.VMEM)
     return pl.pallas_call(
         functools.partial(grid_kernel, cycle_x, cycle_y),
-        in_specs=[pl.BlockSpec(memory_space=pltpu.SMEM)] + [vmem] * 6,
+        in_specs=[pl.BlockSpec(memory_space=pltpu.SMEM)] + [vmem] * 5,
         out_specs=vmem,
         out_shape=jax.ShapeDtypeStruct((devices, 3, atoms), F32),
         scratch_shapes=[plane] * 5
-        + [pltpu.VMEM((devices, 2 * ROWS, atoms), BF16)]
-        + [pltpu.VMEM((t.shape[0], 2 * t.shape[1]), BF16) for t in tables],
+        + [pltpu.VMEM((devices, 2 * ROWS, atoms), BF16)],
         compiler_params=pltpu.CompilerParams(vmem_limit_bytes=60 << 20),
         cost_estimate=pl.CostEstimate(
             flops=8_000_000_000, bytes_accessed=4_000_000, transcendentals=100_000
@@ -496,10 +494,9 @@
     feat = features[0, 0]
     pos = positions[0, 0]
     cycle_x, cycle_y = (lax.axis_size("dx"), lax.axis_size("dy"))
-    exported, charge_cell = prepare(
-        atom_count, feat, pos, ghost_index[0, 0], cell_index[0, 0], w_charge
+    exported, spread = prepare(
+        cycle_x * cycle_y, atom_count, feat, pos, ghost_index[0, 0], cell_index[0, 0], w_charge
     )
-    spread = jnp.broadcast_to(charge_cell, (cycle_x * cycle_y,) + charge_cell.shape)
     gathered = lax.all_to_all(spread, ("dx", "dy"), split_axis=0, concat_axis=0, tiled=True)
     mid = jnp.stack([ring(exported, "dx", 1), exported, ring(exported, "dx", -1)])
     lists = neighbour_list[0, 0].T
@@ -514,7 +511,7 @@
         w_contract, w_final,
     )
     field = jnp.sum(received, axis=0)
-    total = short + charge_cell[:1] * field
+    total = short + spread[0, :1] * field
     live = lax.broadcasted_iota(jnp.int32, (1, feat.shape[0]), 1) < atom_count[0, 0]
     return jnp.where(live, total, jnp.zeros_like(total))[None, None]
 

time: 80 us -> 73.5 us (0.919)
  Pallas kernels: 52.3 us -> 46.2 us
    pallas_call x1, Pallas kernels: 17.4 us -> 11.3 us  [grid_fields(): pl.pallas_call(functools.partial(grid_kernel, cycle_x, cycle_y), in_specs...]
    unnamed x16 -> x14, local copies, waits for them, and re-layouts: 1.98 us -> 1.98 us
  transfers between devices with their start and end apart: 6 -> 6, of which waited for: 1 -> 1; matrix products, arithmetic and copies ran while one was open for 2% -> 2% of each run, Pallas kernels for 63% -> 61%
where the time goes in v7:
time: 73.5 us; the launch traced here: 73.1 us
  Pallas kernels  46.2 us (63%)
  starting transfers between devices  15.3 us (21%)
  waiting for transfers between devices  6.79 us (9%)
  local copies, waits for them, and re-layouts  3.88 us (5%)
  between operations  0.76 us (1%)
    pallas_call x1, Pallas kernels, edge_forces(): pl.pallas_call(edge_kernel, in_specs=[pl.BlockSpec(memory_space=pltpu.SME...  33 us
    pallas_call x1, Pallas kernels, grid_fields(): pl.pallas_call(functools.partial(grid_kernel, cycle_x, cycle_y), in_specs...  11.3 us
    all_to_all x1, waiting for transfers between devices, shards(): lax.all_to_all(spread, ('dx', 'dy'), split_axis=0, concat_axis=0, tiled=T...  6.78 us
    all_to_all x1, starting transfers between devices, shards(): lax.all_to_all(spread, ('dx', 'dy'), split_axis=0, concat_axis=0, tiled=T...  6.1 us
    all_to_all x1, starting transfers between devices, shards(): lax.all_to_all(partial, ('dx', 'dy'), split_axis=0, concat_axis=0, tiled=...  4.78 us
    ppermute x4, starting transfers between devices, ring(): lax.ppermute(array, axis, [(i, (i + step) % size) for i in range(size)])  4.41 us
    unnamed x14, local copies, waits for them, and re-layouts  1.98 us
    pallas_call x1, Pallas kernels, prepare(): pl.pallas_call(prepare_kernel, in_specs=[pl.BlockSpec(memory_space=pltpu....  1.87 us
  transfers between devices with their start and end apart: 6, of which 1 were waited for; matrix products, arithmetic and copies ran while one was open for 2% of the time, Pallas kernels for 61%

profile of v7, /device:TPU:0, one launch (start us, length us, event | category | flops | bytes accessed | tf_op | source)
XLA Modules:
  0.0 73.1 jit_solution(5634887287251719180)
XLA Ops:
  0.7 1.9 %prepare.1 = (bf16[272,128]{1,0:T(8,128)(2,1)}, f32[32,2,384]{2,1,0:T(2,128)}) custom-call(s32[1,1]{1,0:T(1,128)} %copy.19.count_ref, bf16[384,128]{1,0:T(8,128)(2,1)} %bitcast.16, bf16[3,384]{1,0:T(4,128)(2,1)} %bitcast.23, s32[1,256]{1,0:T(1,128)} %bitcast.26, s32[1,384]{1,0:T(1,128)} %bitcast.25, bf16[1,128]{1,0:T(2,128)(2,1)} %bitcast.27), custom_call_target="tpu_custom_call" | custom-call | tf_op jit(solution)/shard_map/prepare/pallas_call | solution.py:63
  2.5 2.4 %collective-permute-start.1 = (bf16[272,128]{1,0:T(8,128)(2,1)}, bf16[272,128]{1,0:T(8,128)(2,1)S(1)}, u32[]{:S(2)}, u32[]{:S(2)}) collective-permute-start(bf16[272,128]{1,0:T(8,128)(2,1)} %get-tuple-element.11), channel_id=1, source_target_pairs={{0,24},{8,0},{16,8},{24,16},{1,25},{9,1},{17,9},{25,17},{2,26},{10... | collective-permute-start | bytes 208904 | tf_op jit(solution)/shard_map/ppermute | solution.py:487
  4.9 0.0 collective-permute-start
  4.9 0.0 copy-start.2
  4.9 6.1 %all-to-all-start = ((f32[32,2,384]{2,1,0:T(2,128)}), f32[32,2,384]{2,1,0:T(2,128)S(1)}, u32[]{:S(2)}, u32[]{:S(2)}) async-start(f32[32,2,384]{2,1,0:T(2,128)} %get-tuple-element.10), calls=%async_computation | async-start | bytes 196608 | tf_op jit(solution)/shard_map/all_to_all | solution.py:500
  11.0 0.7 slice_reduce_fusion
  11.7 0.0 collective-permute-done.1
  11.7 0.0 collective-permute-done
  11.7 0.0 copy-done.2
  11.8 0.0 copy-start
  11.8 6.8 %all-to-all-done.qc_ref = f32[32,2,384]{2,1,0:T(2,128)S(1)} async-done(((f32[32,2,384]{2,1,0:T(2,128)}), f32[32,2,384]{2,1,0:T(2,128)S(1)}, u32[]{:S(2)}, u32[]{:S(2)}) %all-to-all-start) | async-done | bytes 98336 | tf_op jit(solution)/shard_map/all_to_all | solution.py:500
  18.6 0.0 copy-start.1
  18.6 1.5 %collective-permute-start.3 = (bf16[3,272,128]{2,1,0:T(8,128)(2,1)S(1)}, bf16[3,272,128]{2,1,0:T(8,128)(2,1)S(1)}, u32[]{:S(2)}, u32[]{:S(2)}) collective-permute-start(bf16[3,272,128]{2,1,0:T(8,128)(2,1)S(1)} %pad_maximum_fusion.mid_ref), channel_id=1, source_target_pairs={{0,7},{1,0},{2,1},{3,2},{4,3},{5,4},{6,5},{7,6},{8,15},{9,8},{10,9... | collective-permute-start | bytes 626696 | tf_op jit(solution)/shard_map/ppermute | solution.py:487
  20.1 0.5 collective-permute-start.2
  20.6 0.0 copy-done.1
  20.6 0.0 copy-start.3
  20.6 11.3 %grid_fields.1 = f32[32,3,384]{2,1,0:T(4,128)} custom-call(s32[1]{0:T(128)} %bitcast.11.place_ref, f32[32,2,384]{2,1,0:T(2,128)} %copy-done.1, f32[64,192]{1,0:T(8,128)} %constant.21.clone.fy_ref, f32[32,96]{1,0:T(8,128)} %constant.22.clone.fx_ref, f32[64,96]{1,0:T(8,128)} %constant.23.clone.ix_ref, f32[128,192]{1,0:T(8,128)} %constant.24.clone.iy_ref), custom_call_target="tpu_custom_call" | custom-call | flops 8000000000 | bytes 4000000 | tf_op jit(solution)/shard_map/grid_fields/pallas_call | solution.py:273
  31.9 0.0 copy-done
  32.0 0.0 copy-done.3
  32.0 0.6 reshape.9.list_ref
  32.6 4.8 %all-to-all-start.1 = ((f32[32,3,384]{2,1,0:T(4,128)}), f32[32,3,384]{2,1,0:T(4,128)S(1)}, u32[]{:S(2)}, u32[]{:S(2)}) async-start(f32[32,3,384]{2,1,0:T(4,128)} %grid_fields.1), calls=%async_computation.1 | async-start | bytes 393216 | tf_op jit(solution)/shard_map/all_to_all | solution.py:508
  37.4 0.0 collective-permute-done.3.down_ref
  37.4 0.0 copy-start.5
  37.4 0.0 collective-permute-done.2.up_ref
  37.4 0.7 copy-done.5
  38.0 0.0 copy-start.6
  38.0 0.7 copy-done.6
  38.7 33.0 %edge_forces.1 = f32[3,384]{1,0:T(4,128)} custom-call(s32[12288]{0:T(1024)} %reshape.9.list_ref, s32[32,384]{1,0:T(8,128)} %bitcast.21, bf16[384,128]{1,0:T(8,128)(2,1)} %bitcast.17, bf16[3,384]{1,0:T(4,128)(2,1)} %bitcast.24, bf16[3,272,128]{2,1,0:T(8,128)(2,1)} %copy-done, bf16[3,272,128]{2,1,0:T(8,128)(2,1)} %copy-done.6, bf16[3,272,128]{2,1,0:T(8,128)(2,1)} %copy-done.5, ...), custom_call_target="tpu_custom_call" | custom-call | flops 6442450944 | bytes 4000000 | tf_op jit(solution)/shard_map/edge_forces/pallas_call | solution.py:455
  71.8 0.0 copy-start.4
  71.8 0.0 all-to-all-done.1
  71.8 0.1 reduce_sum.9
  71.8 0.6 copy-done.4
  72.5 0.6 copy.18
  (3 shorter events, 0.0 us)
Async XLA Ops:
  2.5 9.2 %collective-permute-start.1 = (bf16[272,128]{1,0:T(8,128)(2,1)}, bf16[272,128]{1,0:T(8,128)(2,1)S(1)}, u32[]{:S(2)}, u32[]{:S(2)}) collective-permute-start(bf16[272,128]{1,0:T(8,128)(2,1)} %get-tuple-element.11), channel_id=1, source_target_pairs={{0,24},{8,0},{16,8},{24,16},{1,25},{9,1},{17,9},{25,17},{2,26},{10... | collective-permute-start | bytes 208904 | tf_op jit(solution)/shard_map/ppermute | solution.py:487
  4.9 6.8 %collective-permute-start = (bf16[272,128]{1,0:T(8,128)(2,1)}, bf16[272,128]{1,0:T(8,128)(2,1)S(1)}, u32[]{:S(2)}, u32[]{:S(2)}) collective-permute-start(bf16[272,128]{1,0:T(8,128)(2,1)} %get-tuple-element.11), channel_id=1, source_target_pairs={{0,8},{8,16},{16,24},{24,0},{1,9},{9,17},{17,25},{25,1},{2,10},{10... | collective-permute-start | bytes 208904 | tf_op jit(solution)/shard_map/ppermute | solution.py:487
  4.9 6.8 %copy-start.2 = (bf16[272,128]{1,0:T(8,128)(2,1)S(1)}, bf16[272,128]{1,0:T(8,128)(2,1)}, u32[]{:S(2)}) copy-start(bf16[272,128]{1,0:T(8,128)(2,1)} %get-tuple-element.11) | copy-start | bytes 208900
  4.9 13.7 %all-to-all-start = ((f32[32,2,384]{2,1,0:T(2,128)}), f32[32,2,384]{2,1,0:T(2,128)S(1)}, u32[]{:S(2)}, u32[]{:S(2)}) async-start(f32[32,2,384]{2,1,0:T(2,128)} %get-tuple-element.10), calls=%async_computation | async-start | bytes 196608 | tf_op jit(solution)/shard_map/all_to_all | solution.py:500
  11.8 20.2 %copy-start = (bf16[3,272,128]{2,1,0:T(8,128)(2,1)}, bf16[3,272,128]{2,1,0:T(8,128)(2,1)S(1)}, u32[]{:S(2)}) copy-start(bf16[3,272,128]{2,1,0:T(8,128)(2,1)S(1)} %pad_maximum_fusion.mid_ref) | copy-start | bytes 626692
  18.6 2.0 %copy-start.1 = (f32[32,2,384]{2,1,0:T(2,128)}, f32[32,2,384]{2,1,0:T(2,128)S(1)}, u32[]{:S(2)}) copy-start(f32[32,2,384]{2,1,0:T(2,128)S(1)} %all-to-all-done.qc_ref) | copy-start | bytes 294916
  18.6 18.8 %collective-permute-start.3 = (bf16[3,272,128]{2,1,0:T(8,128)(2,1)S(1)}, bf16[3,272,128]{2,1,0:T(8,128)(2,1)S(1)}, u32[]{:S(2)}, u32[]{:S(2)}) collective-permute-start(bf16[3,272,128]{2,1,0:T(8,128)(2,1)S(1)} %pad_maximum_fusion.mid_ref), channel_id=1, source_target_pairs={{0,7},{1,0},{2,1},{3,2},{4,3},{5,4},{6,5},{7,6},{8,15},{9,8},{10,9... | collective-permute-start | bytes 626696 | tf_op jit(solution)/shard_map/ppermute | solution.py:487
  20.1 17.3 %collective-permute-start.2 = (bf16[3,272,128]{2,1,0:T(8,128)(2,1)S(1)}, bf16[3,272,128]{2,1,0:T(8,128)(2,1)S(1)}, u32[]{:S(2)}, u32[]{:S(2)}) collective-permute-start(bf16[3,272,128]{2,1,0:T(8,128)(2,1)S(1)} %pad_maximum_fusion.mid_ref), channel_id=1, source_target_pairs={{0,1},{1,2},{2,3},{3,4},{4,5},{5,6},{6,7},{7,0},{8,9},{9,10},{10,1... | collective-permute-start | bytes 626696 | tf_op jit(solution)/shard_map/ppermute | solution.py:487
  20.6 11.3 %copy-start.3 = (s32[1,1,384,32]{2,3,1,0:T(8,128)S(1)}, s32[1,1,384,32]{2,3,1,0:T(8,128)}, u32[]{:S(2)}) copy-start(s32[1,1,384,32]{2,3,1,0:T(8,128)} %param.21) | copy-start | bytes 147460
  32.6 39.2 %all-to-all-start.1 = ((f32[32,3,384]{2,1,0:T(4,128)}), f32[32,3,384]{2,1,0:T(4,128)S(1)}, u32[]{:S(2)}, u32[]{:S(2)}) async-start(f32[32,3,384]{2,1,0:T(4,128)} %grid_fields.1), calls=%async_computation.1 | async-start | bytes 393216 | tf_op jit(solution)/shard_map/all_to_all | solution.py:508
  37.4 0.7 copy-start.5
  38.0 0.7 copy-start.6
  71.8 0.7 copy-start.4

commit v8 on v7

--- a/solution.py
+++ b/solution.py
@@ -22,7 +22,7 @@
 GROUPS = LANES // ROWS
 CHUNK_ATOMS = 16
 PIECES = 4
-TILES = 2
+TILES = 1
 HIGHEST = lax.Precision.HIGHEST
 F32 = jnp.float32
 BF16 = jnp.bfloat16
@@ -251,7 +251,8 @@
         for a in range(3):
             part = jnp.where(match, fields[a * columns : (a + 1) * columns], 0.0)
             picked.append(jnp.sum(part, axis=0, keepdims=True))
-        out_ref[device] = jnp.concatenate(picked, axis=0)
+        for a in range(3):
+            out_ref[device, a] = picked[a]
         return carry
 
     lax.fori_loop(0, devices, sample, 0, unroll=4)
@@ -274,10 +275,14 @@
         functools.partial(grid_kernel, cycle_x, cycle_y),
         in_specs=[pl.BlockSpec(memory_space=pltpu.SMEM)] + [vmem] * 5,
         out_specs=vmem,
-        out_shape=jax.ShapeDtypeStruct((devices, 3, atoms), F32),
+        out_shape=jax.ShapeDtypeStruct((devices, 3, 1, atoms), F32),
         scratch_shapes=[plane] * 5
         + [pltpu.VMEM((devices, 2 * ROWS, atoms), BF16)],
-        compiler_params=pltpu.CompilerParams(vmem_limit_bytes=60 << 20),
+        compiler_params=pltpu.CompilerParams(
+            vmem_limit_bytes=5 * mesh_x * mesh_y * LANES * 4
+            + devices * atoms * (4 * ROWS + 64)
+            + (10 << 20)
+        ),
         cost_estimate=pl.CostEstimate(
             flops=8_000_000_000, bytes_accessed=4_000_000, transcendentals=100_000
         ),
@@ -439,11 +444,11 @@
     gate = jnp.dot(invariant, w_final_ref[...], preferred_element_type=F32)
     gate = gate * (0.5 + 0.5 * jnp.tanh(0.5 * gate)) * (1.0 / math.sqrt(channels))
     ones = jnp.ones((8, channels), F32)
-    short = [contract_last(ones, vector[a] * gate, HIGHEST)[:1] for a in range(3)]
-    out_ref[...] = jnp.concatenate(short, axis=0)
-
-
-def edge_forces(index, feat, pos, mid, up, down, w_self, w_pair, w_radial, w_expand, w_contract, w_final):
+    for a in range(3):
+        out_ref[a] = contract_last(ones, vector[a] * gate, HIGHEST)[:1]
+
+
+def edge_forces(lists, index, feat, pos, mid, up, down, w_self, w_pair, w_radial, w_expand, w_contract, w_final):
     atoms, channels = feat.shape
     per_atom = index.shape[0]
     ghosts = mid.shape[1] - EXTRA
@@ -456,7 +461,7 @@
         edge_kernel,
         in_specs=[pl.BlockSpec(memory_space=pltpu.SMEM)] + [vmem] * 12,
         out_specs=vmem,
-        out_shape=jax.ShapeDtypeStruct((3, atoms), F32),
+        out_shape=jax.ShapeDtypeStruct((3, 1, atoms), F32),
         scratch_shapes=[
             pltpu.VMEM((slots_all, 8, LANES), F32),
             pltpu.VMEM((slots_all // LANES, 8, LANES), F32),
@@ -469,7 +474,7 @@
             pltpu.VMEM((4, atoms, LANES), F32),
             pltpu.VMEM(w_expand.shape, BF16),
         ],
-        compiler_params=pltpu.CompilerParams(vmem_limit_bytes=56 << 20),
+        compiler_params=pltpu.CompilerParams(vmem_limit_bytes=32 << 20),
         cost_estimate=pl.CostEstimate(
             flops=4 * edges * channels * latent,
             bytes_accessed=4_000_000,
@@ -477,7 +482,7 @@
         ),
         name="edge_forces",
     )(
-        index.reshape(-1), index, feat, pos, mid, up, down, w_self, w_pair, w_radial,
+        lists, index, feat, pos, mid, up, down, w_self, w_pair, w_radial,
         w_expand, w_contract, w_final,
     )
 
@@ -499,7 +504,8 @@
     )
     gathered = lax.all_to_all(spread, ("dx", "dy"), split_axis=0, concat_axis=0, tiled=True)
     mid = jnp.stack([ring(exported, "dx", 1), exported, ring(exported, "dx", -1)])
-    lists = neighbour_list[0, 0].T
+    index = neighbour_list[0, 0].T
+    lists = index.reshape(-1)
     gathered, mid, lists = lax.optimization_barrier((gathered, mid, lists))
     up = ring(mid, "dy", 1)
     down = ring(mid, "dy", -1)
@@ -507,13 +513,13 @@
     partial = grid_fields(place[None].astype(jnp.int32), gathered, cycle_x, cycle_y)
     received = lax.all_to_all(partial, ("dx", "dy"), split_axis=0, concat_axis=0, tiled=True)
     short = edge_forces(
-        lists, feat, pos, mid, up, down, w_self, w_pair, w_radial, w_expand,
+        lists, index, feat, pos, mid, up, down, w_self, w_pair, w_radial, w_expand,
         w_contract, w_final,
     )
     field = jnp.sum(received, axis=0)
     total = short + spread[0, :1] * field
     live = lax.broadcasted_iota(jnp.int32, (1, feat.shape[0]), 1) < atom_count[0, 0]
-    return jnp.where(live, total, jnp.zeros_like(total))[None, None]
+    return jnp.where(live, total, jnp.zeros_like(total)).transpose(1, 0, 2)[None]
 
 
 def solution(mesh):

time: 73.5 us -> 71.4 us (0.971)
  local copies, waits for them, and re-layouts: 3.88 us -> 0.87 us
    unnamed x14 -> x28, local copies, waits for them, and re-layouts: 1.98 us -> 0.13 us
    pallas_call x1, Pallas kernels: 33 us -> 34.4 us  [edge_forces(): pl.pallas_call(edge_kernel, in_specs=[pl.BlockSpec(memory_space=pltpu.SME...]
    pallas_call x1, Pallas kernels: 11.3 us -> 10.4 us  [grid_fields(): pl.pallas_call(functools.partial(grid_kernel, cycle_x, cycle_y), in_specs...]
  transfers between devices with their start and end apart: 6 -> 6, of which waited for: 1 -> 1; matrix products, arithmetic and copies ran while one was open for 2% -> 1% of each run, Pallas kernels for 61% -> 63%
where the time goes in v8:
time: 71.4 us; the launch traced here: 71.1 us
  Pallas kernels  46.6 us (65%)
  starting transfers between devices  15.3 us (21%)
  waiting for transfers between devices  6.64 us (9%)
  local copies, waits for them, and re-layouts  0.87 us (1%)
  between operations  0.87 us (1%)
  other arithmetic  0.77 us (1%)
    pallas_call x1, Pallas kernels, edge_forces(): pl.pallas_call(edge_kernel, in_specs=[pl.BlockSpec(memory_space=pltpu.SME...  34.4 us
    pallas_call x1, Pallas kernels, grid_fields(): pl.pallas_call(functools.partial(grid_kernel, cycle_x, cycle_y), in_specs...  10.4 us
    all_to_all x1, waiting for transfers between devices, shards(): lax.all_to_all(spread, ('dx', 'dy'), split_axis=0, concat_axis=0, tiled=T...  6.63 us
    all_to_all x1, starting transfers between devices, shards(): lax.all_to_all(spread, ('dx', 'dy'), split_axis=0, concat_axis=0, tiled=T...  6.1 us
    all_to_all x1, starting transfers between devices, shards(): lax.all_to_all(partial, ('dx', 'dy'), split_axis=0, concat_axis=0, tiled=...  4.78 us
    ppermute x4, starting transfers between devices, ring(): lax.ppermute(array, axis, [(i, (i + step) % size) for i in range(size)])  4.41 us
    pallas_call x1, Pallas kernels, prepare(): pl.pallas_call(prepare_kernel, in_specs=[pl.BlockSpec(memory_space=pltpu....  1.89 us
  transfers between devices with their start and end apart: 6, of which 1 were waited for; matrix products, arithmetic and copies ran while one was open for 1% of the time, Pallas kernels for 63%

profile of v8, /device:TPU:0, one launch (start us, length us, event | category | flops | bytes accessed | tf_op | source)
XLA Modules:
  0.0 71.1 jit_solution(7062408676998635655)
XLA Ops:
  0.7 1.9 %prepare.1 = (bf16[272,128]{1,0:T(8,128)(2,1)}, f32[32,2,384]{2,1,0:T(2,128)}) custom-call(s32[1,1]{1,0:T(1,128)} %copy.19.count_ref, bf16[384,128]{1,0:T(8,128)(2,1)} %bitcast.18, bf16[3,384]{1,0:T(4,128)(2,1)} %bitcast.22, s32[1,256]{1,0:T(1,128)} %bitcast.28, s32[1,384]{1,0:T(1,128)} %bitcast.27, bf16[1,128]{1,0:T(2,128)(2,1)} %bitcast.29), custom_call_target="tpu_custom_call" | custom-call | tf_op jit(solution)/shard_map/prepare/pallas_call | solution.py:63
  2.5 2.4 %collective-permute-start.1 = (bf16[272,128]{1,0:T(8,128)(2,1)}, bf16[272,128]{1,0:T(8,128)(2,1)S(1)}, u32[]{:S(2)}, u32[]{:S(2)}) collective-permute-start(bf16[272,128]{1,0:T(8,128)(2,1)} %get-tuple-element.11), channel_id=1, source_target_pairs={{0,24},{8,0},{16,8},{24,16},{1,25},{9,1},{17,9},{25,17},{2,26},{10... | collective-permute-start | bytes 208904 | tf_op jit(solution)/shard_map/ppermute | solution.py:492
  4.9 0.0 collective-permute-start
  4.9 0.0 copy-start.1
  4.9 6.1 %all-to-all-start = ((f32[32,2,384]{2,1,0:T(2,128)}), f32[32,2,384]{2,1,0:T(2,128)S(1)}, u32[]{:S(2)}, u32[]{:S(2)}) async-start(f32[32,2,384]{2,1,0:T(2,128)} %get-tuple-element.10), calls=%async_computation | async-start | bytes 196608 | tf_op jit(solution)/shard_map/all_to_all | solution.py:505
  11.0 0.0 copy-start.13
  11.0 0.7 %slice_reduce_fusion = f32[384]{0:T(512)S(1)} fusion(f32[32,2,384]{2,1,0:T(2,128)} %get-tuple-element.10), kind=kLoop, calls=%fused_computation.4 | loop fusion | bytes 3072 | tf_op jit(solution)/shard_map/slice | solution.py:520
  11.8 0.0 copy-done.1
  11.8 0.0 collective-permute-done.1
  11.8 0.0 collective-permute-done
  11.8 0.1 copy-done.13
  11.9 0.0 copy-start.9
  11.9 0.0 copy-start.10
  11.9 0.0 copy-start.11
  11.9 0.0 copy-start.12
  12.0 6.6 %all-to-all-done.qc_ref = f32[32,2,384]{2,1,0:T(2,128)S(1)} async-done(((f32[32,2,384]{2,1,0:T(2,128)}), f32[32,2,384]{2,1,0:T(2,128)S(1)}, u32[]{:S(2)}, u32[]{:S(2)}) %all-to-all-start) | async-done | bytes 98336 | tf_op jit(solution)/shard_map/all_to_all | solution.py:505
  18.6 1.5 %collective-permute-start.3 = (bf16[3,272,128]{2,1,0:T(8,128)(2,1)S(1)}, bf16[3,272,128]{2,1,0:T(8,128)(2,1)S(1)}, u32[]{:S(2)}, u32[]{:S(2)}) collective-permute-start(bf16[3,272,128]{2,1,0:T(8,128)(2,1)S(1)} %pad_maximum_fusion.mid_ref), channel_id=1, source_target_pairs={{0,7},{1,0},{2,1},{3,2},{4,3},{5,4},{6,5},{7,6},{8,15},{9,8},{10,9... | collective-permute-start | bytes 626696 | tf_op jit(solution)/shard_map/ppermute | solution.py:492
  20.1 0.5 collective-permute-start.2
  20.6 0.0 copy-done.9
  20.6 0.0 copy-done.10
  20.6 0.0 copy-done.11
  20.6 0.0 copy-done.12
  20.6 0.0 copy-start.3
  20.6 0.0 copy-start.4
  20.7 10.4 %grid_fields.1 = f32[32,3,1,384]{3,2,1,0:T(1,128)} custom-call(s32[1]{0:T(128)} %bitcast.11.place_ref, f32[32,2,384]{2,1,0:T(2,128)S(1)} %all-to-all-done.qc_ref, f32[64,192]{1,0:T(8,128)S(1)} %copy-done.10, f32[32,96]{1,0:T(8,128)S(1)} %copy-done.12, f32[64,96]{1,0:T(8,128)S(1)} %copy-done.11, f32[128,192]{1,0:T(8,128)S(1)} %copy-done.9), custom_call_target="tpu_custom_call" | custom-call | flops 8000000000 | bytes 4000000 | tf_op jit(solution)/shard_map/grid_fields/pallas_call | solution.py:274
  31.0 0.0 copy-start
  31.1 0.0 copy-start.2
  31.1 0.0 copy-start.5
  31.1 0.0 copy-start.6
  31.1 0.0 copy-start.7
  31.1 0.0 copy-start.8
  31.1 4.8 %all-to-all-start.1 = ((f32[32,3,1,384]{3,2,1,0:T(1,128)}), f32[32,3,1,384]{3,2,1,0:T(1,128)S(1)}, u32[]{:S(2)}, u32[]{:S(2)}) async-start(f32[32,3,1,384]{3,2,1,0:T(1,128)} %grid_fields.1), calls=%async_computation.1 | async-start | bytes 294912 | tf_op jit(solution)/shard_map/all_to_all | solution.py:514
  35.9 0.0 collective-permute-done.3.down_ref
  35.9 0.0 collective-permute-done.2.up_ref
  35.9 0.0 copy-done.3
  35.9 0.0 copy-done.4
  35.9 0.0 copy-done
  35.9 0.0 copy-done.2
  35.9 0.0 copy-done.5
  35.9 0.0 copy-done.6
  36.0 0.0 copy-done.7
  36.0 0.0 copy-done.8
  36.0 34.4 %edge_forces.1 = f32[3,1,384]{2,1,0:T(1,128)S(1)} custom-call(s32[12288]{0:T(1024)S(1)} %reshape.46.list_ref, s32[32,384]{1,0:T(8,128)S(1)} %bitcast.21, bf16[384,128]{1,0:T(8,128)(2,1)S(1)} %bitcast.19, bf16[3,384]{1,0:T(4,128)(2,1)S(1)} %bitcast.23, bf16[3,272,128]{2,1,0:T(8,128)(2,1)S(1)} %pad_maximum_fusion.mid_ref, ...), custom_call_target="tpu_custom_call" | custom-call | flops 6442450944 | bytes 4000000 | tf_op jit(solution)/shard_map/edge_forces/pallas_call | solution.py:460
  70.3 0.0 all-to-all-done.1
  70.3 0.1 reduce_sum.11
  70.5 0.6 fusion
  (3 shorter events, 0.0 us)
Async XLA Ops:
  2.5 9.3 %collective-permute-start.1 = (bf16[272,128]{1,0:T(8,128)(2,1)}, bf16[272,128]{1,0:T(8,128)(2,1)S(1)}, u32[]{:S(2)}, u32[]{:S(2)}) collective-permute-start(bf16[272,128]{1,0:T(8,128)(2,1)} %get-tuple-element.11), channel_id=1, source_target_pairs={{0,24},{8,0},{16,8},{24,16},{1,25},{9,1},{17,9},{25,17},{2,26},{10... | collective-permute-start | bytes 208904 | tf_op jit(solution)/shard_map/ppermute | solution.py:492
  4.9 6.9 %collective-permute-start = (bf16[272,128]{1,0:T(8,128)(2,1)}, bf16[272,128]{1,0:T(8,128)(2,1)S(1)}, u32[]{:S(2)}, u32[]{:S(2)}) collective-permute-start(bf16[272,128]{1,0:T(8,128)(2,1)} %get-tuple-element.11), channel_id=1, source_target_pairs={{0,8},{8,16},{16,24},{24,0},{1,9},{9,17},{17,25},{25,1},{2,10},{10... | collective-permute-start | bytes 208904 | tf_op jit(solution)/shard_map/ppermute | solution.py:492
  4.9 6.9 %copy-start.1 = (s32[1,1,384,32]{2,3,1,0:T(8,128)S(1)}, s32[1,1,384,32]{2,3,1,0:T(8,128)}, u32[]{:S(2)}) copy-start(s32[1,1,384,32]{2,3,1,0:T(8,128)} %param.21) | copy-start | bytes 147460
  4.9 13.7 %all-to-all-start = ((f32[32,2,384]{2,1,0:T(2,128)}), f32[32,2,384]{2,1,0:T(2,128)S(1)}, u32[]{:S(2)}, u32[]{:S(2)}) async-start(f32[32,2,384]{2,1,0:T(2,128)} %get-tuple-element.10), calls=%async_computation | async-start | bytes 196608 | tf_op jit(solution)/shard_map/all_to_all | solution.py:505
  11.0 0.9 %copy-start.13 = (bf16[272,128]{1,0:T(8,128)(2,1)S(1)}, bf16[272,128]{1,0:T(8,128)(2,1)}, u32[]{:S(2)}) copy-start(bf16[272,128]{1,0:T(8,128)(2,1)} %get-tuple-element.11) | copy-start | bytes 208900
  11.9 8.7 %copy-start.9 = (f32[128,192]{1,0:T(8,128)S(1)}, f32[128,192]{1,0:T(8,128)}, u32[]{:S(2)}) copy-start(f32[128,192]{1,0:T(8,128)} %constant.24.clone.iy_ref) | copy-start | bytes 294916
  11.9 8.7 %copy-start.10 = (f32[64,192]{1,0:T(8,128)S(1)}, f32[64,192]{1,0:T(8,128)}, u32[]{:S(2)}) copy-start(f32[64,192]{1,0:T(8,128)} %constant.21.clone.fy_ref) | copy-start | bytes 147460
  11.9 8.7 %copy-start.11 = (f32[64,96]{1,0:T(8,128)S(1)}, f32[64,96]{1,0:T(8,128)}, u32[]{:S(2)}) copy-start(f32[64,96]{1,0:T(8,128)} %constant.23.clone.ix_ref) | copy-start | bytes 73732
  11.9 8.7 %copy-start.12 = (f32[32,96]{1,0:T(8,128)S(1)}, f32[32,96]{1,0:T(8,128)}, u32[]{:S(2)}) copy-start(f32[32,96]{1,0:T(8,128)} %constant.22.clone.fx_ref) | copy-start | bytes 36868
  18.6 17.3 %collective-permute-start.3 = (bf16[3,272,128]{2,1,0:T(8,128)(2,1)S(1)}, bf16[3,272,128]{2,1,0:T(8,128)(2,1)S(1)}, u32[]{:S(2)}, u32[]{:S(2)}) collective-permute-start(bf16[3,272,128]{2,1,0:T(8,128)(2,1)S(1)} %pad_maximum_fusion.mid_ref), channel_id=1, source_target_pairs={{0,7},{1,0},{2,1},{3,2},{4,3},{5,4},{6,5},{7,6},{8,15},{9,8},{10,9... | collective-permute-start | bytes 626696 | tf_op jit(solution)/shard_map/ppermute | solution.py:492
  20.1 15.8 %collective-permute-start.2 = (bf16[3,272,128]{2,1,0:T(8,128)(2,1)S(1)}, bf16[3,272,128]{2,1,0:T(8,128)(2,1)S(1)}, u32[]{:S(2)}, u32[]{:S(2)}) collective-permute-start(bf16[3,272,128]{2,1,0:T(8,128)(2,1)S(1)} %pad_maximum_fusion.mid_ref), channel_id=1, source_target_pairs={{0,1},{1,2},{2,3},{3,4},{4,5},{5,6},{6,7},{7,0},{8,9},{9,10},{10,1... | collective-permute-start | bytes 626696 | tf_op jit(solution)/shard_map/ppermute | solution.py:492
  20.6 15.3 %copy-start.3 = (bf16[128,1024]{1,0:T(8,128)(2,1)S(1)}, bf16[128,1024]{1,0:T(8,128)(2,1)}, u32[]{:S(2)}) copy-start(bf16[128,1024]{1,0:T(8,128)(2,1)} %w_expand_ref.1) | copy-start | bytes 786436
  20.6 15.3 %copy-start.4 = (bf16[1024,128]{1,0:T(8,128)(2,1)S(1)}, bf16[1024,128]{1,0:T(8,128)(2,1)}, u32[]{:S(2)}) copy-start(bf16[1024,128]{1,0:T(8,128)(2,1)} %w_contract_ref.1) | copy-start | bytes 786436
  31.0 4.9 %copy-start = (bf16[1,1,384,128]{3,2,1,0:T(8,128)(2,1)S(1)}, bf16[1,1,384,128]{3,2,1,0:T(8,128)(2,1)}, u32[]{:S(2)}) copy-start(bf16[1,1,384,128]{3,2,1,0:T(8,128)(2,1)} %param.17) | copy-start | bytes 294916
  31.1 4.9 %copy-start.2 = (bf16[1,1,3,384]{3,2,1,0:T(4,128)(2,1)S(1)}, bf16[1,1,3,384]{3,2,1,0:T(4,128)(2,1)}, u32[]{:S(2)}) copy-start(bf16[1,1,3,384]{3,2,1,0:T(4,128)(2,1)} %param.18) | copy-start | bytes 6916
  31.1 4.9 %copy-start.5 = (bf16[128,256]{1,0:T(8,128)(2,1)S(1)}, bf16[128,256]{1,0:T(8,128)(2,1)}, u32[]{:S(2)}) copy-start(bf16[128,256]{1,0:T(8,128)(2,1)} %w_pair_ref.1) | copy-start | bytes 196612
  31.1 4.9 %copy-start.6 = (bf16[128,128]{1,0:T(8,128)(2,1)S(1)}, bf16[128,128]{1,0:T(8,128)(2,1)}, u32[]{:S(2)}) copy-start(bf16[128,128]{1,0:T(8,128)(2,1)} %w_self_ref.1) | copy-start | bytes 98308
  31.1 4.9 %copy-start.7 = (bf16[128,128]{1,0:T(8,128)(2,1)S(1)}, bf16[128,128]{1,0:T(8,128)(2,1)}, u32[]{:S(2)}) copy-start(bf16[128,128]{1,0:T(8,128)(2,1)} %w_final_ref.1) | copy-start | bytes 98308
  31.1 4.9 %copy-start.8 = (f32[8,128]{1,0:T(8,128)S(1)}, f32[8,128]{1,0:T(8,128)}, u32[]{:S(2)}) copy-start(f32[8,128]{1,0:T(8,128)} %w_radial_ref.1) | copy-start | bytes 12292
  31.1 39.2 %all-to-all-start.1 = ((f32[32,3,1,384]{3,2,1,0:T(1,128)}), f32[32,3,1,384]{3,2,1,0:T(1,128)S(1)}, u32[]{:S(2)}, u32[]{:S(2)}) async-start(f32[32,3,1,384]{3,2,1,0:T(1,128)} %grid_fields.1), calls=%async_computation.1 | async-start | bytes 294912 | tf_op jit(solution)/shard_map/all_to_all | solution.py:514

commit v9 on v8

--- a/solution.py
+++ b/solution.py
@@ -22,7 +22,7 @@
 GROUPS = LANES // ROWS
 CHUNK_ATOMS = 16
 PIECES = 4
-TILES = 1
+TILES = 2
 HIGHEST = lax.Precision.HIGHEST
 F32 = jnp.float32
 BF16 = jnp.bfloat16
@@ -40,7 +40,16 @@
     )
 
 
-def prepare_kernel(count_ref, feat_ref, pos_ref, export_ref, cell_ref, wq_ref, out_ref, qc_ref):
+def charge_kernel(count_ref, feat_ref, cell_ref, wq_ref, qc_ref):
+    atoms = feat_ref.shape[0]
+    weights = jnp.broadcast_to(wq_ref[...].astype(F32), (16, LANES)).astype(BF16)
+    charge = contract_last(weights, feat_ref[...])[:1]
+    live = lax.broadcasted_iota(jnp.int32, (1, atoms), 1) < count_ref[0, 0]
+    both = jnp.concatenate([jnp.where(live, charge, 0.0), cell_ref[...].astype(F32)], axis=0)
+    qc_ref[...] = jnp.broadcast_to(both[None], qc_ref.shape)
+
+
+def export_kernel(feat_ref, pos_ref, export_ref, after_ref, out_ref):
     atoms = feat_ref.shape[0]
     ghosts = export_ref.shape[1]
     pick = lax.broadcasted_iota(jnp.int32, (atoms, ghosts), 0) == export_ref[...]
@@ -50,26 +59,30 @@
     coords = jnp.dot(pos.astype(BF16), pick, preferred_element_type=F32)
     tail = [coords[:8, h * LANES : (h + 1) * LANES] for h in range(ghosts // LANES)]
     out_ref[pl.ds(ghosts, EXTRA), :] = jnp.concatenate(tail, axis=0).astype(BF16)
-    weights = jnp.broadcast_to(wq_ref[...].astype(F32), (16, LANES)).astype(BF16)
-    charge = contract_last(weights, feat_ref[...])[:1]
-    live = lax.broadcasted_iota(jnp.int32, (1, atoms), 1) < count_ref[0, 0]
-    both = jnp.concatenate([jnp.where(live, charge, 0.0), cell_ref[...].astype(F32)], axis=0)
-    qc_ref[...] = jnp.broadcast_to(both[None], qc_ref.shape)
-
-
-def prepare(devices, count, feat, pos, exports, cells, w_charge):
-    atoms, ghosts = (feat.shape[0], exports.shape[0])
+
+
+def charges(devices, count, feat, cells, w_charge):
     vmem = pl.BlockSpec(memory_space=pltpu.VMEM)
     return pl.pallas_call(
-        prepare_kernel,
-        in_specs=[pl.BlockSpec(memory_space=pltpu.SMEM)] + [vmem] * 5,
-        out_specs=[vmem, vmem],
-        out_shape=[
-            jax.ShapeDtypeStruct((ghosts + EXTRA, feat.shape[1]), BF16),
-            jax.ShapeDtypeStruct((devices, 2, atoms), F32),
-        ],
-        name="prepare",
-    )(count, feat, pos, exports[None], cells[None], w_charge[None])
+        charge_kernel,
+        in_specs=[pl.BlockSpec(memory_space=pltpu.SMEM)] + [vmem] * 3,
+        out_specs=vmem,
+        out_shape=jax.ShapeDtypeStruct((devices, 2, feat.shape[0]), F32),
+        compiler_params=pltpu.CompilerParams(vmem_limit_bytes=16 << 20),
+        name="charges",
+    )(count, feat, cells[None], w_charge[None])
+
+
+def exports_after(after, feat, pos, exports):
+    vmem = pl.BlockSpec(memory_space=pltpu.VMEM)
+    return pl.pallas_call(
+        export_kernel,
+        in_specs=[vmem] * 3 + [pl.BlockSpec(memory_space=pl.ANY)],
+        out_specs=vmem,
+        out_shape=jax.ShapeDtypeStruct((exports.shape[0] + EXTRA, feat.shape[1]), BF16),
+        compiler_params=pltpu.CompilerParams(vmem_limit_bytes=16 << 20),
+        name="exports",
+    )(feat, pos, exports[None], after)
 
 
 def real_tables(count):
@@ -145,7 +158,7 @@
         buf_a[pl.ds(pl.multiple_of(device * columns, 8), columns), :] = total
         return carry
 
-    lax.fori_loop(0, devices, spread, 0, unroll=4)
+    lax.fori_loop(0, devices, spread, 0, unroll=8)
 
     lane = lax.broadcasted_iota(jnp.int32, (1, LANES), 1)
     lane_group = lane // ROWS
@@ -255,7 +268,7 @@
             out_ref[device, a] = picked[a]
         return carry
 
-    lax.fori_loop(0, devices, sample, 0, unroll=4)
+    lax.fori_loop(0, devices, sample, 0, unroll=8)
 
 
 def grid_fields(place, gathered, cycle_x, cycle_y):
@@ -293,7 +306,7 @@
 def edge_kernel(
     list_ref, index_ref, feat_ref, pos_ref, mid_ref, up_ref, down_ref, w_self_ref, w_pair_ref,
     w_radial_ref, w_expand_ref, w_contract_ref, w_final_ref, out_ref,
-    table, places, near_a, near_b, near_c, edge_a, edge_b, edge_c, marks, own_ref, sums_ref, w_half,
+    table, places, near_a, near_b, near_c, edge_a, edge_b, edge_c, marks, own_ref, sums_ref,
 ):
     atoms, channels = feat_ref.shape
     ghosts = mid_ref.shape[1] - EXTRA
@@ -306,7 +319,6 @@
     latent = w_expand_ref.shape[1]
     width = latent // TILES
     slots = per_atom // PIECES
-    w_half[...] = w_expand_ref[...] * 0.5
 
     def fill(start, rows, coords, shift):
         count = rows.shape[0]
@@ -398,8 +410,9 @@
 
     def network(edge_in, part):
         cols = pl.ds(part * width, width)
-        half = jnp.dot(edge_in[...], w_half[:, cols], preferred_element_type=F32).astype(BF16)
-        hidden = half + half * jnp.tanh(half)
+        full = jnp.dot(edge_in[...], w_expand_ref[:, cols], preferred_element_type=F32)
+        decay = jnp.exp(jnp.minimum(-full, 80.0))
+        hidden = (full * pl.reciprocal(1.0 + decay, approx=True)).astype(BF16)
         return jnp.dot(hidden, w_contract_ref[cols, :], preferred_element_type=F32)
 
     def collect(index, mixed, near):
@@ -472,7 +485,6 @@
             pltpu.VMEM((per_atom, atoms, 32), F32),
             pltpu.VMEM((atoms, LANES), F32),
             pltpu.VMEM((4, atoms, LANES), F32),
-            pltpu.VMEM(w_expand.shape, BF16),
         ],
         compiler_params=pltpu.CompilerParams(vmem_limit_bytes=32 << 20),
         cost_estimate=pl.CostEstimate(
@@ -499,9 +511,8 @@
     feat = features[0, 0]
     pos = positions[0, 0]
     cycle_x, cycle_y = (lax.axis_size("dx"), lax.axis_size("dy"))
-    exported, spread = prepare(
-        cycle_x * cycle_y, atom_count, feat, pos, ghost_index[0, 0], cell_index[0, 0], w_charge
-    )
+    spread = charges(cycle_x * cycle_y, atom_count, feat, cell_index[0, 0], w_charge)
+    exported = exports_after(spread, feat, pos, ghost_index[0, 0])
     gathered = lax.all_to_all(spread, ("dx", "dy"), split_axis=0, concat_axis=0, tiled=True)
     mid = jnp.stack([ring(exported, "dx", 1), exported, ring(exported, "dx", -1)])
     index = neighbour_list[0, 0].T

time: 71.4 us -> 75.9 us (1.063)
  starting transfers between devices: 15.3 us -> 17.9 us
  waiting for transfers between devices: 6.64 us -> 4.24 us
  Pallas kernels: 46.6 us -> 48.8 us
  local copies, waits for them, and re-layouts: 0.87 us -> 2.98 us
    all_to_all x1, waiting for transfers between devices: 6.63 us -> 1.01 us  [shards(): lax.all_to_all(spread, ('dx', 'dy'), split_axis=0, concat_axis=0, tiled=T...]
    pallas_call x1, Pallas kernels: 34.4 us -> 38.6 us  [edge_forces(): pl.pallas_call(edge_kernel, in_specs=[pl.BlockSpec(memory_space=pltpu.SME...]
    ppermute x4, waiting for transfers between devices: 0.01 us -> 3.23 us  [ring(): lax.ppermute(array, axis, [(i, (i + step) % size) for i in range(size)])]
    unnamed x28 -> x34, local copies, waits for them, and re-layouts: 0.13 us -> 2.28 us
    pallas_call x1, Pallas kernels: 10.4 us -> 9.07 us  [grid_fields(): pl.pallas_call(functools.partial(grid_kernel, cycle_x, cycle_y), in_specs...]
    all_to_all x1, starting transfers between devices: 6.1 us -> 7.3 us  [shards(): lax.all_to_all(spread, ('dx', 'dy'), split_axis=0, concat_axis=0, tiled=T...]
    all_to_all x1, starting transfers between devices: 4.78 us -> 5.95 us  [shards(): lax.all_to_all(partial, ('dx', 'dy'), split_axis=0, concat_axis=0, tiled=...]
    pallas_call x1 -> x2, Pallas kernels: 1.89 us -> 1.06 us  [the longest x1 0.8 us: charges(): pl.pallas_call(charge_kernel, in_specs=[pl.BlockSpec(memory_space=pltpu.S...]
  transfers between devices with their start and end apart: 6 -> 6, of which waited for: 1 -> 3; matrix products, arithmetic and copies ran while one was open for 1% -> 1% of each run, Pallas kernels for 63% -> 63%
where the time goes in v9:
time: 75.9 us; the launch traced here: 75.6 us
  Pallas kernels  48.8 us (64%)
  starting transfers between devices  17.9 us (24%)
  waiting for transfers between devices  4.24 us (6%)
  local copies, waits for them, and re-layouts  2.98 us (4%)
  between operations  0.89 us (1%)
  other arithmetic  0.77 us (1%)
    pallas_call x1, Pallas kernels, edge_forces(): pl.pallas_call(edge_kernel, in_specs=[pl.BlockSpec(memory_space=pltpu.SME...  38.6 us
    pallas_call x1, Pallas kernels, grid_fields(): pl.pallas_call(functools.partial(grid_kernel, cycle_x, cycle_y), in_specs...  9.07 us
    all_to_all x1, starting transfers between devices, shards(): lax.all_to_all(spread, ('dx', 'dy'), split_axis=0, concat_axis=0, tiled=T...  7.3 us
    all_to_all x1, starting transfers between devices, shards(): lax.all_to_all(partial, ('dx', 'dy'), split_axis=0, concat_axis=0, tiled=...  5.95 us
    ppermute x4, starting transfers between devices, ring(): lax.ppermute(array, axis, [(i, (i + step) % size) for i in range(size)])  4.66 us
    ppermute x4, waiting for transfers between devices, ring(): lax.ppermute(array, axis, [(i, (i + step) % size) for i in range(size)])  3.23 us
    unnamed x34, local copies, waits for them, and re-layouts  2.28 us
  transfers between devices with their start and end apart: 6, of which 3 were waited for; matrix products, arithmetic and copies ran while one was open for 1% of the time, Pallas kernels for 63%

profile of v9, /device:TPU:0, one launch (start us, length us, event | category | flops | bytes accessed | tf_op | source)
XLA Modules:
  0.0 75.6 jit_solution(12903769516219594134)
XLA Ops:
  0.7 0.0 copy-start.4
  0.7 0.0 copy-start.6
  0.7 0.7 copy-done.4
  1.3 0.0 copy-done.6
  1.3 0.0 copy-start
  1.3 0.9 %copy-done = bf16[1,1,384,128]{3,2,1,0:T(8,128)(2,1)S(1)} copy-done((bf16[1,1,384,128]{3,2,1,0:T(8,128)(2,1)S(1)}, bf16[1,1,384,128]{3,2,1,0:T(8,128)(2,1)}, u32[]{:S(2)}) %copy-start) | copy-done | bytes 98328
  2.2 0.8 %charges.1.after_ref = f32[32,2,384]{2,1,0:T(2,128)} custom-call(s32[1,1]{1,0:T(1,128)} %copy.19.count_ref, bf16[384,128]{1,0:T(8,128)(2,1)S(1)} %bitcast.18, s32[1,384]{1,0:T(1,128)S(1)} %bitcast.26, bf16[1,128]{1,0:T(2,128)(2,1)S(1)} %bitcast.28), custom_call_target="tpu_custom_call" | custom-call | tf_op jit(solution)/shard_map/charges/pallas_call | solution.py:66
  3.0 0.0 copy-start.1
  3.0 0.0 copy-start.5
  3.0 7.3 %all-to-all-start = ((f32[32,2,384]{2,1,0:T(2,128)}), f32[32,2,384]{2,1,0:T(2,128)S(1)}, u32[]{:S(2)}, u32[]{:S(2)}) async-start(f32[32,2,384]{2,1,0:T(2,128)} %charges.1.after_ref), calls=%async_computation | async-start | bytes 196608 | tf_op jit(solution)/shard_map/all_to_all | solution.py:516
  10.3 0.0 copy-start.3
  10.3 0.0 copy-done.1
  10.4 0.0 copy-done.5
  10.4 0.7 copy-done.3
  11.0 0.0 copy-start.2
  11.0 0.3 exports.1
  11.3 1.6 %collective-permute-start.1 = (bf16[272,128]{1,0:T(8,128)(2,1)S(1)}, bf16[272,128]{1,0:T(8,128)(2,1)S(1)}, u32[]{:S(2)}, u32[]{:S(2)}) collective-permute-start(bf16[272,128]{1,0:T(8,128)(2,1)S(1)} %exports.1), channel_id=1, source_target_pairs={{0,24},{8,0},{16,8},{24,16},{1,25},{9,1},{17,9},{25,17},{2,26},{10... | collective-permute-start | bytes 208904 | tf_op jit(solution)/shard_map/ppermute | solution.py:504
  12.9 0.0 collective-permute-start
  12.9 0.7 slice_reduce_fusion
  13.6 0.0 copy-done.2
  13.6 2.0 %collective-permute-done.1 = bf16[272,128]{1,0:T(8,128)(2,1)S(1)} collective-permute-done((bf16[272,128]{1,0:T(8,128)(2,1)S(1)}, bf16[272,128]{1,0:T(8,128)(2,1)S(1)}, u32[]{:S(2)}, u32[]{:S(2)}) %collective-permute-start.1) | collective-permute-done | bytes 69664 | tf_op jit(solution)/shard_map/ppermute | solution.py:504
  15.7 1.2 %collective-permute-done = bf16[272,128]{1,0:T(8,128)(2,1)S(1)} collective-permute-done((bf16[272,128]{1,0:T(8,128)(2,1)S(1)}, bf16[272,128]{1,0:T(8,128)(2,1)S(1)}, u32[]{:S(2)}, u32[]{:S(2)}) %collective-permute-start) | collective-permute-done | bytes 69664 | tf_op jit(solution)/shard_map/ppermute | solution.py:504
  16.8 0.0 copy-start.13
  16.8 0.0 copy-start.14
  16.8 0.0 copy-start.15
  16.8 0.0 copy-start.16
  16.9 1.0 %all-to-all-done.qc_ref = f32[32,2,384]{2,1,0:T(2,128)S(1)} async-done(((f32[32,2,384]{2,1,0:T(2,128)}), f32[32,2,384]{2,1,0:T(2,128)S(1)}, u32[]{:S(2)}, u32[]{:S(2)}) %all-to-all-start) | async-done | bytes 98336 | tf_op jit(solution)/shard_map/all_to_all | solution.py:516
  17.9 3.1 %collective-permute-start.3 = (bf16[3,272,128]{2,1,0:T(8,128)(2,1)S(1)}, bf16[3,272,128]{2,1,0:T(8,128)(2,1)S(1)}, u32[]{:S(2)}, u32[]{:S(2)}) collective-permute-start(bf16[3,272,128]{2,1,0:T(8,128)(2,1)S(1)} %pad_maximum_fusion.mid_ref), channel_id=1, source_target_pairs={{0,7},{1,0},{2,1},{3,2},{4,3},{5,4},{6,5},{7,6},{8,15},{9,8},{10,9... | collective-permute-start | bytes 626696 | tf_op jit(solution)/shard_map/ppermute | solution.py:504
  21.0 0.0 collective-permute-start.2
  21.0 0.0 copy-done.13
  21.0 0.0 copy-done.14
  21.0 0.0 copy-done.15
  21.0 0.0 copy-done.16
  21.0 0.0 copy-start.8
  21.0 0.0 copy-start.9
  21.0 0.0 copy-start.11
  21.0 0.0 copy-start.12
  21.1 9.1 %grid_fields.1 = f32[32,3,1,384]{3,2,1,0:T(1,128)} custom-call(s32[1]{0:T(128)} %bitcast.11.place_ref, f32[32,2,384]{2,1,0:T(2,128)S(1)} %all-to-all-done.qc_ref, f32[64,192]{1,0:T(8,128)S(1)} %copy-done.14, f32[32,96]{1,0:T(8,128)S(1)} %copy-done.16, f32[64,96]{1,0:T(8,128)S(1)} %copy-done.15, f32[128,192]{1,0:T(8,128)S(1)} %copy-done.13), custom_call_target="tpu_custom_call" | custom-call | flops 8000000000 | bytes 4000000 | tf_op jit(solution)/shard_map/grid_fields/pallas_call | solution.py:287
  30.1 0.0 copy-start.7
  30.1 0.0 copy-start.10
  30.1 6.0 %all-to-all-start.1 = ((f32[32,3,1,384]{3,2,1,0:T(1,128)}), f32[32,3,1,384]{3,2,1,0:T(1,128)S(1)}, u32[]{:S(2)}, u32[]{:S(2)}) async-start(f32[32,3,1,384]{3,2,1,0:T(1,128)} %grid_fields.1), calls=%async_computation.1 | async-start | bytes 294912 | tf_op jit(solution)/shard_map/all_to_all | solution.py:525
  36.1 0.0 collective-permute-done.3.down_ref
  36.1 0.0 collective-permute-done.2.up_ref
  36.1 0.0 copy-done.8
  36.1 0.0 copy-done.9
  36.1 0.0 copy-done.11
  36.1 0.0 copy-done.12
  36.2 0.0 copy-done.7
  36.2 0.0 copy-done.10
  36.2 38.6 %edge_forces.1 = f32[3,1,384]{2,1,0:T(1,128)S(1)} custom-call(s32[12288]{0:T(1024)S(1)} %reshape.46.list_ref, s32[32,384]{1,0:T(8,128)S(1)} %bitcast.23, bf16[384,128]{1,0:T(8,128)(2,1)S(1)} %bitcast.20, bf16[3,384]{1,0:T(4,128)(2,1)S(1)} %bitcast.25, bf16[3,272,128]{2,1,0:T(8,128)(2,1)S(1)} %pad_maximum_fusion.mid_ref, ...), custom_call_target="tpu_custom_call" | custom-call | flops 6442450944 | bytes 4000000 | tf_op jit(solution)/shard_map/edge_forces/pallas_call | solution.py:473
  74.8 0.0 all-to-all-done.1
  74.8 0.1 reduce_sum.11
  75.0 0.6 fusion
  (3 shorter events, 0.0 us)
Async XLA Ops:
  0.7 0.7 copy-start.4
  0.7 0.7 copy-start.6
  1.3 0.9 %copy-start = (bf16[1,1,384,128]{3,2,1,0:T(8,128)(2,1)S(1)}, bf16[1,1,384,128]{3,2,1,0:T(8,128)(2,1)}, u32[]{:S(2)}) copy-start(bf16[1,1,384,128]{3,2,1,0:T(8,128)(2,1)} %param.17) | copy-start | bytes 294916
  3.0 7.3 %copy-start.1 = (bf16[1,1,384,128]{3,2,1,0:T(8,128)(2,1)S(1)}, bf16[1,1,384,128]{3,2,1,0:T(8,128)(2,1)}, u32[]{:S(2)}) copy-start(bf16[1,1,384,128]{3,2,1,0:T(8,128)(2,1)} %param.17) | copy-start | bytes 294916
  3.0 7.3 %copy-start.5 = (s32[1,1,256]{2,1,0:T(1,128)S(1)}, s32[1,1,256]{2,1,0:T(1,128)}, u32[]{:S(2)}) copy-start(s32[1,1,256]{2,1,0:T(1,128)} %param.20) | copy-start | bytes 3076
  3.0 14.9 %all-to-all-start = ((f32[32,2,384]{2,1,0:T(2,128)}), f32[32,2,384]{2,1,0:T(2,128)S(1)}, u32[]{:S(2)}, u32[]{:S(2)}) async-start(f32[32,2,384]{2,1,0:T(2,128)} %charges.1.after_ref), calls=%async_computation | async-start | bytes 196608 | tf_op jit(solution)/shard_map/all_to_all | solution.py:516
  10.3 0.7 copy-start.3
  11.0 2.5 %copy-start.2 = (s32[1,1,384,32]{2,3,1,0:T(8,128)S(1)}, s32[1,1,384,32]{2,3,1,0:T(8,128)}, u32[]{:S(2)}) copy-start(s32[1,1,384,32]{2,3,1,0:T(8,128)} %param.21) | copy-start | bytes 147460
  11.3 4.4 %collective-permute-start.1 = (bf16[272,128]{1,0:T(8,128)(2,1)S(1)}, bf16[272,128]{1,0:T(8,128)(2,1)S(1)}, u32[]{:S(2)}, u32[]{:S(2)}) collective-permute-start(bf16[272,128]{1,0:T(8,128)(2,1)S(1)} %exports.1), channel_id=1, source_target_pairs={{0,24},{8,0},{16,8},{24,16},{1,25},{9,1},{17,9},{25,17},{2,26},{10... | collective-permute-start | bytes 208904 | tf_op jit(solution)/shard_map/ppermute | solution.py:504
  12.9 4.0 %collective-permute-start = (bf16[272,128]{1,0:T(8,128)(2,1)S(1)}, bf16[272,128]{1,0:T(8,128)(2,1)S(1)}, u32[]{:S(2)}, u32[]{:S(2)}) collective-permute-start(bf16[272,128]{1,0:T(8,128)(2,1)S(1)} %exports.1), channel_id=1, source_target_pairs={{0,8},{8,16},{16,24},{24,0},{1,9},{9,17},{17,25},{25,1},{2,10},{10... | collective-permute-start | bytes 208904 | tf_op jit(solution)/shard_map/ppermute | solution.py:504
  16.8 4.2 %copy-start.13 = (f32[128,192]{1,0:T(8,128)S(1)}, f32[128,192]{1,0:T(8,128)}, u32[]{:S(2)}) copy-start(f32[128,192]{1,0:T(8,128)} %constant.24.clone.iy_ref) | copy-start | bytes 294916
  16.8 4.2 %copy-start.14 = (f32[64,192]{1,0:T(8,128)S(1)}, f32[64,192]{1,0:T(8,128)}, u32[]{:S(2)}) copy-start(f32[64,192]{1,0:T(8,128)} %constant.21.clone.fy_ref) | copy-start | bytes 147460
  16.8 4.2 %copy-start.15 = (f32[64,96]{1,0:T(8,128)S(1)}, f32[64,96]{1,0:T(8,128)}, u32[]{:S(2)}) copy-start(f32[64,96]{1,0:T(8,128)} %constant.23.clone.ix_ref) | copy-start | bytes 73732
  16.8 4.2 %copy-start.16 = (f32[32,96]{1,0:T(8,128)S(1)}, f32[32,96]{1,0:T(8,128)}, u32[]{:S(2)}) copy-start(f32[32,96]{1,0:T(8,128)} %constant.22.clone.fx_ref) | copy-start | bytes 36868
  17.9 18.2 %collective-permute-start.3 = (bf16[3,272,128]{2,1,0:T(8,128)(2,1)S(1)}, bf16[3,272,128]{2,1,0:T(8,128)(2,1)S(1)}, u32[]{:S(2)}, u32[]{:S(2)}) collective-permute-start(bf16[3,272,128]{2,1,0:T(8,128)(2,1)S(1)} %pad_maximum_fusion.mid_ref), channel_id=1, source_target_pairs={{0,7},{1,0},{2,1},{3,2},{4,3},{5,4},{6,5},{7,6},{8,15},{9,8},{10,9... | collective-permute-start | bytes 626696 | tf_op jit(solution)/shard_map/ppermute | solution.py:504
  21.0 15.1 %collective-permute-start.2 = (bf16[3,272,128]{2,1,0:T(8,128)(2,1)S(1)}, bf16[3,272,128]{2,1,0:T(8,128)(2,1)S(1)}, u32[]{:S(2)}, u32[]{:S(2)}) collective-permute-start(bf16[3,272,128]{2,1,0:T(8,128)(2,1)S(1)} %pad_maximum_fusion.mid_ref), channel_id=1, source_target_pairs={{0,1},{1,2},{2,3},{3,4},{4,5},{5,6},{6,7},{7,0},{8,9},{9,10},{10,1... | collective-permute-start | bytes 626696 | tf_op jit(solution)/shard_map/ppermute | solution.py:504
  21.0 15.1 %copy-start.8 = (bf16[1024,128]{1,0:T(8,128)(2,1)S(1)}, bf16[1024,128]{1,0:T(8,128)(2,1)}, u32[]{:S(2)}) copy-start(bf16[1024,128]{1,0:T(8,128)(2,1)} %w_contract_ref.1) | copy-start | bytes 786436
  21.0 15.1 %copy-start.9 = (bf16[128,256]{1,0:T(8,128)(2,1)S(1)}, bf16[128,256]{1,0:T(8,128)(2,1)}, u32[]{:S(2)}) copy-start(bf16[128,256]{1,0:T(8,128)(2,1)} %w_pair_ref.1) | copy-start | bytes 196612
  21.0 15.1 %copy-start.11 = (bf16[128,128]{1,0:T(8,128)(2,1)S(1)}, bf16[128,128]{1,0:T(8,128)(2,1)}, u32[]{:S(2)}) copy-start(bf16[128,128]{1,0:T(8,128)(2,1)} %w_final_ref.1) | copy-start | bytes 98308
  21.0 15.1 %copy-start.12 = (f32[8,128]{1,0:T(8,128)S(1)}, f32[8,128]{1,0:T(8,128)}, u32[]{:S(2)}) copy-start(f32[8,128]{1,0:T(8,128)} %w_radial_ref.1) | copy-start | bytes 12292
  30.1 6.0 %copy-start.7 = (bf16[128,1024]{1,0:T(8,128)(2,1)S(1)}, bf16[128,1024]{1,0:T(8,128)(2,1)}, u32[]{:S(2)}) copy-start(bf16[128,1024]{1,0:T(8,128)(2,1)} %w_expand_ref.1) | copy-start | bytes 786436
  30.1 6.0 %copy-start.10 = (bf16[128,128]{1,0:T(8,128)(2,1)S(1)}, bf16[128,128]{1,0:T(8,128)(2,1)}, u32[]{:S(2)}) copy-start(bf16[128,128]{1,0:T(8,128)(2,1)} %w_self_ref.1) | copy-start | bytes 98308
  30.1 44.7 %all-to-all-start.1 = ((f32[32,3,1,384]{3,2,1,0:T(1,128)}), f32[32,3,1,384]{3,2,1,0:T(1,128)S(1)}, u32[]{:S(2)}, u32[]{:S(2)}) async-start(f32[32,3,1,384]{3,2,1,0:T(1,128)} %grid_fields.1), calls=%async_computation.1 | async-start | bytes 294912 | tf_op jit(solution)/shard_map/all_to_all | solution.py:525

commit v10 on v9

--- a/solution.py
+++ b/solution.py
@@ -22,7 +22,6 @@
 GROUPS = LANES // ROWS
 CHUNK_ATOMS = 16
 PIECES = 4
-TILES = 2
 HIGHEST = lax.Precision.HIGHEST
 F32 = jnp.float32
 BF16 = jnp.bfloat16
@@ -68,7 +67,7 @@
         in_specs=[pl.BlockSpec(memory_space=pltpu.SMEM)] + [vmem] * 3,
         out_specs=vmem,
         out_shape=jax.ShapeDtypeStruct((devices, 2, feat.shape[0]), F32),
-        compiler_params=pltpu.CompilerParams(vmem_limit_bytes=16 << 20),
+        compiler_params=pltpu.CompilerParams(vmem_limit_bytes=60 << 20),
         name="charges",
     )(count, feat, cells[None], w_charge[None])
 
@@ -306,7 +305,8 @@
 def edge_kernel(
     list_ref, index_ref, feat_ref, pos_ref, mid_ref, up_ref, down_ref, w_self_ref, w_pair_ref,
     w_radial_ref, w_expand_ref, w_contract_ref, w_final_ref, out_ref,
-    table, places, near_a, near_b, near_c, edge_a, edge_b, edge_c, marks, own_ref, sums_ref,
+    table, places, near_a, near_b, near_c, edge_a, edge_b, edge_c,
+    total_a, total_b, total_c, marks, own_ref, sums_ref, w_half,
 ):
     atoms, channels = feat_ref.shape
     ghosts = mid_ref.shape[1] - EXTRA
@@ -317,8 +317,9 @@
     basis_count = w_radial_ref.shape[0]
     spacing = CUTOFF_SQ / (basis_count - 1)
     latent = w_expand_ref.shape[1]
-    width = latent // TILES
+    width = latent // PIECES
     slots = per_atom // PIECES
+    w_half[...] = w_expand_ref[...] * 0.5
 
     def fill(start, rows, coords, shift):
         count = rows.shape[0]
@@ -389,6 +390,12 @@
         [high, high, w_radial - high, jnp.zeros((8, channels), F32)], axis=0
     ).astype(BF16)
 
+    part_rows = slots * CHUNK_ATOMS
+    shape = (slots, CHUNK_ATOMS, LANES)
+
+    def atoms_of(index):
+        return pl.ds(pl.multiple_of(index * CHUNK_ATOMS, 16), CHUNK_ATOMS)
+
     def gather(index, near, part):
         for k in range(part * slots, (part + 1) * slots):
             start = k * atoms + index * CHUNK_ATOMS
@@ -397,58 +404,75 @@
                 near[pl.ds(k * CHUNK_ATOMS + a, 2, stride=chunk), :] = tile[:2]
 
     def enter(index, near, edge_in, part):
-        first = pl.multiple_of(index * CHUNK_ATOMS, 8)
-        rows = pl.ds(part * slots * CHUNK_ATOMS, slots * CHUNK_ATOMS)
-        shape = (slots, CHUNK_ATOMS, LANES)
-        basis = marks[pl.ds(part * slots, slots), pl.ds(first, CHUNK_ATOMS), :]
-        basis = basis.reshape(slots * CHUNK_ATOMS, basis.shape[2]).astype(BF16)
+        rows = pl.ds(part * part_rows, part_rows)
+        basis = marks[pl.ds(part * slots, slots), atoms_of(index), :]
+        basis = basis.reshape(part_rows, basis.shape[2]).astype(BF16)
         radial = jnp.dot(basis, w_basis, preferred_element_type=F32).reshape(shape)
-        own = own_ref[pl.ds(first, CHUNK_ATOMS), :][None]
-        half = radial + own + near[rows, :].reshape(shape)
+        half = radial + own_ref[atoms_of(index), :][None] + near[rows, :].reshape(shape)
         turn = jnp.tanh(half.astype(BF16)).astype(F32)
-        edge_in[rows, :] = (half + half * turn).astype(BF16).reshape(-1, LANES)
-
-    def network(edge_in, part):
+        edge_in[rows, :] = (half + half * turn).astype(BF16).reshape(part_rows, LANES)
+
+    def expand(edge_in, part):
         cols = pl.ds(part * width, width)
-        full = jnp.dot(edge_in[...], w_expand_ref[:, cols], preferred_element_type=F32)
-        decay = jnp.exp(jnp.minimum(-full, 80.0))
-        hidden = (full * pl.reciprocal(1.0 + decay, approx=True)).astype(BF16)
+        return jnp.dot(edge_in[...], w_half[:, cols], preferred_element_type=F32).astype(BF16)
+
+    def contract(half, part):
+        hidden = half + half * jnp.tanh(half)
+        cols = pl.ds(part * width, width)
         return jnp.dot(hidden, w_contract_ref[cols, :], preferred_element_type=F32)
 
-    def collect(index, mixed, near):
-        first = pl.multiple_of(index * CHUNK_ATOMS, 8)
-        weight = (mixed * near[pl.ds(chunk, chunk), :]).reshape(per_atom, CHUNK_ATOMS, LANES)
+    def collect(index, near, total, part, before):
+        rows = pl.ds(part * part_rows, part_rows)
+        other = pl.ds(chunk + part * part_rows, part_rows)
+        weight = (total[rows, :] * near[other, :]).reshape(shape)
+        after = []
         for s in range(4):
-            mark = marks[:, pl.ds(first, CHUNK_ATOMS), 3 * basis_count + s : 3 * basis_count + s + 1]
-            sums_ref[s, pl.ds(first, CHUNK_ATOMS), :] = jnp.sum(weight * mark, axis=0)
-
-    def stage(index, nears, edges):
+            column = 3 * basis_count + s
+            mark = marks[pl.ds(part * slots, slots), atoms_of(index), column : column + 1]
+            summed = jnp.sum(weight * mark, axis=0)
+            after.append(summed if before is None else before[s] + summed)
+        return after
+
+    def keep(index, sums):
+        for s in range(4):
+            sums_ref[s, atoms_of(index), :] = sums[s]
+
+    def stage(index, nears, edges, totals):
         after = jnp.minimum(index + 1, chunks - 1)
-        later = jnp.minimum(index + 2, chunks - 1)
-        mixed = None
+        before = jnp.maximum(index - 1, 0)
+        mixed, sums = (None, None)
+        half = expand(edges[0], 0)
         for part in range(PIECES):
-            gather(later, nears[2], part)
+            gather(after, nears[1], part)
+            following = expand(edges[0], part + 1) if part + 1 < PIECES else None
+            sums = collect(before, nears[2], totals[2], part, sums)
+            term = contract(half, part)
+            mixed = term if mixed is None else mixed + term
             enter(after, nears[1], edges[1], part)
-            if part % (PIECES // TILES) == PIECES // TILES - 1:
-                term = network(edges[0], part // (PIECES // TILES))
-                mixed = term if mixed is None else mixed + term
-        collect(index, mixed, nears[0])
+            half = following
+        totals[0][...] = mixed
+        keep(before, sums)
 
     nears = (near_a, near_b, near_c)
     edges = (edge_a, edge_b, edge_c)
+    totals = (total_a, total_b, total_c)
     for part in range(PIECES):
         gather(0, near_a, part)
     for part in range(PIECES):
-        gather(1, near_b, part)
         enter(0, near_a, edge_a, part)
 
     def triple(step, carry):
         for i in range(3):
             order = (i, (i + 1) % 3, (i + 2) % 3)
-            stage(3 * step + i, [nears[o] for o in order], [edges[o] for o in order])
+            pick = lambda refs: [refs[o] for o in order]
+            stage(3 * step + i, pick(nears), pick(edges), pick(totals))
         return carry
 
     lax.fori_loop(0, chunks // 3, triple, 0)
+    sums = None
+    for part in range(PIECES):
+        sums = collect(chunks - 1, near_c, total_c, part, sums)
+    keep(chunks - 1, sums)
 
     scale = 1.0 / math.sqrt(per_atom)
     vector = [sums_ref[1 + a] * scale for a in range(3)]
@@ -481,10 +505,12 @@
         ]
         + [pltpu.VMEM((2 * chunk, LANES), F32)] * 3
         + [pltpu.VMEM((chunk, LANES), BF16)] * 3
+        + [pltpu.VMEM((chunk, LANES), F32)] * 3
         + [
             pltpu.VMEM((per_atom, atoms, 32), F32),
             pltpu.VMEM((atoms, LANES), F32),
             pltpu.VMEM((4, atoms, LANES), F32),
+            pltpu.VMEM(w_expand.shape, BF16),
         ],
         compiler_params=pltpu.CompilerParams(vmem_limit_bytes=32 << 20),
         cost_estimate=pl.CostEstimate(

time: 75.9 us -> 70.4 us (0.928)
  Pallas kernels: 48.8 us -> 44.8 us
  local copies, waits for them, and re-layouts: 2.98 us -> 0.74 us
    pallas_call x1, Pallas kernels: 38.6 us -> 33.8 us  [edge_forces(): pl.pallas_call(edge_kernel, in_specs=[pl.BlockSpec(memory_space=pltpu.SME...]
    unnamed x34 -> x30, local copies, waits for them, and re-layouts: 2.28 us -> 0.71 us
    pallas_call x1, Pallas kernels: 0.8 us -> 1.72 us  [charges(): pl.pallas_call(charge_kernel, in_specs=[pl.BlockSpec(memory_space=pltpu.S...]
  transfers between devices with their start and end apart: 6 -> 6, of which waited for: 3 -> 3; matrix products, arithmetic and copies ran while one was open for 1% -> 0% of each run, Pallas kernels for 63% -> 62%
where the time goes in v10:
time: 70.4 us; the launch traced here: 70.1 us
  Pallas kernels  44.8 us (64%)
  starting transfers between devices  17.9 us (25%)
  waiting for transfers between devices  4.92 us (7%)
  between operations  0.88 us (1%)
  other arithmetic  0.77 us (1%)
  local copies, waits for them, and re-layouts  0.74 us (1%)
    pallas_call x1, Pallas kernels, edge_forces(): pl.pallas_call(edge_kernel, in_specs=[pl.BlockSpec(memory_space=pltpu.SME...  33.8 us
    pallas_call x1, Pallas kernels, grid_fields(): pl.pallas_call(functools.partial(grid_kernel, cycle_x, cycle_y), in_specs...  9.06 us
    all_to_all x1, starting transfers between devices, shards(): lax.all_to_all(spread, ('dx', 'dy'), split_axis=0, concat_axis=0, tiled=T...  7.3 us
    all_to_all x1, starting transfers between devices, shards(): lax.all_to_all(partial, ('dx', 'dy'), split_axis=0, concat_axis=0, tiled=...  5.95 us
    ppermute x4, starting transfers between devices, ring(): lax.ppermute(array, axis, [(i, (i + step) % size) for i in range(size)])  4.67 us
    ppermute x4, waiting for transfers between devices, ring(): lax.ppermute(array, axis, [(i, (i + step) % size) for i in range(size)])  3.9 us
    pallas_call x1, Pallas kernels, charges(): pl.pallas_call(charge_kernel, in_specs=[pl.BlockSpec(memory_space=pltpu.S...  1.72 us
  transfers between devices with their start and end apart: 6, of which 3 were waited for; matrix products, arithmetic and copies ran while one was open for 0% of the time, Pallas kernels for 62%

profile of v10, /device:TPU:0, one launch (start us, length us, event | category | flops | bytes accessed | tf_op | source)
XLA Modules:
  0.0 70.1 jit_solution(10664342725013598710)
XLA Ops:
  0.7 0.0 copy-start.4
  0.7 1.7 %charges.1.after_ref = f32[32,2,384]{2,1,0:T(2,128)} custom-call(s32[1,1]{1,0:T(1,128)} %copy.19.count_ref, bf16[384,128]{1,0:T(8,128)(2,1)} %bitcast.18, s32[1,384]{1,0:T(1,128)} %bitcast.29, bf16[1,128]{1,0:T(2,128)(2,1)} %bitcast.30), custom_call_target="tpu_custom_call" | custom-call | tf_op jit(solution)/shard_map/charges/pallas_call | solution.py:65
  2.4 0.0 copy-start
  2.4 0.0 copy-start.1
  2.4 7.3 %all-to-all-start = ((f32[32,2,384]{2,1,0:T(2,128)}), f32[32,2,384]{2,1,0:T(2,128)S(1)}, u32[]{:S(2)}, u32[]{:S(2)}) async-start(f32[32,2,384]{2,1,0:T(2,128)} %charges.1.after_ref), calls=%async_computation | async-start | bytes 196608 | tf_op jit(solution)/shard_map/all_to_all | solution.py:542
  9.7 0.0 copy-start.3
  9.7 0.0 copy-done.4
  9.7 0.0 copy-done
  9.7 0.0 copy-done.1
  9.7 0.6 copy-done.3
  10.4 0.0 copy-start.2
  10.4 0.3 exports.1
  10.7 1.6 %collective-permute-start.1 = (bf16[272,128]{1,0:T(8,128)(2,1)S(1)}, bf16[272,128]{1,0:T(8,128)(2,1)S(1)}, u32[]{:S(2)}, u32[]{:S(2)}) collective-permute-start(bf16[272,128]{1,0:T(8,128)(2,1)S(1)} %exports.1), channel_id=1, source_target_pairs={{0,24},{8,0},{16,8},{24,16},{1,25},{9,1},{17,9},{25,17},{2,26},{10... | collective-permute-start | bytes 208904 | tf_op jit(solution)/shard_map/ppermute | solution.py:530
  12.2 0.0 collective-permute-start
  12.3 0.0 copy-done.2
  12.3 2.7 %collective-permute-done.1 = bf16[272,128]{1,0:T(8,128)(2,1)S(1)} collective-permute-done((bf16[272,128]{1,0:T(8,128)(2,1)S(1)}, bf16[272,128]{1,0:T(8,128)(2,1)S(1)}, u32[]{:S(2)}, u32[]{:S(2)}) %collective-permute-start.1) | collective-permute-done | bytes 69664 | tf_op jit(solution)/shard_map/ppermute | solution.py:530
  15.0 1.2 %collective-permute-done = bf16[272,128]{1,0:T(8,128)(2,1)S(1)} collective-permute-done((bf16[272,128]{1,0:T(8,128)(2,1)S(1)}, bf16[272,128]{1,0:T(8,128)(2,1)S(1)}, u32[]{:S(2)}, u32[]{:S(2)}) %collective-permute-start) | collective-permute-done | bytes 69664 | tf_op jit(solution)/shard_map/ppermute | solution.py:530
  16.2 0.0 copy-start.11
  16.2 0.0 copy-start.12
  16.2 0.0 copy-start.13
  16.2 0.0 copy-start.14
  16.2 1.0 %all-to-all-done.qc_ref = f32[32,2,384]{2,1,0:T(2,128)S(1)} async-done(((f32[32,2,384]{2,1,0:T(2,128)}), f32[32,2,384]{2,1,0:T(2,128)S(1)}, u32[]{:S(2)}, u32[]{:S(2)}) %all-to-all-start) | async-done | bytes 98336 | tf_op jit(solution)/shard_map/all_to_all | solution.py:542
  17.3 3.1 %collective-permute-start.3 = (bf16[3,272,128]{2,1,0:T(8,128)(2,1)S(1)}, bf16[3,272,128]{2,1,0:T(8,128)(2,1)S(1)}, u32[]{:S(2)}, u32[]{:S(2)}) collective-permute-start(bf16[3,272,128]{2,1,0:T(8,128)(2,1)S(1)} %pad_maximum_fusion.mid_ref), channel_id=1, source_target_pairs={{0,7},{1,0},{2,1},{3,2},{4,3},{5,4},{6,5},{7,6},{8,15},{9,8},{10,9... | collective-permute-start | bytes 626696 | tf_op jit(solution)/shard_map/ppermute | solution.py:530
  20.3 0.0 collective-permute-start.2
  20.3 0.0 copy-done.11
  20.4 0.0 copy-done.12
  20.4 0.0 copy-done.13
  20.4 0.0 copy-done.14
  20.4 0.0 copy-start.6
  20.4 0.0 copy-start.7
  20.4 0.0 copy-start.9
  20.4 0.0 copy-start.10
  20.4 9.1 %grid_fields.1 = f32[32,3,1,384]{3,2,1,0:T(1,128)} custom-call(s32[1]{0:T(128)} %bitcast.11.place_ref, f32[32,2,384]{2,1,0:T(2,128)S(1)} %all-to-all-done.qc_ref, f32[64,192]{1,0:T(8,128)S(1)} %copy-done.12, f32[32,96]{1,0:T(8,128)S(1)} %copy-done.14, f32[64,96]{1,0:T(8,128)S(1)} %copy-done.13, f32[128,192]{1,0:T(8,128)S(1)} %copy-done.11), custom_call_target="tpu_custom_call" | custom-call | flops 8000000000 | bytes 4000000 | tf_op jit(solution)/shard_map/grid_fields/pallas_call | solution.py:286
  29.5 0.0 copy-start.5
  29.5 0.0 copy-start.8
  29.5 6.0 %all-to-all-start.1 = ((f32[32,3,1,384]{3,2,1,0:T(1,128)}), f32[32,3,1,384]{3,2,1,0:T(1,128)S(1)}, u32[]{:S(2)}, u32[]{:S(2)}) async-start(f32[32,3,1,384]{3,2,1,0:T(1,128)} %grid_fields.1), calls=%async_computation.1 | async-start | bytes 294912 | tf_op jit(solution)/shard_map/all_to_all | solution.py:551
  35.4 0.0 collective-permute-done.3.down_ref
  35.5 0.0 collective-permute-done.2.up_ref
  35.5 0.0 copy-done.6
  35.5 0.0 copy-done.7
  35.5 0.0 copy-done.9
  35.5 0.0 copy-done.10
  35.5 0.0 copy-done.5
  35.5 0.0 copy-done.8
  35.5 33.8 %edge_forces.1 = f32[3,1,384]{2,1,0:T(1,128)S(1)} custom-call(s32[12288]{0:T(1024)S(1)} %reshape.46.list_ref, s32[32,384]{1,0:T(8,128)S(1)} %bitcast.23, bf16[384,128]{1,0:T(8,128)(2,1)S(1)} %bitcast.20, bf16[3,384]{1,0:T(4,128)(2,1)S(1)} %bitcast.25, bf16[3,272,128]{2,1,0:T(8,128)(2,1)S(1)} %pad_maximum_fusion.mid_ref, ...), custom_call_target="tpu_custom_call" | custom-call | flops 6442450944 | bytes 4000000 | tf_op jit(solution)/shard_map/edge_forces/pallas_call | solution.py:497
  69.3 0.0 all-to-all-done.1
  69.3 0.1 reduce_sum.11
  69.5 0.6 fusion
  (4 shorter events, 0.1 us)
Async XLA Ops:
  0.7 9.1 %copy-start.4 = (s32[1,1,256]{2,1,0:T(1,128)S(1)}, s32[1,1,256]{2,1,0:T(1,128)}, u32[]{:S(2)}) copy-start(s32[1,1,256]{2,1,0:T(1,128)} %param.20) | copy-start | bytes 3076
  2.4 7.3 %copy-start = (f32[32,2,384]{2,1,0:T(2,128)S(1)}, f32[32,2,384]{2,1,0:T(2,128)}, u32[]{:S(2)}) copy-start(f32[32,2,384]{2,1,0:T(2,128)} %charges.1.after_ref) | copy-start | bytes 294916
  2.4 7.3 %copy-start.1 = (bf16[1,1,384,128]{3,2,1,0:T(8,128)(2,1)S(1)}, bf16[1,1,384,128]{3,2,1,0:T(8,128)(2,1)}, u32[]{:S(2)}) copy-start(bf16[1,1,384,128]{3,2,1,0:T(8,128)(2,1)} %param.17) | copy-start | bytes 294916
  2.4 14.9 %all-to-all-start = ((f32[32,2,384]{2,1,0:T(2,128)}), f32[32,2,384]{2,1,0:T(2,128)S(1)}, u32[]{:S(2)}, u32[]{:S(2)}) async-start(f32[32,2,384]{2,1,0:T(2,128)} %charges.1.after_ref), calls=%async_computation | async-start | bytes 196608 | tf_op jit(solution)/shard_map/all_to_all | solution.py:542
  9.7 0.7 copy-start.3
  10.4 1.9 %copy-start.2 = (s32[1,1,384,32]{2,3,1,0:T(8,128)S(1)}, s32[1,1,384,32]{2,3,1,0:T(8,128)}, u32[]{:S(2)}) copy-start(s32[1,1,384,32]{2,3,1,0:T(8,128)} %param.21) | copy-start | bytes 147460
  10.7 4.4 %collective-permute-start.1 = (bf16[272,128]{1,0:T(8,128)(2,1)S(1)}, bf16[272,128]{1,0:T(8,128)(2,1)S(1)}, u32[]{:S(2)}, u32[]{:S(2)}) collective-permute-start(bf16[272,128]{1,0:T(8,128)(2,1)S(1)} %exports.1), channel_id=1, source_target_pairs={{0,24},{8,0},{16,8},{24,16},{1,25},{9,1},{17,9},{25,17},{2,26},{10... | collective-permute-start | bytes 208904 | tf_op jit(solution)/shard_map/ppermute | solution.py:530
  12.2 4.0 %collective-permute-start = (bf16[272,128]{1,0:T(8,128)(2,1)S(1)}, bf16[272,128]{1,0:T(8,128)(2,1)S(1)}, u32[]{:S(2)}, u32[]{:S(2)}) collective-permute-start(bf16[272,128]{1,0:T(8,128)(2,1)S(1)} %exports.1), channel_id=1, source_target_pairs={{0,8},{8,16},{16,24},{24,0},{1,9},{9,17},{17,25},{25,1},{2,10},{10... | collective-permute-start | bytes 208904 | tf_op jit(solution)/shard_map/ppermute | solution.py:530
  16.2 4.2 %copy-start.11 = (f32[128,192]{1,0:T(8,128)S(1)}, f32[128,192]{1,0:T(8,128)}, u32[]{:S(2)}) copy-start(f32[128,192]{1,0:T(8,128)} %constant.24.clone.iy_ref) | copy-start | bytes 294916
  16.2 4.2 %copy-start.12 = (f32[64,192]{1,0:T(8,128)S(1)}, f32[64,192]{1,0:T(8,128)}, u32[]{:S(2)}) copy-start(f32[64,192]{1,0:T(8,128)} %constant.21.clone.fy_ref) | copy-start | bytes 147460
  16.2 4.2 %copy-start.13 = (f32[64,96]{1,0:T(8,128)S(1)}, f32[64,96]{1,0:T(8,128)}, u32[]{:S(2)}) copy-start(f32[64,96]{1,0:T(8,128)} %constant.23.clone.ix_ref) | copy-start | bytes 73732
  16.2 4.2 %copy-start.14 = (f32[32,96]{1,0:T(8,128)S(1)}, f32[32,96]{1,0:T(8,128)}, u32[]{:S(2)}) copy-start(f32[32,96]{1,0:T(8,128)} %constant.22.clone.fx_ref) | copy-start | bytes 36868
  17.3 18.2 %collective-permute-start.3 = (bf16[3,272,128]{2,1,0:T(8,128)(2,1)S(1)}, bf16[3,272,128]{2,1,0:T(8,128)(2,1)S(1)}, u32[]{:S(2)}, u32[]{:S(2)}) collective-permute-start(bf16[3,272,128]{2,1,0:T(8,128)(2,1)S(1)} %pad_maximum_fusion.mid_ref), channel_id=1, source_target_pairs={{0,7},{1,0},{2,1},{3,2},{4,3},{5,4},{6,5},{7,6},{8,15},{9,8},{10,9... | collective-permute-start | bytes 626696 | tf_op jit(solution)/shard_map/ppermute | solution.py:530
  20.3 15.1 %collective-permute-start.2 = (bf16[3,272,128]{2,1,0:T(8,128)(2,1)S(1)}, bf16[3,272,128]{2,1,0:T(8,128)(2,1)S(1)}, u32[]{:S(2)}, u32[]{:S(2)}) collective-permute-start(bf16[3,272,128]{2,1,0:T(8,128)(2,1)S(1)} %pad_maximum_fusion.mid_ref), channel_id=1, source_target_pairs={{0,1},{1,2},{2,3},{3,4},{4,5},{5,6},{6,7},{7,0},{8,9},{9,10},{10,1... | collective-permute-start | bytes 626696 | tf_op jit(solution)/shard_map/ppermute | solution.py:530
  20.4 15.1 %copy-start.6 = (bf16[1024,128]{1,0:T(8,128)(2,1)S(1)}, bf16[1024,128]{1,0:T(8,128)(2,1)}, u32[]{:S(2)}) copy-start(bf16[1024,128]{1,0:T(8,128)(2,1)} %w_contract_ref.1) | copy-start | bytes 786436
  20.4 15.1 %copy-start.7 = (bf16[128,256]{1,0:T(8,128)(2,1)S(1)}, bf16[128,256]{1,0:T(8,128)(2,1)}, u32[]{:S(2)}) copy-start(bf16[128,256]{1,0:T(8,128)(2,1)} %w_pair_ref.1) | copy-start | bytes 196612
  20.4 15.1 %copy-start.9 = (bf16[128,128]{1,0:T(8,128)(2,1)S(1)}, bf16[128,128]{1,0:T(8,128)(2,1)}, u32[]{:S(2)}) copy-start(bf16[128,128]{1,0:T(8,128)(2,1)} %w_final_ref.1) | copy-start | bytes 98308
  20.4 15.1 %copy-start.10 = (f32[8,128]{1,0:T(8,128)S(1)}, f32[8,128]{1,0:T(8,128)}, u32[]{:S(2)}) copy-start(f32[8,128]{1,0:T(8,128)} %w_radial_ref.1) | copy-start | bytes 12292
  29.5 6.0 %copy-start.5 = (bf16[128,1024]{1,0:T(8,128)(2,1)S(1)}, bf16[128,1024]{1,0:T(8,128)(2,1)}, u32[]{:S(2)}) copy-start(bf16[128,1024]{1,0:T(8,128)(2,1)} %w_expand_ref.1) | copy-start | bytes 786436
  29.5 6.0 %copy-start.8 = (bf16[128,128]{1,0:T(8,128)(2,1)S(1)}, bf16[128,128]{1,0:T(8,128)(2,1)}, u32[]{:S(2)}) copy-start(bf16[128,128]{1,0:T(8,128)(2,1)} %w_self_ref.1) | copy-start | bytes 98308
  29.5 39.8 %all-to-all-start.1 = ((f32[32,3,1,384]{3,2,1,0:T(1,128)}), f32[32,3,1,384]{3,2,1,0:T(1,128)S(1)}, u32[]{:S(2)}, u32[]{:S(2)}) async-start(f32[32,3,1,384]{3,2,1,0:T(1,128)} %grid_fields.1), calls=%async_computation.1 | async-start | bytes 294912 | tf_op jit(solution)/shard_map/all_to_all | solution.py:551

commit v11 on v10

--- a/solution.py
+++ b/solution.py
@@ -303,10 +303,11 @@
 
 
 def edge_kernel(
-    list_ref, index_ref, feat_ref, pos_ref, mid_ref, up_ref, down_ref, w_self_ref, w_pair_ref,
+    list_hbm, index_ref, feat_ref, pos_ref, mid_ref, up_ref, down_ref, w_self_ref, w_pair_ref,
     w_radial_ref, w_expand_ref, w_contract_ref, w_final_ref, out_ref,
     table, places, near_a, near_b, near_c, edge_a, edge_b, edge_c,
     total_a, total_b, total_c, marks, own_ref, sums_ref, w_half,
+    list_ref, list_sem,
 ):
     atoms, channels = feat_ref.shape
     ghosts = mid_ref.shape[1] - EXTRA
@@ -321,13 +322,16 @@
     slots = per_atom // PIECES
     w_half[...] = w_expand_ref[...] * 0.5
 
+    fetch = pltpu.make_async_copy(list_hbm, list_ref, list_sem)
+    fetch.start()
+
     def fill(start, rows, coords, shift):
         count = rows.shape[0]
         projected = jnp.dot(rows, w_pair_ref[...], preferred_element_type=F32)
         projected = projected.astype(BF16).astype(F32)
-        rows_of = table.reshape(slots_all * 8, LANES)
-        rows_of[pl.ds(start * 8, count, stride=8), :] = projected[:, :channels] * 0.5
-        rows_of[pl.ds(start * 8 + 1, count, stride=8), :] = projected[:, channels:]
+        rows_of = table.reshape(slots_all * 2, LANES)
+        rows_of[pl.ds(start * 2, count, stride=2), :] = projected[:, :channels] * 0.5
+        rows_of[pl.ds(start * 2 + 1, count, stride=2), :] = projected[:, channels:]
         row = lax.broadcasted_iota(jnp.int32, (8, LANES), 0)
         offset = jnp.where(row == 0, shift[0], jnp.where(row == 1, shift[1], 0.0))
         places[start // LANES] = coords + offset
@@ -371,24 +375,30 @@
         envelope = jnp.maximum(0.0, 1.0 - d2 * (1.0 / CUTOFF_SQ))
         envelope = envelope * envelope
         moments = [envelope] + [envelope * disp[a] for a in range(3)]
-        for k in range(per_atom):
-            def wide(value):
-                return jnp.broadcast_to(value[k : k + 1], (8, LANES))
-
-            t = wide(d2) * (1.0 / spacing) - feature.astype(F32)
-            basis = jnp.exp(-(t * t))
-            high = basis.astype(BF16).astype(F32)
-            tail = jnp.where(feature == 0, wide(moments[0]), 0.0)
-            for a in range(3):
-                tail = jnp.where(feature == 1 + a, wide(moments[1 + a]), tail)
-            stacked = jnp.concatenate([high, basis - high, high, tail], axis=0)
-            marks[k, pl.ds(i * LANES, LANES), :] = stacked.T
+        for group in range(per_atom // GROUPS):
+            stacked = []
+            for k in range(group * GROUPS, (group + 1) * GROUPS):
+                def wide(value):
+                    return jnp.broadcast_to(value[k : k + 1], (8, LANES))
+
+                t = wide(d2) * (1.0 / spacing) - feature.astype(F32)
+                basis = jnp.exp(-(t * t))
+                high = basis.astype(BF16).astype(F32)
+                tail = jnp.where(feature == 0, wide(moments[0]), 0.0)
+                for a in range(3):
+                    tail = jnp.where(feature == 1 + a, wide(moments[1 + a]), tail)
+                stacked += [high, basis - high, high, tail]
+            marks[group, pl.ds(i * LANES, LANES), :] = jnp.concatenate(stacked, axis=0).T
 
     w_radial = w_radial_ref[...] * 0.5
     high = w_radial.astype(BF16).astype(F32)
-    w_basis = jnp.concatenate(
-        [high, high, w_radial - high, jnp.zeros((8, channels), F32)], axis=0
-    ).astype(BF16)
+    one = jnp.concatenate([high, high, w_radial - high, jnp.zeros((8, channels), F32)], axis=0)
+    none = jnp.zeros((ROWS, channels), F32)
+    blocks = []
+    for g in range(GROUPS):
+        column = [one if other == g else none for other in range(GROUPS)]
+        blocks.append(jnp.concatenate(column, axis=0))
+    w_basis = jnp.concatenate(blocks, axis=1).astype(BF16)
 
     part_rows = slots * CHUNK_ATOMS
     shape = (slots, CHUNK_ATOMS, LANES)
@@ -401,13 +411,20 @@
             start = k * atoms + index * CHUNK_ATOMS
             loaded = [table[list_ref[start + a]] for a in range(CHUNK_ATOMS)]
             for a, tile in enumerate(loaded):
-                near[pl.ds(k * CHUNK_ATOMS + a, 2, stride=chunk), :] = tile[:2]
+                near[pl.ds(k * CHUNK_ATOMS + a, 2, stride=chunk), :] = tile
 
     def enter(index, near, edge_in, part):
         rows = pl.ds(part * part_rows, part_rows)
-        basis = marks[pl.ds(part * slots, slots), atoms_of(index), :]
-        basis = basis.reshape(part_rows, basis.shape[2]).astype(BF16)
-        radial = jnp.dot(basis, w_basis, preferred_element_type=F32).reshape(shape)
+        groups = slots // GROUPS
+        basis = marks[pl.ds(part * groups, groups), atoms_of(index), :]
+        basis = basis.reshape(groups * CHUNK_ATOMS, LANES).astype(BF16)
+        wide = jnp.dot(basis, w_basis, preferred_element_type=F32)
+        pieces = []
+        for q in range(groups):
+            for g in range(GROUPS):
+                rows_q = slice(q * CHUNK_ATOMS, (q + 1) * CHUNK_ATOMS)
+                pieces.append(wide[rows_q, g * LANES : (g + 1) * LANES])
+        radial = jnp.concatenate(pieces, axis=0).reshape(shape)
         half = radial + own_ref[atoms_of(index), :][None] + near[rows, :].reshape(shape)
         turn = jnp.tanh(half.astype(BF16)).astype(F32)
         edge_in[rows, :] = (half + half * turn).astype(BF16).reshape(part_rows, LANES)
@@ -427,9 +444,11 @@
         weight = (total[rows, :] * near[other, :]).reshape(shape)
         after = []
         for s in range(4):
-            column = 3 * basis_count + s
-            mark = marks[pl.ds(part * slots, slots), atoms_of(index), column : column + 1]
-            summed = jnp.sum(weight * mark, axis=0)
+            summed = 0.0
+            for k in range(slots):
+                column = k % GROUPS * ROWS + 3 * basis_count + s
+                tile = marks[(part * slots + k) // GROUPS, atoms_of(index), :]
+                summed = summed + weight[k] * tile[:, column : column + 1]
             after.append(summed if before is None else before[s] + summed)
         return after
 
@@ -456,6 +475,7 @@
     nears = (near_a, near_b, near_c)
     edges = (edge_a, edge_b, edge_c)
     totals = (total_a, total_b, total_c)
+    fetch.wait()
     for part in range(PIECES):
         gather(0, near_a, part)
     for part in range(PIECES):
@@ -496,21 +516,23 @@
     latent = w_expand.shape[1]
     return pl.pallas_call(
         edge_kernel,
-        in_specs=[pl.BlockSpec(memory_space=pltpu.SMEM)] + [vmem] * 12,
+        in_specs=[pl.BlockSpec(memory_space=pl.ANY)] + [vmem] * 12,
         out_specs=vmem,
         out_shape=jax.ShapeDtypeStruct((3, 1, atoms), F32),
         scratch_shapes=[
-            pltpu.VMEM((slots_all, 8, LANES), F32),
+            pltpu.VMEM((slots_all, 2, LANES), F32),
             pltpu.VMEM((slots_all // LANES, 8, LANES), F32),
         ]
         + [pltpu.VMEM((2 * chunk, LANES), F32)] * 3
         + [pltpu.VMEM((chunk, LANES), BF16)] * 3
         + [pltpu.VMEM((chunk, LANES), F32)] * 3
         + [
-            pltpu.VMEM((per_atom, atoms, 32), F32),
+            pltpu.VMEM((per_atom // GROUPS, atoms, LANES), F32),
             pltpu.VMEM((atoms, LANES), F32),
             pltpu.VMEM((4, atoms, LANES), F32),
             pltpu.VMEM(w_expand.shape, BF16),
+            pltpu.SMEM(lists.shape, lists.dtype),
+            pltpu.SemaphoreType.DMA(()),
         ],
         compiler_params=pltpu.CompilerParams(vmem_limit_bytes=32 << 20),
         cost_estimate=pl.CostEstimate(

time: 70.4 us -> 68.3 us (0.970)
  Pallas kernels: 44.8 us -> 42.7 us
    pallas_call x1, Pallas kernels: 33.8 us -> 31.7 us  [edge_forces(): pl.pallas_call(edge_kernel, in_specs=[pl.BlockSpec(memory_space=pl.ANY)]...]
  transfers between devices with their start and end apart: 6 -> 6, of which waited for: 3 -> 3; matrix products, arithmetic and copies ran while one was open for 0% -> 0% of each run, Pallas kernels for 62% -> 60%
where the time goes in v11:
time: 68.3 us; the launch traced here: 68 us
  Pallas kernels  42.7 us (63%)
  starting transfers between devices  17.9 us (26%)
  waiting for transfers between devices  4.92 us (7%)
  between operations  0.9 us (1%)
  other arithmetic  0.75 us (1%)
  local copies, waits for them, and re-layouts  0.74 us (1%)
    pallas_call x1, Pallas kernels, edge_forces(): pl.pallas_call(edge_kernel, in_specs=[pl.BlockSpec(memory_space=pl.ANY)]...  31.7 us
    pallas_call x1, Pallas kernels, grid_fields(): pl.pallas_call(functools.partial(grid_kernel, cycle_x, cycle_y), in_specs...  9.06 us
    all_to_all x1, starting transfers between devices, shards(): lax.all_to_all(spread, ('dx', 'dy'), split_axis=0, concat_axis=0, tiled=T...  7.3 us
    all_to_all x1, starting transfers between devices, shards(): lax.all_to_all(partial, ('dx', 'dy'), split_axis=0, concat_axis=0, tiled=...  5.95 us
    ppermute x4, starting transfers between devices, ring(): lax.ppermute(array, axis, [(i, (i + step) % size) for i in range(size)])  4.67 us
    ppermute x4, waiting for transfers between devices, ring(): lax.ppermute(array, axis, [(i, (i + step) % size) for i in range(size)])  3.9 us
    pallas_call x1, Pallas kernels, charges(): pl.pallas_call(charge_kernel, in_specs=[pl.BlockSpec(memory_space=pltpu.S...  1.72 us
  transfers between devices with their start and end apart: 6, of which 3 were waited for; matrix products, arithmetic and copies ran while one was open for 0% of the time, Pallas kernels for 60%

profile of v11, /device:TPU:0, one launch (start us, length us, event | category | flops | bytes accessed | tf_op | source)
XLA Modules:
  0.0 68.0 jit_solution(16366885280034201645)
XLA Ops:
  0.7 0.0 copy-start.4
  0.7 1.7 %charges.1.after_ref = f32[32,2,384]{2,1,0:T(2,128)} custom-call(s32[1,1]{1,0:T(1,128)} %copy.19.count_ref, bf16[384,128]{1,0:T(8,128)(2,1)} %bitcast.18, s32[1,384]{1,0:T(1,128)} %bitcast.29, bf16[1,128]{1,0:T(2,128)(2,1)} %bitcast.30), custom_call_target="tpu_custom_call" | custom-call | tf_op jit(solution)/shard_map/charges/pallas_call | solution.py:65
  2.4 0.0 copy-start
  2.4 0.0 copy-start.1
  2.4 7.3 %all-to-all-start = ((f32[32,2,384]{2,1,0:T(2,128)}), f32[32,2,384]{2,1,0:T(2,128)S(1)}, u32[]{:S(2)}, u32[]{:S(2)}) async-start(f32[32,2,384]{2,1,0:T(2,128)} %charges.1.after_ref), calls=%async_computation | async-start | bytes 196608 | tf_op jit(solution)/shard_map/all_to_all | solution.py:564
  9.7 0.0 copy-start.3
  9.7 0.0 copy-done.4
  9.7 0.0 copy-done
  9.7 0.0 copy-done.1
  9.7 0.6 copy-done.3
  10.4 0.0 copy-start.2
  10.4 0.3 exports.1
  10.7 1.6 %collective-permute-start.1 = (bf16[272,128]{1,0:T(8,128)(2,1)S(1)}, bf16[272,128]{1,0:T(8,128)(2,1)S(1)}, u32[]{:S(2)}, u32[]{:S(2)}) collective-permute-start(bf16[272,128]{1,0:T(8,128)(2,1)S(1)} %exports.1), channel_id=1, source_target_pairs={{0,24},{8,0},{16,8},{24,16},{1,25},{9,1},{17,9},{25,17},{2,26},{10... | collective-permute-start | bytes 208904 | tf_op jit(solution)/shard_map/ppermute | solution.py:552
  12.2 0.0 collective-permute-start
  12.3 0.0 copy-done.2
  12.3 2.7 %collective-permute-done.1 = bf16[272,128]{1,0:T(8,128)(2,1)S(1)} collective-permute-done((bf16[272,128]{1,0:T(8,128)(2,1)S(1)}, bf16[272,128]{1,0:T(8,128)(2,1)S(1)}, u32[]{:S(2)}, u32[]{:S(2)}) %collective-permute-start.1) | collective-permute-done | bytes 69664 | tf_op jit(solution)/shard_map/ppermute | solution.py:552
  15.0 1.2 %collective-permute-done = bf16[272,128]{1,0:T(8,128)(2,1)S(1)} collective-permute-done((bf16[272,128]{1,0:T(8,128)(2,1)S(1)}, bf16[272,128]{1,0:T(8,128)(2,1)S(1)}, u32[]{:S(2)}, u32[]{:S(2)}) %collective-permute-start) | collective-permute-done | bytes 69664 | tf_op jit(solution)/shard_map/ppermute | solution.py:552
  16.2 0.0 copy-start.11
  16.2 0.0 copy-start.12
  16.2 0.0 copy-start.13
  16.2 0.0 copy-start.14
  16.2 1.0 %all-to-all-done.qc_ref = f32[32,2,384]{2,1,0:T(2,128)S(1)} async-done(((f32[32,2,384]{2,1,0:T(2,128)}), f32[32,2,384]{2,1,0:T(2,128)S(1)}, u32[]{:S(2)}, u32[]{:S(2)}) %all-to-all-start) | async-done | bytes 98336 | tf_op jit(solution)/shard_map/all_to_all | solution.py:564
  17.3 3.1 %collective-permute-start.3 = (bf16[3,272,128]{2,1,0:T(8,128)(2,1)S(1)}, bf16[3,272,128]{2,1,0:T(8,128)(2,1)S(1)}, u32[]{:S(2)}, u32[]{:S(2)}) collective-permute-start(bf16[3,272,128]{2,1,0:T(8,128)(2,1)S(1)} %pad_maximum_fusion.mid_ref), channel_id=1, source_target_pairs={{0,7},{1,0},{2,1},{3,2},{4,3},{5,4},{6,5},{7,6},{8,15},{9,8},{10,9... | collective-permute-start | bytes 626696 | tf_op jit(solution)/shard_map/ppermute | solution.py:552
  20.3 0.0 collective-permute-start.2
  20.3 0.0 copy-done.11
  20.4 0.0 copy-done.12
  20.4 0.0 copy-done.13
  20.4 0.0 copy-done.14
  20.4 0.0 copy-start.6
  20.4 0.0 copy-start.7
  20.4 0.0 copy-start.9
  20.4 0.0 copy-start.10
  20.4 9.1 %grid_fields.1 = f32[32,3,1,384]{3,2,1,0:T(1,128)} custom-call(s32[1]{0:T(128)} %bitcast.11.place_ref, f32[32,2,384]{2,1,0:T(2,128)S(1)} %all-to-all-done.qc_ref, f32[64,192]{1,0:T(8,128)S(1)} %copy-done.12, f32[32,96]{1,0:T(8,128)S(1)} %copy-done.14, f32[64,96]{1,0:T(8,128)S(1)} %copy-done.13, f32[128,192]{1,0:T(8,128)S(1)} %copy-done.11), custom_call_target="tpu_custom_call" | custom-call | flops 8000000000 | bytes 4000000 | tf_op jit(solution)/shard_map/grid_fields/pallas_call | solution.py:286
  29.5 0.0 copy-start.5
  29.5 0.0 copy-start.8
  29.5 6.0 %all-to-all-start.1 = ((f32[32,3,1,384]{3,2,1,0:T(1,128)}), f32[32,3,1,384]{3,2,1,0:T(1,128)S(1)}, u32[]{:S(2)}, u32[]{:S(2)}) async-start(f32[32,3,1,384]{3,2,1,0:T(1,128)} %grid_fields.1), calls=%async_computation.1 | async-start | bytes 294912 | tf_op jit(solution)/shard_map/all_to_all | solution.py:573
  35.4 0.0 collective-permute-done.3.down_ref
  35.5 0.0 collective-permute-done.2.up_ref
  35.5 0.0 copy-done.6
  35.5 0.0 copy-done.7
  35.5 0.0 copy-done.9
  35.5 0.0 copy-done.10
  35.5 0.0 copy-done.5
  35.5 0.0 copy-done.8
  35.5 31.7 %edge_forces.1 = f32[3,1,384]{2,1,0:T(1,128)S(1)} custom-call(s32[12288]{0:T(1024)S(1)} %reshape.46.list_hbm, s32[32,384]{1,0:T(8,128)S(1)} %bitcast.23, bf16[384,128]{1,0:T(8,128)(2,1)S(1)} %bitcast.20, bf16[3,384]{1,0:T(4,128)(2,1)S(1)} %bitcast.25, bf16[3,272,128]{2,1,0:T(8,128)(2,1)S(1)} %pad_maximum_fusion.mid_ref, ...), custom_call_target="tpu_custom_call" | custom-call | flops 6442450944 | bytes 4000000 | tf_op jit(solution)/shard_map/edge_forces/pallas_call | solution.py:517
  67.2 0.0 all-to-all-done.1
  67.2 0.1 reduce_sum.11
  67.4 0.6 fusion
  (4 shorter events, 0.1 us)
Async XLA Ops:
  0.7 9.1 %copy-start.4 = (s32[1,1,256]{2,1,0:T(1,128)S(1)}, s32[1,1,256]{2,1,0:T(1,128)}, u32[]{:S(2)}) copy-start(s32[1,1,256]{2,1,0:T(1,128)} %param.20) | copy-start | bytes 3076
  2.4 7.3 %copy-start = (f32[32,2,384]{2,1,0:T(2,128)S(1)}, f32[32,2,384]{2,1,0:T(2,128)}, u32[]{:S(2)}) copy-start(f32[32,2,384]{2,1,0:T(2,128)} %charges.1.after_ref) | copy-start | bytes 294916
  2.4 7.3 %copy-start.1 = (bf16[1,1,384,128]{3,2,1,0:T(8,128)(2,1)S(1)}, bf16[1,1,384,128]{3,2,1,0:T(8,128)(2,1)}, u32[]{:S(2)}) copy-start(bf16[1,1,384,128]{3,2,1,0:T(8,128)(2,1)} %param.17) | copy-start | bytes 294916
  2.4 14.9 %all-to-all-start = ((f32[32,2,384]{2,1,0:T(2,128)}), f32[32,2,384]{2,1,0:T(2,128)S(1)}, u32[]{:S(2)}, u32[]{:S(2)}) async-start(f32[32,2,384]{2,1,0:T(2,128)} %charges.1.after_ref), calls=%async_computation | async-start | bytes 196608 | tf_op jit(solution)/shard_map/all_to_all | solution.py:564
  9.7 0.7 %copy-start.3 = (bf16[1,1,3,384]{3,2,1,0:T(4,128)(2,1)S(1)}, bf16[1,1,3,384]{3,2,1,0:T(4,128)(2,1)}, u32[]{:S(2)}) copy-start(bf16[1,1,3,384]{3,2,1,0:T(4,128)(2,1)} %param.18) | copy-start | bytes 6916
  10.4 1.9 %copy-start.2 = (s32[1,1,384,32]{2,3,1,0:T(8,128)S(1)}, s32[1,1,384,32]{2,3,1,0:T(8,128)}, u32[]{:S(2)}) copy-start(s32[1,1,384,32]{2,3,1,0:T(8,128)} %param.21) | copy-start | bytes 147460
  10.7 4.4 %collective-permute-start.1 = (bf16[272,128]{1,0:T(8,128)(2,1)S(1)}, bf16[272,128]{1,0:T(8,128)(2,1)S(1)}, u32[]{:S(2)}, u32[]{:S(2)}) collective-permute-start(bf16[272,128]{1,0:T(8,128)(2,1)S(1)} %exports.1), channel_id=1, source_target_pairs={{0,24},{8,0},{16,8},{24,16},{1,25},{9,1},{17,9},{25,17},{2,26},{10... | collective-permute-start | bytes 208904 | tf_op jit(solution)/shard_map/ppermute | solution.py:552
  12.2 4.0 %collective-permute-start = (bf16[272,128]{1,0:T(8,128)(2,1)S(1)}, bf16[272,128]{1,0:T(8,128)(2,1)S(1)}, u32[]{:S(2)}, u32[]{:S(2)}) collective-permute-start(bf16[272,128]{1,0:T(8,128)(2,1)S(1)} %exports.1), channel_id=1, source_target_pairs={{0,8},{8,16},{16,24},{24,0},{1,9},{9,17},{17,25},{25,1},{2,10},{10... | collective-permute-start | bytes 208904 | tf_op jit(solution)/shard_map/ppermute | solution.py:552
  16.2 4.2 %copy-start.11 = (f32[128,192]{1,0:T(8,128)S(1)}, f32[128,192]{1,0:T(8,128)}, u32[]{:S(2)}) copy-start(f32[128,192]{1,0:T(8,128)} %constant.24.clone.iy_ref) | copy-start | bytes 294916
  16.2 4.2 %copy-start.12 = (f32[64,192]{1,0:T(8,128)S(1)}, f32[64,192]{1,0:T(8,128)}, u32[]{:S(2)}) copy-start(f32[64,192]{1,0:T(8,128)} %constant.21.clone.fy_ref) | copy-start | bytes 147460
  16.2 4.2 %copy-start.13 = (f32[64,96]{1,0:T(8,128)S(1)}, f32[64,96]{1,0:T(8,128)}, u32[]{:S(2)}) copy-start(f32[64,96]{1,0:T(8,128)} %constant.23.clone.ix_ref) | copy-start | bytes 73732
  16.2 4.2 %copy-start.14 = (f32[32,96]{1,0:T(8,128)S(1)}, f32[32,96]{1,0:T(8,128)}, u32[]{:S(2)}) copy-start(f32[32,96]{1,0:T(8,128)} %constant.22.clone.fx_ref) | copy-start | bytes 36868
  17.3 18.2 %collective-permute-start.3 = (bf16[3,272,128]{2,1,0:T(8,128)(2,1)S(1)}, bf16[3,272,128]{2,1,0:T(8,128)(2,1)S(1)}, u32[]{:S(2)}, u32[]{:S(2)}) collective-permute-start(bf16[3,272,128]{2,1,0:T(8,128)(2,1)S(1)} %pad_maximum_fusion.mid_ref), channel_id=1, source_target_pairs={{0,7},{1,0},{2,1},{3,2},{4,3},{5,4},{6,5},{7,6},{8,15},{9,8},{10,9... | collective-permute-start | bytes 626696 | tf_op jit(solution)/shard_map/ppermute | solution.py:552
  20.3 15.1 %collective-permute-start.2 = (bf16[3,272,128]{2,1,0:T(8,128)(2,1)S(1)}, bf16[3,272,128]{2,1,0:T(8,128)(2,1)S(1)}, u32[]{:S(2)}, u32[]{:S(2)}) collective-permute-start(bf16[3,272,128]{2,1,0:T(8,128)(2,1)S(1)} %pad_maximum_fusion.mid_ref), channel_id=1, source_target_pairs={{0,1},{1,2},{2,3},{3,4},{4,5},{5,6},{6,7},{7,0},{8,9},{9,10},{10,1... | collective-permute-start | bytes 626696 | tf_op jit(solution)/shard_map/ppermute | solution.py:552
  20.4 15.1 %copy-start.6 = (bf16[1024,128]{1,0:T(8,128)(2,1)S(1)}, bf16[1024,128]{1,0:T(8,128)(2,1)}, u32[]{:S(2)}) copy-start(bf16[1024,128]{1,0:T(8,128)(2,1)} %w_contract_ref.1) | copy-start | bytes 786436
  20.4 15.1 %copy-start.7 = (bf16[128,256]{1,0:T(8,128)(2,1)S(1)}, bf16[128,256]{1,0:T(8,128)(2,1)}, u32[]{:S(2)}) copy-start(bf16[128,256]{1,0:T(8,128)(2,1)} %w_pair_ref.1) | copy-start | bytes 196612
  20.4 15.1 %copy-start.9 = (bf16[128,128]{1,0:T(8,128)(2,1)S(1)}, bf16[128,128]{1,0:T(8,128)(2,1)}, u32[]{:S(2)}) copy-start(bf16[128,128]{1,0:T(8,128)(2,1)} %w_final_ref.1) | copy-start | bytes 98308
  20.4 15.1 %copy-start.10 = (f32[8,128]{1,0:T(8,128)S(1)}, f32[8,128]{1,0:T(8,128)}, u32[]{:S(2)}) copy-start(f32[8,128]{1,0:T(8,128)} %w_radial_ref.1) | copy-start | bytes 12292
  29.5 6.0 %copy-start.5 = (bf16[128,1024]{1,0:T(8,128)(2,1)S(1)}, bf16[128,1024]{1,0:T(8,128)(2,1)}, u32[]{:S(2)}) copy-start(bf16[128,1024]{1,0:T(8,128)(2,1)} %w_expand_ref.1) | copy-start | bytes 786436
  29.5 6.0 %copy-start.8 = (bf16[128,128]{1,0:T(8,128)(2,1)S(1)}, bf16[128,128]{1,0:T(8,128)(2,1)}, u32[]{:S(2)}) copy-start(bf16[128,128]{1,0:T(8,128)(2,1)} %w_self_ref.1) | copy-start | bytes 98308
  29.5 37.7 %all-to-all-start.1 = ((f32[32,3,1,384]{3,2,1,0:T(1,128)}), f32[32,3,1,384]{3,2,1,0:T(1,128)S(1)}, u32[]{:S(2)}, u32[]{:S(2)}) async-start(f32[32,3,1,384]{3,2,1,0:T(1,128)} %grid_fields.1), calls=%async_computation.1 | async-start | bytes 294912 | tf_op jit(solution)/shard_map/all_to_all | solution.py:573

commit v12 on v11

--- a/solution.py
+++ b/solution.py
@@ -20,7 +20,7 @@
 EXTRA = 16
 ROWS = 32
 GROUPS = LANES // ROWS
-CHUNK_ATOMS = 16
+CHUNK_ATOMS = 32
 PIECES = 4
 HIGHEST = lax.Precision.HIGHEST
 F32 = jnp.float32
@@ -411,21 +411,23 @@
             start = k * atoms + index * CHUNK_ATOMS
             loaded = [table[list_ref[start + a]] for a in range(CHUNK_ATOMS)]
             for a, tile in enumerate(loaded):
-                near[pl.ds(k * CHUNK_ATOMS + a, 2, stride=chunk), :] = tile
-
-    def enter(index, near, edge_in, part):
+                near[k * CHUNK_ATOMS + a] = tile
+
+    def radials(index):
+        basis = marks[:, atoms_of(index), :].reshape(-1, LANES).astype(BF16)
+        return jnp.dot(basis, w_basis, preferred_element_type=F32)
+
+    def enter(index, near, edge_in, part, wide):
         rows = pl.ds(part * part_rows, part_rows)
         groups = slots // GROUPS
-        basis = marks[pl.ds(part * groups, groups), atoms_of(index), :]
-        basis = basis.reshape(groups * CHUNK_ATOMS, LANES).astype(BF16)
-        wide = jnp.dot(basis, w_basis, preferred_element_type=F32)
         pieces = []
-        for q in range(groups):
+        for q in range(part * groups, (part + 1) * groups):
             for g in range(GROUPS):
                 rows_q = slice(q * CHUNK_ATOMS, (q + 1) * CHUNK_ATOMS)
                 pieces.append(wide[rows_q, g * LANES : (g + 1) * LANES])
         radial = jnp.concatenate(pieces, axis=0).reshape(shape)
-        half = radial + own_ref[atoms_of(index), :][None] + near[rows, :].reshape(shape)
+        bias = near.reshape(2 * chunk, LANES)[pl.ds(part * part_rows * 2, part_rows, stride=2), :]
+        half = radial + own_ref[atoms_of(index), :][None] + bias.reshape(shape)
         turn = jnp.tanh(half.astype(BF16)).astype(F32)
         edge_in[rows, :] = (half + half * turn).astype(BF16).reshape(part_rows, LANES)
 
@@ -440,8 +442,8 @@
 
     def collect(index, near, total, part, before):
         rows = pl.ds(part * part_rows, part_rows)
-        other = pl.ds(chunk + part * part_rows, part_rows)
-        weight = (total[rows, :] * near[other, :]).reshape(shape)
+        other = pl.ds(part * part_rows * 2 + 1, part_rows, stride=2)
+        weight = (total[rows, :] * near.reshape(2 * chunk, LANES)[other, :]).reshape(shape)
         after = []
         for s in range(4):
             summed = 0.0
@@ -461,13 +463,14 @@
         before = jnp.maximum(index - 1, 0)
         mixed, sums = (None, None)
         half = expand(edges[0], 0)
+        wide = radials(after)
         for part in range(PIECES):
             gather(after, nears[1], part)
             following = expand(edges[0], part + 1) if part + 1 < PIECES else None
             sums = collect(before, nears[2], totals[2], part, sums)
             term = contract(half, part)
             mixed = term if mixed is None else mixed + term
-            enter(after, nears[1], edges[1], part)
+            enter(after, nears[1], edges[1], part, wide)
             half = following
         totals[0][...] = mixed
         keep(before, sums)
@@ -478,8 +481,9 @@
     fetch.wait()
     for part in range(PIECES):
         gather(0, near_a, part)
+    wide = radials(0)
     for part in range(PIECES):
-        enter(0, near_a, edge_a, part)
+        enter(0, near_a, edge_a, part, wide)
 
     def triple(step, carry):
         for i in range(3):
@@ -523,7 +527,7 @@
             pltpu.VMEM((slots_all, 2, LANES), F32),
             pltpu.VMEM((slots_all // LANES, 8, LANES), F32),
         ]
-        + [pltpu.VMEM((2 * chunk, LANES), F32)] * 3
+        + [pltpu.VMEM((chunk, 2, LANES), F32)] * 3
         + [pltpu.VMEM((chunk, LANES), BF16)] * 3
         + [pltpu.VMEM((chunk, LANES), F32)] * 3
         + [

time: 68.3 us -> 68 us (level)
  no operation moved by 1% of the time
where the time goes in v12:
time: 68 us; the launch traced here: 67.7 us
  Pallas kernels  42.5 us (62%)
  starting transfers between devices  17.9 us (26%)
  waiting for transfers between devices  4.92 us (7%)
  between operations  0.9 us (1%)
  other arithmetic  0.75 us (1%)
  local copies, waits for them, and re-layouts  0.74 us (1%)
    pallas_call x1, Pallas kernels, edge_forces(): pl.pallas_call(edge_kernel, in_specs=[pl.BlockSpec(memory_space=pl.ANY)]...  31.4 us
    pallas_call x1, Pallas kernels, grid_fields(): pl.pallas_call(functools.partial(grid_kernel, cycle_x, cycle_y), in_specs...  9.06 us
    all_to_all x1, starting transfers between devices, shards(): lax.all_to_all(spread, ('dx', 'dy'), split_axis=0, concat_axis=0, tiled=T...  7.3 us
    all_to_all x1, starting transfers between devices, shards(): lax.all_to_all(partial, ('dx', 'dy'), split_axis=0, concat_axis=0, tiled=...  5.95 us
    ppermute x4, starting transfers between devices, ring(): lax.ppermute(array, axis, [(i, (i + step) % size) for i in range(size)])  4.67 us
    ppermute x4, waiting for transfers between devices, ring(): lax.ppermute(array, axis, [(i, (i + step) % size) for i in range(size)])  3.9 us
    pallas_call x1, Pallas kernels, charges(): pl.pallas_call(charge_kernel, in_specs=[pl.BlockSpec(memory_space=pltpu.S...  1.72 us
  transfers between devices with their start and end apart: 6, of which 3 were waited for; matrix products, arithmetic and copies ran while one was open for 0% of the time, Pallas kernels for 60%

profile of v12, /device:TPU:0, one launch (start us, length us, event | category | flops | bytes accessed | tf_op | source)
XLA Modules:
  0.0 67.7 jit_solution(16355731491280912657)
XLA Ops:
  0.7 0.0 copy-start.4
  0.7 1.7 %charges.1.after_ref = f32[32,2,384]{2,1,0:T(2,128)} custom-call(s32[1,1]{1,0:T(1,128)} %copy.19.count_ref, bf16[384,128]{1,0:T(8,128)(2,1)} %bitcast.18, s32[1,384]{1,0:T(1,128)} %bitcast.29, bf16[1,128]{1,0:T(2,128)(2,1)} %bitcast.30), custom_call_target="tpu_custom_call" | custom-call | tf_op jit(solution)/shard_map/charges/pallas_call | solution.py:65
  2.4 0.0 copy-start
  2.4 0.0 copy-start.1
  2.4 7.3 %all-to-all-start = ((f32[32,2,384]{2,1,0:T(2,128)}), f32[32,2,384]{2,1,0:T(2,128)S(1)}, u32[]{:S(2)}, u32[]{:S(2)}) async-start(f32[32,2,384]{2,1,0:T(2,128)} %charges.1.after_ref), calls=%async_computation | async-start | bytes 196608 | tf_op jit(solution)/shard_map/all_to_all | solution.py:568
  9.7 0.0 copy-start.3
  9.7 0.0 copy-done.4
  9.7 0.0 copy-done
  9.7 0.0 copy-done.1
  9.7 0.6 copy-done.3
  10.4 0.0 copy-start.2
  10.4 0.3 exports.1
  10.7 1.6 %collective-permute-start.1 = (bf16[272,128]{1,0:T(8,128)(2,1)S(1)}, bf16[272,128]{1,0:T(8,128)(2,1)S(1)}, u32[]{:S(2)}, u32[]{:S(2)}) collective-permute-start(bf16[272,128]{1,0:T(8,128)(2,1)S(1)} %exports.1), channel_id=1, source_target_pairs={{0,24},{8,0},{16,8},{24,16},{1,25},{9,1},{17,9},{25,17},{2,26},{10... | collective-permute-start | bytes 208904 | tf_op jit(solution)/shard_map/ppermute | solution.py:556
  12.2 0.0 collective-permute-start
  12.3 0.0 copy-done.2
  12.3 2.7 %collective-permute-done.1 = bf16[272,128]{1,0:T(8,128)(2,1)S(1)} collective-permute-done((bf16[272,128]{1,0:T(8,128)(2,1)S(1)}, bf16[272,128]{1,0:T(8,128)(2,1)S(1)}, u32[]{:S(2)}, u32[]{:S(2)}) %collective-permute-start.1) | collective-permute-done | bytes 69664 | tf_op jit(solution)/shard_map/ppermute | solution.py:556
  15.0 1.2 %collective-permute-done = bf16[272,128]{1,0:T(8,128)(2,1)S(1)} collective-permute-done((bf16[272,128]{1,0:T(8,128)(2,1)S(1)}, bf16[272,128]{1,0:T(8,128)(2,1)S(1)}, u32[]{:S(2)}, u32[]{:S(2)}) %collective-permute-start) | collective-permute-done | bytes 69664 | tf_op jit(solution)/shard_map/ppermute | solution.py:556
  16.2 0.0 copy-start.11
  16.2 0.0 copy-start.12
  16.2 0.0 copy-start.13
  16.2 0.0 copy-start.14
  16.2 1.0 %all-to-all-done.qc_ref = f32[32,2,384]{2,1,0:T(2,128)S(1)} async-done(((f32[32,2,384]{2,1,0:T(2,128)}), f32[32,2,384]{2,1,0:T(2,128)S(1)}, u32[]{:S(2)}, u32[]{:S(2)}) %all-to-all-start) | async-done | bytes 98336 | tf_op jit(solution)/shard_map/all_to_all | solution.py:568
  17.3 3.1 %collective-permute-start.3 = (bf16[3,272,128]{2,1,0:T(8,128)(2,1)S(1)}, bf16[3,272,128]{2,1,0:T(8,128)(2,1)S(1)}, u32[]{:S(2)}, u32[]{:S(2)}) collective-permute-start(bf16[3,272,128]{2,1,0:T(8,128)(2,1)S(1)} %pad_maximum_fusion.mid_ref), channel_id=1, source_target_pairs={{0,7},{1,0},{2,1},{3,2},{4,3},{5,4},{6,5},{7,6},{8,15},{9,8},{10,9... | collective-permute-start | bytes 626696 | tf_op jit(solution)/shard_map/ppermute | solution.py:556
  20.3 0.0 collective-permute-start.2
  20.3 0.0 copy-done.11
  20.4 0.0 copy-done.12
  20.4 0.0 copy-done.13
  20.4 0.0 copy-done.14
  20.4 0.0 copy-start.6
  20.4 0.0 copy-start.7
  20.4 0.0 copy-start.9
  20.4 0.0 copy-start.10
  20.4 9.1 %grid_fields.1 = f32[32,3,1,384]{3,2,1,0:T(1,128)} custom-call(s32[1]{0:T(128)} %bitcast.11.place_ref, f32[32,2,384]{2,1,0:T(2,128)S(1)} %all-to-all-done.qc_ref, f32[64,192]{1,0:T(8,128)S(1)} %copy-done.12, f32[32,96]{1,0:T(8,128)S(1)} %copy-done.14, f32[64,96]{1,0:T(8,128)S(1)} %copy-done.13, f32[128,192]{1,0:T(8,128)S(1)} %copy-done.11), custom_call_target="tpu_custom_call" | custom-call | flops 8000000000 | bytes 4000000 | tf_op jit(solution)/shard_map/grid_fields/pallas_call | solution.py:286
  29.5 0.0 copy-start.5
  29.5 0.0 copy-start.8
  29.5 6.0 %all-to-all-start.1 = ((f32[32,3,1,384]{3,2,1,0:T(1,128)}), f32[32,3,1,384]{3,2,1,0:T(1,128)S(1)}, u32[]{:S(2)}, u32[]{:S(2)}) async-start(f32[32,3,1,384]{3,2,1,0:T(1,128)} %grid_fields.1), calls=%async_computation.1 | async-start | bytes 294912 | tf_op jit(solution)/shard_map/all_to_all | solution.py:577
  35.4 0.0 collective-permute-done.3.down_ref
  35.5 0.0 collective-permute-done.2.up_ref
  35.5 0.0 copy-done.6
  35.5 0.0 copy-done.7
  35.5 0.0 copy-done.9
  35.5 0.0 copy-done.10
  35.5 0.0 copy-done.5
  35.5 0.0 copy-done.8
  35.5 31.4 %edge_forces.1 = f32[3,1,384]{2,1,0:T(1,128)S(1)} custom-call(s32[12288]{0:T(1024)S(1)} %reshape.46.list_hbm, s32[32,384]{1,0:T(8,128)S(1)} %bitcast.23, bf16[384,128]{1,0:T(8,128)(2,1)S(1)} %bitcast.20, bf16[3,384]{1,0:T(4,128)(2,1)S(1)} %bitcast.25, bf16[3,272,128]{2,1,0:T(8,128)(2,1)S(1)} %pad_maximum_fusion.mid_ref, ...), custom_call_target="tpu_custom_call" | custom-call | flops 6442450944 | bytes 4000000 | tf_op jit(solution)/shard_map/edge_forces/pallas_call | solution.py:521
  67.0 0.0 all-to-all-done.1
  67.0 0.1 reduce_sum.11
  67.1 0.6 fusion
  (4 shorter events, 0.1 us)
Async XLA Ops:
  0.7 9.1 %copy-start.4 = (s32[1,1,256]{2,1,0:T(1,128)S(1)}, s32[1,1,256]{2,1,0:T(1,128)}, u32[]{:S(2)}) copy-start(s32[1,1,256]{2,1,0:T(1,128)} %param.20) | copy-start | bytes 3076
  2.4 7.3 %copy-start = (f32[32,2,384]{2,1,0:T(2,128)S(1)}, f32[32,2,384]{2,1,0:T(2,128)}, u32[]{:S(2)}) copy-start(f32[32,2,384]{2,1,0:T(2,128)} %charges.1.after_ref) | copy-start | bytes 294916
  2.4 7.3 %copy-start.1 = (bf16[1,1,384,128]{3,2,1,0:T(8,128)(2,1)S(1)}, bf16[1,1,384,128]{3,2,1,0:T(8,128)(2,1)}, u32[]{:S(2)}) copy-start(bf16[1,1,384,128]{3,2,1,0:T(8,128)(2,1)} %param.17) | copy-start | bytes 294916
  2.4 14.9 %all-to-all-start = ((f32[32,2,384]{2,1,0:T(2,128)}), f32[32,2,384]{2,1,0:T(2,128)S(1)}, u32[]{:S(2)}, u32[]{:S(2)}) async-start(f32[32,2,384]{2,1,0:T(2,128)} %charges.1.after_ref), calls=%async_computation | async-start | bytes 196608 | tf_op jit(solution)/shard_map/all_to_all | solution.py:568
  9.7 0.7 %copy-start.3 = (bf16[1,1,3,384]{3,2,1,0:T(4,128)(2,1)S(1)}, bf16[1,1,3,384]{3,2,1,0:T(4,128)(2,1)}, u32[]{:S(2)}) copy-start(bf16[1,1,3,384]{3,2,1,0:T(4,128)(2,1)} %param.18) | copy-start | bytes 6916
  10.4 1.9 %copy-start.2 = (s32[1,1,384,32]{2,3,1,0:T(8,128)S(1)}, s32[1,1,384,32]{2,3,1,0:T(8,128)}, u32[]{:S(2)}) copy-start(s32[1,1,384,32]{2,3,1,0:T(8,128)} %param.21) | copy-start | bytes 147460
  10.7 4.4 %collective-permute-start.1 = (bf16[272,128]{1,0:T(8,128)(2,1)S(1)}, bf16[272,128]{1,0:T(8,128)(2,1)S(1)}, u32[]{:S(2)}, u32[]{:S(2)}) collective-permute-start(bf16[272,128]{1,0:T(8,128)(2,1)S(1)} %exports.1), channel_id=1, source_target_pairs={{0,24},{8,0},{16,8},{24,16},{1,25},{9,1},{17,9},{25,17},{2,26},{10... | collective-permute-start | bytes 208904 | tf_op jit(solution)/shard_map/ppermute | solution.py:556
  12.2 4.0 %collective-permute-start = (bf16[272,128]{1,0:T(8,128)(2,1)S(1)}, bf16[272,128]{1,0:T(8,128)(2,1)S(1)}, u32[]{:S(2)}, u32[]{:S(2)}) collective-permute-start(bf16[272,128]{1,0:T(8,128)(2,1)S(1)} %exports.1), channel_id=1, source_target_pairs={{0,8},{8,16},{16,24},{24,0},{1,9},{9,17},{17,25},{25,1},{2,10},{10... | collective-permute-start | bytes 208904 | tf_op jit(solution)/shard_map/ppermute | solution.py:556
  16.2 4.2 %copy-start.11 = (f32[128,192]{1,0:T(8,128)S(1)}, f32[128,192]{1,0:T(8,128)}, u32[]{:S(2)}) copy-start(f32[128,192]{1,0:T(8,128)} %constant.24.clone.iy_ref) | copy-start | bytes 294916
  16.2 4.2 %copy-start.12 = (f32[64,192]{1,0:T(8,128)S(1)}, f32[64,192]{1,0:T(8,128)}, u32[]{:S(2)}) copy-start(f32[64,192]{1,0:T(8,128)} %constant.21.clone.fy_ref) | copy-start | bytes 147460
  16.2 4.2 %copy-start.13 = (f32[64,96]{1,0:T(8,128)S(1)}, f32[64,96]{1,0:T(8,128)}, u32[]{:S(2)}) copy-start(f32[64,96]{1,0:T(8,128)} %constant.23.clone.ix_ref) | copy-start | bytes 73732
  16.2 4.2 %copy-start.14 = (f32[32,96]{1,0:T(8,128)S(1)}, f32[32,96]{1,0:T(8,128)}, u32[]{:S(2)}) copy-start(f32[32,96]{1,0:T(8,128)} %constant.22.clone.fx_ref) | copy-start | bytes 36868
  17.3 18.2 %collective-permute-start.3 = (bf16[3,272,128]{2,1,0:T(8,128)(2,1)S(1)}, bf16[3,272,128]{2,1,0:T(8,128)(2,1)S(1)}, u32[]{:S(2)}, u32[]{:S(2)}) collective-permute-start(bf16[3,272,128]{2,1,0:T(8,128)(2,1)S(1)} %pad_maximum_fusion.mid_ref), channel_id=1, source_target_pairs={{0,7},{1,0},{2,1},{3,2},{4,3},{5,4},{6,5},{7,6},{8,15},{9,8},{10,9... | collective-permute-start | bytes 626696 | tf_op jit(solution)/shard_map/ppermute | solution.py:556
  20.3 15.1 %collective-permute-start.2 = (bf16[3,272,128]{2,1,0:T(8,128)(2,1)S(1)}, bf16[3,272,128]{2,1,0:T(8,128)(2,1)S(1)}, u32[]{:S(2)}, u32[]{:S(2)}) collective-permute-start(bf16[3,272,128]{2,1,0:T(8,128)(2,1)S(1)} %pad_maximum_fusion.mid_ref), channel_id=1, source_target_pairs={{0,1},{1,2},{2,3},{3,4},{4,5},{5,6},{6,7},{7,0},{8,9},{9,10},{10,1... | collective-permute-start | bytes 626696 | tf_op jit(solution)/shard_map/ppermute | solution.py:556
  20.4 15.1 %copy-start.6 = (bf16[1024,128]{1,0:T(8,128)(2,1)S(1)}, bf16[1024,128]{1,0:T(8,128)(2,1)}, u32[]{:S(2)}) copy-start(bf16[1024,128]{1,0:T(8,128)(2,1)} %w_contract_ref.1) | copy-start | bytes 786436
  20.4 15.1 %copy-start.7 = (bf16[128,256]{1,0:T(8,128)(2,1)S(1)}, bf16[128,256]{1,0:T(8,128)(2,1)}, u32[]{:S(2)}) copy-start(bf16[128,256]{1,0:T(8,128)(2,1)} %w_pair_ref.1) | copy-start | bytes 196612
  20.4 15.1 %copy-start.9 = (bf16[128,128]{1,0:T(8,128)(2,1)S(1)}, bf16[128,128]{1,0:T(8,128)(2,1)}, u32[]{:S(2)}) copy-start(bf16[128,128]{1,0:T(8,128)(2,1)} %w_final_ref.1) | copy-start | bytes 98308
  20.4 15.1 %copy-start.10 = (f32[8,128]{1,0:T(8,128)S(1)}, f32[8,128]{1,0:T(8,128)}, u32[]{:S(2)}) copy-start(f32[8,128]{1,0:T(8,128)} %w_radial_ref.1) | copy-start | bytes 12292
  29.5 6.0 %copy-start.5 = (bf16[128,1024]{1,0:T(8,128)(2,1)S(1)}, bf16[128,1024]{1,0:T(8,128)(2,1)}, u32[]{:S(2)}) copy-start(bf16[128,1024]{1,0:T(8,128)(2,1)} %w_expand_ref.1) | copy-start | bytes 786436
  29.5 6.0 %copy-start.8 = (bf16[128,128]{1,0:T(8,128)(2,1)S(1)}, bf16[128,128]{1,0:T(8,128)(2,1)}, u32[]{:S(2)}) copy-start(bf16[128,128]{1,0:T(8,128)(2,1)} %w_self_ref.1) | copy-start | bytes 98308
  29.5 37.5 %all-to-all-start.1 = ((f32[32,3,1,384]{3,2,1,0:T(1,128)}), f32[32,3,1,384]{3,2,1,0:T(1,128)S(1)}, u32[]{:S(2)}, u32[]{:S(2)}) async-start(f32[32,3,1,384]{3,2,1,0:T(1,128)} %grid_fields.1), calls=%async_computation.1 | async-start | bytes 294912 | tf_op jit(solution)/shard_map/all_to_all | solution.py:577

commit v13 on v12

--- a/solution.py
+++ b/solution.py
@@ -306,7 +306,7 @@
     list_hbm, index_ref, feat_ref, pos_ref, mid_ref, up_ref, down_ref, w_self_ref, w_pair_ref,
     w_radial_ref, w_expand_ref, w_contract_ref, w_final_ref, out_ref,
     table, places, near_a, near_b, near_c, edge_a, edge_b, edge_c,
-    total_a, total_b, total_c, marks, own_ref, sums_ref, w_half,
+    total_a, total_b, total_c, marks, own_ref, sums_ref, w_half, w_back,
     list_ref, list_sem,
 ):
     atoms, channels = feat_ref.shape
@@ -318,9 +318,11 @@
     basis_count = w_radial_ref.shape[0]
     spacing = CUTOFF_SQ / (basis_count - 1)
     latent = w_expand_ref.shape[1]
-    width = latent // PIECES
     slots = per_atom // PIECES
-    w_half[...] = w_expand_ref[...] * 0.5
+    for i in range(latent // LANES):
+        rows = pl.ds(i * LANES, LANES)
+        w_half[rows, :] = (w_expand_ref[:, rows].astype(F32) * 0.5).T.astype(BF16)
+        w_back[:, rows] = w_contract_ref[rows, :].astype(F32).T.astype(BF16)
 
     fetch = pltpu.make_async_copy(list_hbm, list_ref, list_sem)
     fetch.start()
@@ -431,14 +433,11 @@
         turn = jnp.tanh(half.astype(BF16)).astype(F32)
         edge_in[rows, :] = (half + half * turn).astype(BF16).reshape(part_rows, LANES)
 
-    def expand(edge_in, part):
-        cols = pl.ds(part * width, width)
-        return jnp.dot(edge_in[...], w_half[:, cols], preferred_element_type=F32).astype(BF16)
-
-    def contract(half, part):
+    def network(edge_in, part):
+        rows = pl.ds(part * part_rows, part_rows)
+        half = contract_last(w_half[...], edge_in[rows, :]).astype(BF16)
         hidden = half + half * jnp.tanh(half)
-        cols = pl.ds(part * width, width)
-        return jnp.dot(hidden, w_contract_ref[cols, :], preferred_element_type=F32)
+        return jnp.dot(w_back[...], hidden, preferred_element_type=F32).T
 
     def collect(index, near, total, part, before):
         rows = pl.ds(part * part_rows, part_rows)
@@ -461,18 +460,13 @@
     def stage(index, nears, edges, totals):
         after = jnp.minimum(index + 1, chunks - 1)
         before = jnp.maximum(index - 1, 0)
-        mixed, sums = (None, None)
-        half = expand(edges[0], 0)
+        sums = None
         wide = radials(after)
         for part in range(PIECES):
             gather(after, nears[1], part)
-            following = expand(edges[0], part + 1) if part + 1 < PIECES else None
             sums = collect(before, nears[2], totals[2], part, sums)
-            term = contract(half, part)
-            mixed = term if mixed is None else mixed + term
+            totals[0][pl.ds(part * part_rows, part_rows), :] = network(edges[0], part)
             enter(after, nears[1], edges[1], part, wide)
-            half = following
-        totals[0][...] = mixed
         keep(before, sums)
 
     nears = (near_a, near_b, near_c)
@@ -534,6 +528,7 @@
             pltpu.VMEM((per_atom // GROUPS, atoms, LANES), F32),
             pltpu.VMEM((atoms, LANES), F32),
             pltpu.VMEM((4, atoms, LANES), F32),
+            pltpu.VMEM(w_contract.shape, BF16),
             pltpu.VMEM(w_expand.shape, BF16),
             pltpu.SMEM(lists.shape, lists.dtype),
             pltpu.SemaphoreType.DMA(()),

time: 68 us -> 74.7 us (1.099)
  Pallas kernels: 42.5 us -> 49.2 us
    pallas_call x1, Pallas kernels: 31.4 us -> 38.1 us  [edge_forces(): pl.pallas_call(edge_kernel, in_specs=[pl.BlockSpec(memory_space=pl.ANY)]...]
  transfers between devices with their start and end apart: 6 -> 6, of which waited for: 3 -> 3; matrix products, arithmetic and copies ran while one was open for 0% -> 0% of each run, Pallas kernels for 60% -> 64%
where the time goes in v13:
time: 74.7 us; the launch traced here: 74.4 us
  Pallas kernels  49.2 us (66%)
  starting transfers between devices  17.9 us (24%)
  waiting for transfers between devices  4.92 us (7%)
  between operations  0.9 us (1%)
  other arithmetic  0.75 us (1%)
    pallas_call x1, Pallas kernels, edge_forces(): pl.pallas_call(edge_kernel, in_specs=[pl.BlockSpec(memory_space=pl.ANY)]...  38.1 us
    pallas_call x1, Pallas kernels, grid_fields(): pl.pallas_call(functools.partial(grid_kernel, cycle_x, cycle_y), in_specs...  9.06 us
    all_to_all x1, starting transfers between devices, shards(): lax.all_to_all(spread, ('dx', 'dy'), split_axis=0, concat_axis=0, tiled=T...  7.3 us
    all_to_all x1, starting transfers between devices, shards(): lax.all_to_all(partial, ('dx', 'dy'), split_axis=0, concat_axis=0, tiled=...  5.95 us
    ppermute x4, starting transfers between devices, ring(): lax.ppermute(array, axis, [(i, (i + step) % size) for i in range(size)])  4.67 us
    ppermute x4, waiting for transfers between devices, ring(): lax.ppermute(array, axis, [(i, (i + step) % size) for i in range(size)])  3.9 us
    pallas_call x1, Pallas kernels, charges(): pl.pallas_call(charge_kernel, in_specs=[pl.BlockSpec(memory_space=pltpu.S...  1.72 us
  transfers between devices with their start and end apart: 6, of which 3 were waited for; matrix products, arithmetic and copies ran while one was open for 0% of the time, Pallas kernels for 64%

profile of v13, /device:TPU:0, one launch (start us, length us, event | category | flops | bytes accessed | tf_op | source)
XLA Modules:
  0.0 74.4 jit_solution(10488451018893377571)
XLA Ops:
  0.7 0.0 copy-start.4
  0.7 1.7 %charges.1.after_ref = f32[32,2,384]{2,1,0:T(2,128)} custom-call(s32[1,1]{1,0:T(1,128)} %copy.19.count_ref, bf16[384,128]{1,0:T(8,128)(2,1)} %bitcast.18, s32[1,384]{1,0:T(1,128)} %bitcast.29, bf16[1,128]{1,0:T(2,128)(2,1)} %bitcast.30), custom_call_target="tpu_custom_call" | custom-call | tf_op jit(solution)/shard_map/charges/pallas_call | solution.py:65
  2.4 0.0 copy-start
  2.4 0.0 copy-start.1
  2.4 7.3 %all-to-all-start = ((f32[32,2,384]{2,1,0:T(2,128)}), f32[32,2,384]{2,1,0:T(2,128)S(1)}, u32[]{:S(2)}, u32[]{:S(2)}) async-start(f32[32,2,384]{2,1,0:T(2,128)} %charges.1.after_ref), calls=%async_computation | async-start | bytes 196608 | tf_op jit(solution)/shard_map/all_to_all | solution.py:563
  9.7 0.0 copy-start.3
  9.7 0.0 copy-done.4
  9.7 0.0 copy-done
  9.7 0.0 copy-done.1
  9.7 0.6 copy-done.3
  10.4 0.0 copy-start.2
  10.4 0.3 exports.1
  10.7 1.6 %collective-permute-start.1 = (bf16[272,128]{1,0:T(8,128)(2,1)S(1)}, bf16[272,128]{1,0:T(8,128)(2,1)S(1)}, u32[]{:S(2)}, u32[]{:S(2)}) collective-permute-start(bf16[272,128]{1,0:T(8,128)(2,1)S(1)} %exports.1), channel_id=1, source_target_pairs={{0,24},{8,0},{16,8},{24,16},{1,25},{9,1},{17,9},{25,17},{2,26},{10... | collective-permute-start | bytes 208904 | tf_op jit(solution)/shard_map/ppermute | solution.py:551
  12.2 0.0 collective-permute-start
  12.3 0.0 copy-done.2
  12.3 2.7 %collective-permute-done.1 = bf16[272,128]{1,0:T(8,128)(2,1)S(1)} collective-permute-done((bf16[272,128]{1,0:T(8,128)(2,1)S(1)}, bf16[272,128]{1,0:T(8,128)(2,1)S(1)}, u32[]{:S(2)}, u32[]{:S(2)}) %collective-permute-start.1) | collective-permute-done | bytes 69664 | tf_op jit(solution)/shard_map/ppermute | solution.py:551
  15.0 1.2 %collective-permute-done = bf16[272,128]{1,0:T(8,128)(2,1)S(1)} collective-permute-done((bf16[272,128]{1,0:T(8,128)(2,1)S(1)}, bf16[272,128]{1,0:T(8,128)(2,1)S(1)}, u32[]{:S(2)}, u32[]{:S(2)}) %collective-permute-start) | collective-permute-done | bytes 69664 | tf_op jit(solution)/shard_map/ppermute | solution.py:551
  16.2 0.0 copy-start.11
  16.2 0.0 copy-start.12
  16.2 0.0 copy-start.13
  16.2 0.0 copy-start.14
  16.2 1.0 %all-to-all-done.qc_ref = f32[32,2,384]{2,1,0:T(2,128)S(1)} async-done(((f32[32,2,384]{2,1,0:T(2,128)}), f32[32,2,384]{2,1,0:T(2,128)S(1)}, u32[]{:S(2)}, u32[]{:S(2)}) %all-to-all-start) | async-done | bytes 98336 | tf_op jit(solution)/shard_map/all_to_all | solution.py:563
  17.3 3.1 %collective-permute-start.3 = (bf16[3,272,128]{2,1,0:T(8,128)(2,1)S(1)}, bf16[3,272,128]{2,1,0:T(8,128)(2,1)S(1)}, u32[]{:S(2)}, u32[]{:S(2)}) collective-permute-start(bf16[3,272,128]{2,1,0:T(8,128)(2,1)S(1)} %pad_maximum_fusion.mid_ref), channel_id=1, source_target_pairs={{0,7},{1,0},{2,1},{3,2},{4,3},{5,4},{6,5},{7,6},{8,15},{9,8},{10,9... | collective-permute-start | bytes 626696 | tf_op jit(solution)/shard_map/ppermute | solution.py:551
  20.3 0.0 collective-permute-start.2
  20.3 0.0 copy-done.11
  20.4 0.0 copy-done.12
  20.4 0.0 copy-done.13
  20.4 0.0 copy-done.14
  20.4 0.0 copy-start.6
  20.4 0.0 copy-start.7
  20.4 0.0 copy-start.9
  20.4 0.0 copy-start.10
  20.4 9.1 %grid_fields.1 = f32[32,3,1,384]{3,2,1,0:T(1,128)} custom-call(s32[1]{0:T(128)} %bitcast.11.place_ref, f32[32,2,384]{2,1,0:T(2,128)S(1)} %all-to-all-done.qc_ref, f32[64,192]{1,0:T(8,128)S(1)} %copy-done.12, f32[32,96]{1,0:T(8,128)S(1)} %copy-done.14, f32[64,96]{1,0:T(8,128)S(1)} %copy-done.13, f32[128,192]{1,0:T(8,128)S(1)} %copy-done.11), custom_call_target="tpu_custom_call" | custom-call | flops 8000000000 | bytes 4000000 | tf_op jit(solution)/shard_map/grid_fields/pallas_call | solution.py:286
  29.5 0.0 copy-start.5
  29.5 0.0 copy-start.8
  29.5 6.0 %all-to-all-start.1 = ((f32[32,3,1,384]{3,2,1,0:T(1,128)}), f32[32,3,1,384]{3,2,1,0:T(1,128)S(1)}, u32[]{:S(2)}, u32[]{:S(2)}) async-start(f32[32,3,1,384]{3,2,1,0:T(1,128)} %grid_fields.1), calls=%async_computation.1 | async-start | bytes 294912 | tf_op jit(solution)/shard_map/all_to_all | solution.py:572
  35.4 0.0 collective-permute-done.3.down_ref
  35.5 0.0 collective-permute-done.2.up_ref
  35.5 0.0 copy-done.6
  35.5 0.0 copy-done.7
  35.5 0.0 copy-done.9
  35.5 0.0 copy-done.10
  35.5 0.0 copy-done.5
  35.5 0.0 copy-done.8
  35.5 38.1 %edge_forces.1 = f32[3,1,384]{2,1,0:T(1,128)S(1)} custom-call(s32[12288]{0:T(1024)S(1)} %reshape.46.list_hbm, s32[32,384]{1,0:T(8,128)S(1)} %bitcast.23, bf16[384,128]{1,0:T(8,128)(2,1)S(1)} %bitcast.20, bf16[3,384]{1,0:T(4,128)(2,1)S(1)} %bitcast.25, bf16[3,272,128]{2,1,0:T(8,128)(2,1)S(1)} %pad_maximum_fusion.mid_ref, ...), custom_call_target="tpu_custom_call" | custom-call | flops 6442450944 | bytes 4000000 | tf_op jit(solution)/shard_map/edge_forces/pallas_call | solution.py:515
  73.6 0.0 all-to-all-done.1
  73.7 0.1 reduce_sum.11
  73.8 0.6 fusion
  (4 shorter events, 0.1 us)
Async XLA Ops:
  0.7 9.1 %copy-start.4 = (s32[1,1,256]{2,1,0:T(1,128)S(1)}, s32[1,1,256]{2,1,0:T(1,128)}, u32[]{:S(2)}) copy-start(s32[1,1,256]{2,1,0:T(1,128)} %param.20) | copy-start | bytes 3076
  2.4 7.3 %copy-start = (f32[32,2,384]{2,1,0:T(2,128)S(1)}, f32[32,2,384]{2,1,0:T(2,128)}, u32[]{:S(2)}) copy-start(f32[32,2,384]{2,1,0:T(2,128)} %charges.1.after_ref) | copy-start | bytes 294916
  2.4 7.3 %copy-start.1 = (bf16[1,1,384,128]{3,2,1,0:T(8,128)(2,1)S(1)}, bf16[1,1,384,128]{3,2,1,0:T(8,128)(2,1)}, u32[]{:S(2)}) copy-start(bf16[1,1,384,128]{3,2,1,0:T(8,128)(2,1)} %param.17) | copy-start | bytes 294916
  2.4 14.9 %all-to-all-start = ((f32[32,2,384]{2,1,0:T(2,128)}), f32[32,2,384]{2,1,0:T(2,128)S(1)}, u32[]{:S(2)}, u32[]{:S(2)}) async-start(f32[32,2,384]{2,1,0:T(2,128)} %charges.1.after_ref), calls=%async_computation | async-start | bytes 196608 | tf_op jit(solution)/shard_map/all_to_all | solution.py:563
  9.7 0.7 copy-start.3
  10.4 1.9 %copy-start.2 = (s32[1,1,384,32]{2,3,1,0:T(8,128)S(1)}, s32[1,1,384,32]{2,3,1,0:T(8,128)}, u32[]{:S(2)}) copy-start(s32[1,1,384,32]{2,3,1,0:T(8,128)} %param.21) | copy-start | bytes 147460
  10.7 4.4 %collective-permute-start.1 = (bf16[272,128]{1,0:T(8,128)(2,1)S(1)}, bf16[272,128]{1,0:T(8,128)(2,1)S(1)}, u32[]{:S(2)}, u32[]{:S(2)}) collective-permute-start(bf16[272,128]{1,0:T(8,128)(2,1)S(1)} %exports.1), channel_id=1, source_target_pairs={{0,24},{8,0},{16,8},{24,16},{1,25},{9,1},{17,9},{25,17},{2,26},{10... | collective-permute-start | bytes 208904 | tf_op jit(solution)/shard_map/ppermute | solution.py:551
  12.2 4.0 %collective-permute-start = (bf16[272,128]{1,0:T(8,128)(2,1)S(1)}, bf16[272,128]{1,0:T(8,128)(2,1)S(1)}, u32[]{:S(2)}, u32[]{:S(2)}) collective-permute-start(bf16[272,128]{1,0:T(8,128)(2,1)S(1)} %exports.1), channel_id=1, source_target_pairs={{0,8},{8,16},{16,24},{24,0},{1,9},{9,17},{17,25},{25,1},{2,10},{10... | collective-permute-start | bytes 208904 | tf_op jit(solution)/shard_map/ppermute | solution.py:551
  16.2 4.2 %copy-start.11 = (f32[128,192]{1,0:T(8,128)S(1)}, f32[128,192]{1,0:T(8,128)}, u32[]{:S(2)}) copy-start(f32[128,192]{1,0:T(8,128)} %constant.24.clone.iy_ref) | copy-start | bytes 294916
  16.2 4.2 %copy-start.12 = (f32[64,192]{1,0:T(8,128)S(1)}, f32[64,192]{1,0:T(8,128)}, u32[]{:S(2)}) copy-start(f32[64,192]{1,0:T(8,128)} %constant.21.clone.fy_ref) | copy-start | bytes 147460
  16.2 4.2 %copy-start.13 = (f32[64,96]{1,0:T(8,128)S(1)}, f32[64,96]{1,0:T(8,128)}, u32[]{:S(2)}) copy-start(f32[64,96]{1,0:T(8,128)} %constant.23.clone.ix_ref) | copy-start | bytes 73732
  16.2 4.2 %copy-start.14 = (f32[32,96]{1,0:T(8,128)S(1)}, f32[32,96]{1,0:T(8,128)}, u32[]{:S(2)}) copy-start(f32[32,96]{1,0:T(8,128)} %constant.22.clone.fx_ref) | copy-start | bytes 36868
  17.3 18.2 %collective-permute-start.3 = (bf16[3,272,128]{2,1,0:T(8,128)(2,1)S(1)}, bf16[3,272,128]{2,1,0:T(8,128)(2,1)S(1)}, u32[]{:S(2)}, u32[]{:S(2)}) collective-permute-start(bf16[3,272,128]{2,1,0:T(8,128)(2,1)S(1)} %pad_maximum_fusion.mid_ref), channel_id=1, source_target_pairs={{0,7},{1,0},{2,1},{3,2},{4,3},{5,4},{6,5},{7,6},{8,15},{9,8},{10,9... | collective-permute-start | bytes 626696 | tf_op jit(solution)/shard_map/ppermute | solution.py:551
  20.3 15.1 %collective-permute-start.2 = (bf16[3,272,128]{2,1,0:T(8,128)(2,1)S(1)}, bf16[3,272,128]{2,1,0:T(8,128)(2,1)S(1)}, u32[]{:S(2)}, u32[]{:S(2)}) collective-permute-start(bf16[3,272,128]{2,1,0:T(8,128)(2,1)S(1)} %pad_maximum_fusion.mid_ref), channel_id=1, source_target_pairs={{0,1},{1,2},{2,3},{3,4},{4,5},{5,6},{6,7},{7,0},{8,9},{9,10},{10,1... | collective-permute-start | bytes 626696 | tf_op jit(solution)/shard_map/ppermute | solution.py:551
  20.4 15.1 %copy-start.6 = (bf16[1024,128]{1,0:T(8,128)(2,1)S(1)}, bf16[1024,128]{1,0:T(8,128)(2,1)}, u32[]{:S(2)}) copy-start(bf16[1024,128]{1,0:T(8,128)(2,1)} %w_contract_ref.1) | copy-start | bytes 786436
  20.4 15.1 %copy-start.7 = (bf16[128,256]{1,0:T(8,128)(2,1)S(1)}, bf16[128,256]{1,0:T(8,128)(2,1)}, u32[]{:S(2)}) copy-start(bf16[128,256]{1,0:T(8,128)(2,1)} %w_pair_ref.1) | copy-start | bytes 196612
  20.4 15.1 %copy-start.9 = (bf16[128,128]{1,0:T(8,128)(2,1)S(1)}, bf16[128,128]{1,0:T(8,128)(2,1)}, u32[]{:S(2)}) copy-start(bf16[128,128]{1,0:T(8,128)(2,1)} %w_final_ref.1) | copy-start | bytes 98308
  20.4 15.1 %copy-start.10 = (f32[8,128]{1,0:T(8,128)S(1)}, f32[8,128]{1,0:T(8,128)}, u32[]{:S(2)}) copy-start(f32[8,128]{1,0:T(8,128)} %w_radial_ref.1) | copy-start | bytes 12292
  29.5 6.0 %copy-start.5 = (bf16[128,1024]{1,0:T(8,128)(2,1)S(1)}, bf16[128,1024]{1,0:T(8,128)(2,1)}, u32[]{:S(2)}) copy-start(bf16[128,1024]{1,0:T(8,128)(2,1)} %w_expand_ref.1) | copy-start | bytes 786436
  29.5 6.0 %copy-start.8 = (bf16[128,128]{1,0:T(8,128)(2,1)S(1)}, bf16[128,128]{1,0:T(8,128)(2,1)}, u32[]{:S(2)}) copy-start(bf16[128,128]{1,0:T(8,128)(2,1)} %w_self_ref.1) | copy-start | bytes 98308
  29.5 44.2 %all-to-all-start.1 = ((f32[32,3,1,384]{3,2,1,0:T(1,128)}), f32[32,3,1,384]{3,2,1,0:T(1,128)S(1)}, u32[]{:S(2)}, u32[]{:S(2)}) async-start(f32[32,3,1,384]{3,2,1,0:T(1,128)} %grid_fields.1), calls=%async_computation.1 | async-start | bytes 294912 | tf_op jit(solution)/shard_map/all_to_all | solution.py:572

commit v14 on v12

--- a/solution.py
+++ b/solution.py
@@ -20,7 +20,7 @@
 EXTRA = 16
 ROWS = 32
 GROUPS = LANES // ROWS
-CHUNK_ATOMS = 32
+CHUNK_ATOMS = 64
 PIECES = 4
 HIGHEST = lax.Precision.HIGHEST
 F32 = jnp.float32
@@ -409,9 +409,10 @@
     def gather(index, near, part):
         for k in range(part * slots, (part + 1) * slots):
             start = k * atoms + index * CHUNK_ATOMS
-            loaded = [table[list_ref[start + a]] for a in range(CHUNK_ATOMS)]
-            for a, tile in enumerate(loaded):
-                near[k * CHUNK_ATOMS + a] = tile
+            for first in range(0, CHUNK_ATOMS, 16):
+                loaded = [table[list_ref[start + first + a]] for a in range(16)]
+                for a, tile in enumerate(loaded):
+                    near[k * CHUNK_ATOMS + first + a] = tile
 
     def radials(index):
         basis = marks[:, atoms_of(index), :].reshape(-1, LANES).astype(BF16)

time: 68 us -> 70 us (1.029)
  Pallas kernels: 42.5 us -> 44.7 us
    pallas_call x1, Pallas kernels: 31.4 us -> 33.7 us  [edge_forces(): pl.pallas_call(edge_kernel, in_specs=[pl.BlockSpec(memory_space=pl.ANY)]...]
  transfers between devices with their start and end apart: 6 -> 6, of which waited for: 3 -> 3; matrix products, arithmetic and copies ran while one was open for 0% -> 0% of each run, Pallas kernels for 60% -> 62%
where the time goes in v14:
time: 70 us; the launch traced here: 69.8 us
  Pallas kernels  44.7 us (64%)
  starting transfers between devices  17.7 us (25%)
  waiting for transfers between devices  4.92 us (7%)
  between operations  0.9 us (1%)
  other arithmetic  0.75 us (1%)
  local copies, waits for them, and re-layouts  0.74 us (1%)
    pallas_call x1, Pallas kernels, edge_forces(): pl.pallas_call(edge_kernel, in_specs=[pl.BlockSpec(memory_space=pl.ANY)]...  33.7 us
    pallas_call x1, Pallas kernels, grid_fields(): pl.pallas_call(functools.partial(grid_kernel, cycle_x, cycle_y), in_specs...  9.06 us
    all_to_all x1, starting transfers between devices, shards(): lax.all_to_all(spread, ('dx', 'dy'), split_axis=0, concat_axis=0, tiled=T...  7.3 us
    all_to_all x1, starting transfers between devices, shards(): lax.all_to_all(partial, ('dx', 'dy'), split_axis=0, concat_axis=0, tiled=...  5.77 us
    ppermute x4, starting transfers between devices, ring(): lax.ppermute(array, axis, [(i, (i + step) % size) for i in range(size)])  4.67 us
    ppermute x4, waiting for transfers between devices, ring(): lax.ppermute(array, axis, [(i, (i + step) % size) for i in range(size)])  3.9 us
    pallas_call x1, Pallas kernels, charges(): pl.pallas_call(charge_kernel, in_specs=[pl.BlockSpec(memory_space=pltpu.S...  1.72 us
  transfers between devices with their start and end apart: 6, of which 3 were waited for; matrix products, arithmetic and copies ran while one was open for 0% of the time, Pallas kernels for 62%

profile of v14, /device:TPU:0, one launch (start us, length us, event | category | flops | bytes accessed | tf_op | source)
XLA Modules:
  0.0 69.8 jit_solution(5863915340420236827)
XLA Ops:
  0.7 0.0 copy-start.4
  0.7 1.7 %charges.1.after_ref = f32[32,2,384]{2,1,0:T(2,128)} custom-call(s32[1,1]{1,0:T(1,128)} %copy.19.count_ref, bf16[384,128]{1,0:T(8,128)(2,1)} %bitcast.18, s32[1,384]{1,0:T(1,128)} %bitcast.29, bf16[1,128]{1,0:T(2,128)(2,1)} %bitcast.30), custom_call_target="tpu_custom_call" | custom-call | tf_op jit(solution)/shard_map/charges/pallas_call | solution.py:65
  2.4 0.0 copy-start
  2.4 0.0 copy-start.1
  2.4 7.3 %all-to-all-start = ((f32[32,2,384]{2,1,0:T(2,128)}), f32[32,2,384]{2,1,0:T(2,128)S(1)}, u32[]{:S(2)}, u32[]{:S(2)}) async-start(f32[32,2,384]{2,1,0:T(2,128)} %charges.1.after_ref), calls=%async_computation | async-start | bytes 196608 | tf_op jit(solution)/shard_map/all_to_all | solution.py:569
  9.7 0.0 copy-start.3
  9.7 0.0 copy-done.4
  9.7 0.0 copy-done
  9.7 0.0 copy-done.1
  9.7 0.6 copy-done.3
  10.4 0.0 copy-start.2
  10.4 0.3 exports.1
  10.7 1.6 %collective-permute-start.1 = (bf16[272,128]{1,0:T(8,128)(2,1)S(1)}, bf16[272,128]{1,0:T(8,128)(2,1)S(1)}, u32[]{:S(2)}, u32[]{:S(2)}) collective-permute-start(bf16[272,128]{1,0:T(8,128)(2,1)S(1)} %exports.1), channel_id=1, source_target_pairs={{0,24},{8,0},{16,8},{24,16},{1,25},{9,1},{17,9},{25,17},{2,26},{10... | collective-permute-start | bytes 208904 | tf_op jit(solution)/shard_map/ppermute | solution.py:557
  12.2 0.0 collective-permute-start
  12.3 0.0 copy-done.2
  12.3 2.7 %collective-permute-done.1 = bf16[272,128]{1,0:T(8,128)(2,1)S(1)} collective-permute-done((bf16[272,128]{1,0:T(8,128)(2,1)S(1)}, bf16[272,128]{1,0:T(8,128)(2,1)S(1)}, u32[]{:S(2)}, u32[]{:S(2)}) %collective-permute-start.1) | collective-permute-done | bytes 69664 | tf_op jit(solution)/shard_map/ppermute | solution.py:557
  15.0 1.2 %collective-permute-done = bf16[272,128]{1,0:T(8,128)(2,1)S(1)} collective-permute-done((bf16[272,128]{1,0:T(8,128)(2,1)S(1)}, bf16[272,128]{1,0:T(8,128)(2,1)S(1)}, u32[]{:S(2)}, u32[]{:S(2)}) %collective-permute-start) | collective-permute-done | bytes 69664 | tf_op jit(solution)/shard_map/ppermute | solution.py:557
  16.2 0.0 copy-start.11
  16.2 0.0 copy-start.12
  16.2 0.0 copy-start.13
  16.2 0.0 copy-start.14
  16.2 1.0 %all-to-all-done.qc_ref = f32[32,2,384]{2,1,0:T(2,128)S(1)} async-done(((f32[32,2,384]{2,1,0:T(2,128)}), f32[32,2,384]{2,1,0:T(2,128)S(1)}, u32[]{:S(2)}, u32[]{:S(2)}) %all-to-all-start) | async-done | bytes 98336 | tf_op jit(solution)/shard_map/all_to_all | solution.py:569
  17.3 3.1 %collective-permute-start.3 = (bf16[3,272,128]{2,1,0:T(8,128)(2,1)S(1)}, bf16[3,272,128]{2,1,0:T(8,128)(2,1)S(1)}, u32[]{:S(2)}, u32[]{:S(2)}) collective-permute-start(bf16[3,272,128]{2,1,0:T(8,128)(2,1)S(1)} %pad_maximum_fusion.mid_ref), channel_id=1, source_target_pairs={{0,7},{1,0},{2,1},{3,2},{4,3},{5,4},{6,5},{7,6},{8,15},{9,8},{10,9... | collective-permute-start | bytes 626696 | tf_op jit(solution)/shard_map/ppermute | solution.py:557
  20.3 0.0 collective-permute-start.2
  20.3 0.0 copy-done.11
  20.4 0.0 copy-done.12
  20.4 0.0 copy-done.13
  20.4 0.0 copy-done.14
  20.4 0.0 copy-start.6
  20.4 0.0 copy-start.7
  20.4 0.0 copy-start.9
  20.4 0.0 copy-start.10
  20.4 9.1 %grid_fields.1 = f32[32,3,1,384]{3,2,1,0:T(1,128)} custom-call(s32[1]{0:T(128)} %bitcast.11.place_ref, f32[32,2,384]{2,1,0:T(2,128)S(1)} %all-to-all-done.qc_ref, f32[64,192]{1,0:T(8,128)S(1)} %copy-done.12, f32[32,96]{1,0:T(8,128)S(1)} %copy-done.14, f32[64,96]{1,0:T(8,128)S(1)} %copy-done.13, f32[128,192]{1,0:T(8,128)S(1)} %copy-done.11), custom_call_target="tpu_custom_call" | custom-call | flops 8000000000 | bytes 4000000 | tf_op jit(solution)/shard_map/grid_fields/pallas_call | solution.py:286
  29.5 0.0 copy-start.5
  29.5 0.0 copy-start.8
  29.5 5.8 %all-to-all-start.1 = ((f32[32,3,1,384]{3,2,1,0:T(1,128)}), f32[32,3,1,384]{3,2,1,0:T(1,128)S(1)}, u32[]{:S(2)}, u32[]{:S(2)}) async-start(f32[32,3,1,384]{3,2,1,0:T(1,128)} %grid_fields.1), calls=%async_computation.1 | async-start | bytes 294912 | tf_op jit(solution)/shard_map/all_to_all | solution.py:578
  35.3 0.0 collective-permute-done.3.down_ref
  35.3 0.0 collective-permute-done.2.up_ref
  35.3 0.0 copy-done.6
  35.3 0.0 copy-done.7
  35.3 0.0 copy-done.9
  35.3 0.0 copy-done.10
  35.3 0.0 copy-done.5
  35.3 0.0 copy-done.8
  35.3 33.7 %edge_forces.1 = f32[3,1,384]{2,1,0:T(1,128)S(1)} custom-call(s32[12288]{0:T(1024)S(1)} %reshape.46.list_hbm, s32[32,384]{1,0:T(8,128)S(1)} %bitcast.23, bf16[384,128]{1,0:T(8,128)(2,1)S(1)} %bitcast.20, bf16[3,384]{1,0:T(4,128)(2,1)S(1)} %bitcast.25, bf16[3,272,128]{2,1,0:T(8,128)(2,1)S(1)} %pad_maximum_fusion.mid_ref, ...), custom_call_target="tpu_custom_call" | custom-call | flops 6442450944 | bytes 4000000 | tf_op jit(solution)/shard_map/edge_forces/pallas_call | solution.py:522
  69.0 0.0 all-to-all-done.1
  69.0 0.1 reduce_sum.11
  69.2 0.6 fusion
  (4 shorter events, 0.1 us)
Async XLA Ops:
  0.7 9.1 %copy-start.4 = (s32[1,1,256]{2,1,0:T(1,128)S(1)}, s32[1,1,256]{2,1,0:T(1,128)}, u32[]{:S(2)}) copy-start(s32[1,1,256]{2,1,0:T(1,128)} %param.20) | copy-start | bytes 3076
  2.4 7.3 %copy-start = (f32[32,2,384]{2,1,0:T(2,128)S(1)}, f32[32,2,384]{2,1,0:T(2,128)}, u32[]{:S(2)}) copy-start(f32[32,2,384]{2,1,0:T(2,128)} %charges.1.after_ref) | copy-start | bytes 294916
  2.4 7.3 %copy-start.1 = (bf16[1,1,384,128]{3,2,1,0:T(8,128)(2,1)S(1)}, bf16[1,1,384,128]{3,2,1,0:T(8,128)(2,1)}, u32[]{:S(2)}) copy-start(bf16[1,1,384,128]{3,2,1,0:T(8,128)(2,1)} %param.17) | copy-start | bytes 294916
  2.4 14.9 %all-to-all-start = ((f32[32,2,384]{2,1,0:T(2,128)}), f32[32,2,384]{2,1,0:T(2,128)S(1)}, u32[]{:S(2)}, u32[]{:S(2)}) async-start(f32[32,2,384]{2,1,0:T(2,128)} %charges.1.after_ref), calls=%async_computation | async-start | bytes 196608 | tf_op jit(solution)/shard_map/all_to_all | solution.py:569
  9.7 0.7 copy-start.3
  10.4 1.9 %copy-start.2 = (s32[1,1,384,32]{2,3,1,0:T(8,128)S(1)}, s32[1,1,384,32]{2,3,1,0:T(8,128)}, u32[]{:S(2)}) copy-start(s32[1,1,384,32]{2,3,1,0:T(8,128)} %param.21) | copy-start | bytes 147460
  10.7 4.4 %collective-permute-start.1 = (bf16[272,128]{1,0:T(8,128)(2,1)S(1)}, bf16[272,128]{1,0:T(8,128)(2,1)S(1)}, u32[]{:S(2)}, u32[]{:S(2)}) collective-permute-start(bf16[272,128]{1,0:T(8,128)(2,1)S(1)} %exports.1), channel_id=1, source_target_pairs={{0,24},{8,0},{16,8},{24,16},{1,25},{9,1},{17,9},{25,17},{2,26},{10... | collective-permute-start | bytes 208904 | tf_op jit(solution)/shard_map/ppermute | solution.py:557
  12.2 4.0 %collective-permute-start = (bf16[272,128]{1,0:T(8,128)(2,1)S(1)}, bf16[272,128]{1,0:T(8,128)(2,1)S(1)}, u32[]{:S(2)}, u32[]{:S(2)}) collective-permute-start(bf16[272,128]{1,0:T(8,128)(2,1)S(1)} %exports.1), channel_id=1, source_target_pairs={{0,8},{8,16},{16,24},{24,0},{1,9},{9,17},{17,25},{25,1},{2,10},{10... | collective-permute-start | bytes 208904 | tf_op jit(solution)/shard_map/ppermute | solution.py:557
  16.2 4.2 %copy-start.11 = (f32[128,192]{1,0:T(8,128)S(1)}, f32[128,192]{1,0:T(8,128)}, u32[]{:S(2)}) copy-start(f32[128,192]{1,0:T(8,128)} %constant.24.clone.iy_ref) | copy-start | bytes 294916
  16.2 4.2 %copy-start.12 = (f32[64,192]{1,0:T(8,128)S(1)}, f32[64,192]{1,0:T(8,128)}, u32[]{:S(2)}) copy-start(f32[64,192]{1,0:T(8,128)} %constant.21.clone.fy_ref) | copy-start | bytes 147460
  16.2 4.2 %copy-start.13 = (f32[64,96]{1,0:T(8,128)S(1)}, f32[64,96]{1,0:T(8,128)}, u32[]{:S(2)}) copy-start(f32[64,96]{1,0:T(8,128)} %constant.23.clone.ix_ref) | copy-start | bytes 73732
  16.2 4.2 %copy-start.14 = (f32[32,96]{1,0:T(8,128)S(1)}, f32[32,96]{1,0:T(8,128)}, u32[]{:S(2)}) copy-start(f32[32,96]{1,0:T(8,128)} %constant.22.clone.fx_ref) | copy-start | bytes 36868
  17.3 18.0 %collective-permute-start.3 = (bf16[3,272,128]{2,1,0:T(8,128)(2,1)S(1)}, bf16[3,272,128]{2,1,0:T(8,128)(2,1)S(1)}, u32[]{:S(2)}, u32[]{:S(2)}) collective-permute-start(bf16[3,272,128]{2,1,0:T(8,128)(2,1)S(1)} %pad_maximum_fusion.mid_ref), channel_id=1, source_target_pairs={{0,7},{1,0},{2,1},{3,2},{4,3},{5,4},{6,5},{7,6},{8,15},{9,8},{10,9... | collective-permute-start | bytes 626696 | tf_op jit(solution)/shard_map/ppermute | solution.py:557
  20.3 14.9 %collective-permute-start.2 = (bf16[3,272,128]{2,1,0:T(8,128)(2,1)S(1)}, bf16[3,272,128]{2,1,0:T(8,128)(2,1)S(1)}, u32[]{:S(2)}, u32[]{:S(2)}) collective-permute-start(bf16[3,272,128]{2,1,0:T(8,128)(2,1)S(1)} %pad_maximum_fusion.mid_ref), channel_id=1, source_target_pairs={{0,1},{1,2},{2,3},{3,4},{4,5},{5,6},{6,7},{7,0},{8,9},{9,10},{10,1... | collective-permute-start | bytes 626696 | tf_op jit(solution)/shard_map/ppermute | solution.py:557
  20.4 14.9 %copy-start.6 = (bf16[1024,128]{1,0:T(8,128)(2,1)S(1)}, bf16[1024,128]{1,0:T(8,128)(2,1)}, u32[]{:S(2)}) copy-start(bf16[1024,128]{1,0:T(8,128)(2,1)} %w_contract_ref.1) | copy-start | bytes 786436
  20.4 14.9 %copy-start.7 = (bf16[128,256]{1,0:T(8,128)(2,1)S(1)}, bf16[128,256]{1,0:T(8,128)(2,1)}, u32[]{:S(2)}) copy-start(bf16[128,256]{1,0:T(8,128)(2,1)} %w_pair_ref.1) | copy-start | bytes 196612
  20.4 14.9 %copy-start.9 = (bf16[128,128]{1,0:T(8,128)(2,1)S(1)}, bf16[128,128]{1,0:T(8,128)(2,1)}, u32[]{:S(2)}) copy-start(bf16[128,128]{1,0:T(8,128)(2,1)} %w_final_ref.1) | copy-start | bytes 98308
  20.4 14.9 %copy-start.10 = (f32[8,128]{1,0:T(8,128)S(1)}, f32[8,128]{1,0:T(8,128)}, u32[]{:S(2)}) copy-start(f32[8,128]{1,0:T(8,128)} %w_radial_ref.1) | copy-start | bytes 12292
  29.5 5.8 %copy-start.5 = (bf16[128,1024]{1,0:T(8,128)(2,1)S(1)}, bf16[128,1024]{1,0:T(8,128)(2,1)}, u32[]{:S(2)}) copy-start(bf16[128,1024]{1,0:T(8,128)(2,1)} %w_expand_ref.1) | copy-start | bytes 786436
  29.5 5.9 %copy-start.8 = (bf16[128,128]{1,0:T(8,128)(2,1)S(1)}, bf16[128,128]{1,0:T(8,128)(2,1)}, u32[]{:S(2)}) copy-start(bf16[128,128]{1,0:T(8,128)(2,1)} %w_self_ref.1) | copy-start | bytes 98308
  29.5 39.5 %all-to-all-start.1 = ((f32[32,3,1,384]{3,2,1,0:T(1,128)}), f32[32,3,1,384]{3,2,1,0:T(1,128)S(1)}, u32[]{:S(2)}, u32[]{:S(2)}) async-start(f32[32,3,1,384]{3,2,1,0:T(1,128)} %grid_fields.1), calls=%async_computation.1 | async-start | bytes 294912 | tf_op jit(solution)/shard_map/all_to_all | solution.py:578
